TPU v7x, 32 devices: a whole 2x2x4 slice. The times are simulated.
32 devices in a mesh: vec: 4 (over y, core), space: 8 (over z, x).
Axes of the slice: x: 2, y: 2, z: 4, core: 2. Of those that a mesh axis runs over, the one named last changes fastest.
Arguments:
- tangents: float32 [16, 2, 16, 128, 128], P('vec', None, 'space'), may hold values from -16 to 16
- background: bfloat16 [3, 4, 16, 128, 128], P(None, None, 'space', 'vec'), may hold values from -4 to 4
Outputs:
- basis: float32 [16, 2, 16, 128, 128], P('vec', None, 'space')
- growth: float32 [16], replicated
All inputs are finite; a program needn't handle non-finite values.
Results may differ from a plain program's by a relative error of at most 0.00045.
Values may be sent and summed in bfloat16 or wider, within the bound.
No kernel may reach another device: no remote copies, remote signals or barrier semaphores. Data moves between devices by JAX's collectives and lax.ppermute only.
A program may use at most 64 MiB of HBM per device.

v0:
```python
import jax
import jax.numpy as jnp
from jax import lax
from jax.sharding import PartitionSpec as P

time_step = 0.1
diffusion = 0.5


def padded_2(value, sides, width):
    for axis, dim in sides:
        count, length = (lax.axis_size(axis), value.shape[dim])
        up = [(i, (i + 1) % count) for i in range(count)]
        down = [(j, i) for i, j in up]
        last = lax.slice_in_dim(value, length - width, length, axis=dim)
        leading = lax.slice_in_dim(value, 0, width, axis=dim)
        before = lax.ppermute(last, axis, up)
        after = lax.ppermute(leading, axis, down)
        value = jnp.concatenate([before, value, after], axis=dim)
    return value


def combine(center, x_next, x_prev, y_next, y_prev, z_next, z_prev, section):
    dxf = (x_next - x_prev) * 0.5
    dyf = (y_next - y_prev) * 0.5
    dzf = (z_next - z_prev) * 0.5
    lap = x_next + x_prev + y_next + y_prev + z_next + z_prev - 6.0 * center
    speed_u = section[0]
    speed_v = section[1]
    speed_r = section[2]
    strat = section[3]
    adv = speed_u * dxf + speed_v * dyf + speed_r * dzf
    w_rate = -adv[..., 0, :, :, :] + center[..., 1, :, :, :] + diffusion * lap[..., 0, :, :, :]
    b_rate = (
        -adv[..., 1, :, :, :] - strat * center[..., 0, :, :, :] + diffusion * lap[..., 1, :, :, :]
    )
    return jnp.stack([w_rate, b_rate], -4)


def vertical(center):
    widths = [(0, 0)] * (center.ndim - 1) + [(1, 1)]
    zpad = jnp.pad(center, widths)
    return (zpad[..., 2:], zpad[..., :-2])


def rates(field, section):
    padded = padded_2(field.astype(jnp.bfloat16), (("space", 2),), 1).astype(field.dtype)
    x_next = jnp.roll(field, -1, -2)
    x_prev = jnp.roll(field, 1, -2)
    y_next = padded[:, :, 2:]
    y_prev = padded[:, :, :-2]
    z_next, z_prev = vertical(field)
    return combine(field, x_next, x_prev, y_next, y_prev, z_next, z_prev, section)


def runge_kutta(start, sections, rate_fn):
    section_one = start + time_step * rate_fn(start, sections[0])
    section_two = 0.75 * start + 0.25 * (
        section_one + time_step * rate_fn(section_one, sections[1])
    )
    return start / 3.0 + 2.0 / 3.0 * (section_two + time_step * rate_fn(section_two, sections[2]))


def factor(gram, vectors):
    lower = jnp.linalg.cholesky(gram)
    eye = jnp.eye(vectors, dtype=jnp.float32)
    inverse = lax.linalg.triangular_solve(lower, eye, left_side=True, lower=True)
    return (lower, inverse)


def on_device(tangents, background):
    per_dev = tangents.shape[0]
    vectors = per_dev * lax.axis_size("vec")
    own_index = lax.axis_index("vec")
    sections = lax.all_gather(background, "vec", axis=3, tiled=True).astype(jnp.float32)
    advanced = runge_kutta(tangents, sections, rates)
    flat = advanced.reshape(per_dev, -1)
    cells = flat.shape[1] * lax.axis_size("space")
    total = jnp.zeros((per_dev, vectors), jnp.float32)
    product = jnp.dot(
        flat,
        lax.all_gather(flat.astype(jnp.bfloat16), "vec", axis=0, tiled=True).astype(jnp.float32).T,
        precision=lax.Precision.HIGHEST,
    )
    rows = lax.dynamic_update_slice_in_dim(total, total + product, jnp.int32(0), 1)
    summed = lax.psum(rows, "space")
    gram = lax.all_gather(summed, "vec", axis=0, tiled=True) / cells
    lower, inverse = factor(gram, vectors)
    own_rows = lax.dynamic_slice_in_dim(inverse, own_index * per_dev, per_dev, 0)
    basis = jnp.dot(
        own_rows, lax.all_gather(flat, "vec", axis=0, tiled=True), precision=lax.Precision.HIGHEST
    )
    growth = jnp.log(jnp.diagonal(lower))
    return (basis.reshape(advanced.shape), growth)


def solution(mesh):
    in_specs = (P("vec", None, "space", None, None), P(None, None, "space", "vec", None))
    out_specs = (P("vec", None, "space", None, None), P())
    return jax.shard_map(
        on_device, mesh=mesh, in_specs=in_specs, out_specs=out_specs, check_vma=False
    )
```

profile of v0, /device:TPU:0, one launch (start us, length us, event | category | flops | bytes accessed | tf_op | source)
XLA Modules:
  0.0 138.8 jit_solution(14047280961818243280)
XLA Ops:
  7.2 1.4 %convert_element_type.31 = bf16[4,2,2,128,128]{4,3,2,1,0:T(8,128)(2,1)S(1)} convert(f32[4,2,2,128,128]{4,3,2,1,0:T(8,128)} %param.2) | non-fusion elementwise | flops 262144 | bytes 1572864 | tf_op jit(solution)/shard_map/convert_element_type | solution.py:47
  8.7 3.0 %collective-permute-start = (bf16[4,2,1,128,128]{4,3,2,1,0:T(8,128)(2,1)S(1)}, bf16[4,2,1,128,128]{4,3,2,1,0:T(8,128)(2,1)S(1)}, u32[]{:S(2)}, u32[]{:S(2)}) collective-permute-start(bf16[4,2,1,128,128]{4,3,2,1,0:T(8,128)(2,1)S(1)} %get-tuple-element.48), channel_id=1, source_target_pairs={{0,1},{1,2},{2,3},{3,4},{4,5},{5,6},{6,7},{7,0},{8,9},{9,10},{10,1... | collective-permute-start | bytes 786440 | tf_op jit(solution)/shard_map/ppermute | solution.py:17
  11.7 3.1 %collective-permute-start.1 = (bf16[4,2,1,128,128]{4,3,2,1,0:T(8,128)(2,1)S(1)}, bf16[4,2,1,128,128]{4,3,2,1,0:T(8,128)(2,1)S(1)}, u32[]{:S(2)}, u32[]{:S(2)}) collective-permute-start(bf16[4,2,1,128,128]{4,3,2,1,0:T(8,128)(2,1)S(1)} %get-tuple-element.49), channel_id=1, source_target_pairs={{1,0},{2,1},{3,2},{4,3},{5,4},{6,5},{7,6},{0,7},{9,8},{10,9},{11,1... | collective-permute-start | bytes 786440 | tf_op jit(solution)/shard_map/ppermute | solution.py:18
  15.0 8.7 %all_gather.12 = bf16[3,4,2,128,128]{4,3,2,1,0:T(8,128)(2,1)S(1)} all-gather(bf16[3,4,2,32,128]{4,3,2,1,0:T(8,128)(2,1)S(1)} %copy-done.1), channel_id=1, replica_groups=mesh['vec'=4,'space'=8] {'vec'}, dimensions={3}, use_global_device_ids=true | all-gather | bytes 983040 | tf_op jit(solution)/shard_map/all_gather | solution.py:75
  24.1 1.0 collective-permute-done.1
  25.2 1.2 multiply_add_fusion.2
  26.9 0.3 collective-permute-start.2
  27.2 4.4 %collective-permute-start.3 = (bf16[4,2,1,128,128]{4,3,2,1,0:T(8,128)(2,1)S(1)}, bf16[4,2,1,128,128]{4,3,2,1,0:T(8,128)(2,1)S(1)}, u32[]{:S(2)}, u32[]{:S(2)}) collective-permute-start(bf16[4,2,1,128,128]{4,3,2,1,0:T(8,128)(2,1)S(1)} %get-tuple-element.47), channel_id=1, source_target_pairs={{1,0},{2,1},{3,2},{4,3},{5,4},{6,5},{7,6},{0,7},{9,8},{10,9},{11,1... | collective-permute-start | bytes 786440 | tf_op jit(solution)/shard_map/ppermute | solution.py:18
  31.9 6.1 %collective-permute-done.2 = bf16[4,2,1,128,128]{4,3,2,1,0:T(8,128)(2,1)S(1)} collective-permute-done((bf16[4,2,1,128,128]{4,3,2,1,0:T(8,128)(2,1)S(1)}, bf16[4,2,1,128,128]{4,3,2,1,0:T(8,128)(2,1)S(1)}, u32[]{:S(2)}, u32[]{:S(2)}) %collective-permute-start.2) | collective-permute-done | bytes 262176 | tf_op jit(solution)/shard_map/ppermute | solution.py:17
  37.9 3.5 %collective-permute-done.3 = bf16[4,2,1,128,128]{4,3,2,1,0:T(8,128)(2,1)S(1)} collective-permute-done((bf16[4,2,1,128,128]{4,3,2,1,0:T(8,128)(2,1)S(1)}, bf16[4,2,1,128,128]{4,3,2,1,0:T(8,128)(2,1)S(1)}, u32[]{:S(2)}, u32[]{:S(2)}) %collective-permute-start.3) | collective-permute-done | bytes 262176 | tf_op jit(solution)/shard_map/ppermute | solution.py:18
  41.6 1.2 multiply_add_fusion.1
  43.0 0.3 fusion.35
  43.4 4.7 %collective-permute-start.5 = (bf16[4,2,1,128,128]{4,3,2,1,0:T(8,128)(2,1)S(1)}, bf16[4,2,1,128,128]{4,3,2,1,0:T(8,128)(2,1)S(1)}, u32[]{:S(2)}, u32[]{:S(2)}) collective-permute-start(bf16[4,2,1,128,128]{4,3,2,1,0:T(8,128)(2,1)S(1)} %get-tuple-element.45), channel_id=1, source_target_pairs={{1,0},{2,1},{3,2},{4,3},{5,4},{6,5},{7,6},{0,7},{9,8},{10,9},{11,1... | collective-permute-start | bytes 786440 | tf_op jit(solution)/shard_map/ppermute | solution.py:18
  48.4 5.9 %collective-permute-done.4 = bf16[4,2,1,128,128]{4,3,2,1,0:T(8,128)(2,1)S(1)} collective-permute-done((bf16[4,2,1,128,128]{4,3,2,1,0:T(8,128)(2,1)S(1)}, bf16[4,2,1,128,128]{4,3,2,1,0:T(8,128)(2,1)S(1)}, u32[]{:S(2)}, u32[]{:S(2)}) %collective-permute-start.4) | collective-permute-done | bytes 262176 | tf_op jit(solution)/shard_map/ppermute | solution.py:17
  54.2 3.9 %collective-permute-done.5 = bf16[4,2,1,128,128]{4,3,2,1,0:T(8,128)(2,1)S(1)} collective-permute-done((bf16[4,2,1,128,128]{4,3,2,1,0:T(8,128)(2,1)S(1)}, bf16[4,2,1,128,128]{4,3,2,1,0:T(8,128)(2,1)S(1)}, u32[]{:S(2)}, u32[]{:S(2)}) %collective-permute-start.5) | collective-permute-done | bytes 262176 | tf_op jit(solution)/shard_map/ppermute | solution.py:18
  58.3 1.2 multiply_add_fusion
  60.0 1.5 %copy.17 = bf16[1,4,512,128]{3,1,2,0:T(4,128)(2,1)} copy(f32[1,4,512,128]{3,2,1,0:T(8,128)S(1)} %bitcast.57) | data formatting | bytes 1572864
  61.6 1.5 %reshape.73 = f32[1,4,65536]{2,1,0:T(4,128)} reshape(f32[4,2,2,128,128]{4,3,2,1,0:T(8,128)S(1)} %fusion.8) | data formatting | bytes 2097152
  63.1 19.7 %all-gather.6.cloned.1.call-done = bf16[4,4,65536]{2,1,0:T(4,128)(2,1)} async-done(((bf16[1,4,65536]{2,1,0:T(4,128)(2,1)}), bf16[4,4,65536]{2,1,0:T(4,128)(2,1)}) %all-gather.6.cloned.1.call-update) | async-done | bytes 2097168 | tf_op jit(solution)/shard_map/all_gather | solution.py:82
  82.7 2.9 %reshape.70 = bf16[16,65536]{1,0:T(8,128)(2,1)} reshape(bf16[4,4,65536]{2,1,0:T(4,128)(2,1)} %all-gather.6.cloned.1.call-done) | data formatting | bytes 4194304
  85.6 4.4 %fusion = f32[4,16]{1,0:T(4,128)S(1)} fusion(bf16[16,65536]{1,0:T(8,128)(2,1)} %reshape.70, f32[1,4,512,128]{3,2,1,0:T(8,128)S(1)} %bitcast.58), kind=kOutput, calls=%fused_computation.8 | convolution fusion | flops 50331648 | bytes 3145984 | tf_op jit(solution)/shard_map/dot_general | solution.py:80
  90.1 21.4 %psum.7 = f32[4,16]{1,0:T(4,128)S(1)} all-reduce(f32[4,16]{1,0:T(4,128)S(1)} %fusion), channel_id=1, replica_groups=mesh['vec'=4,'space'=8] {'space'}, use_global_device_ids=true, to_apply=%region_0.1 | all-reduce | flops 64 | bytes 512 | tf_op jit(solution)/shard_map/psum | solution.py:86
  111.4 5.3 %all-gather.1 = f32[4,4,16]{2,1,0:T(4,128)S(1)} all-gather(f32[1,4,16]{2,1,0:T(4,128)S(1)} %bitcast.63), channel_id=1, replica_groups=mesh['vec'=4,'space'=8] {'vec'}, dimensions={0}, use_global_device_ids=true | all-gather | bytes 1280 | tf_op jit(solution)/shard_map/all_gather | solution.py:87
  116.8 1.5 %cholesky.17 = f32[16,16]{1,0:T(8,128)S(1)} custom-call(f32[16,16]{1,0:T(8,128)S(1)} %fusion.32), custom_call_target="Cholesky" | custom-call | tf_op jit(solution)/shard_map/jit(cholesky)/cholesky | solution.py:65
  118.3 0.6 compare_reduce_fusion
  119.0 0.6 select_bitcast_fusion
  119.6 1.2 custom-call.6
  120.9 0.7 gather_fusion
  121.5 0.5 log.3
  122.3 4.4 %reshape.74 = f32[16,65536]{1,0:T(8,128)} reshape(f32[4,4,65536]{2,1,0:T(4,128)} %all-gather.8.cloned.1.call-done) | data formatting | bytes 8388608
  126.7 4.3 %convolution_bitcast_fusion = f32[1,4,512,128]{3,1,2,0:T(4,128)S(1)} fusion(f32[16,65536]{1,0:T(8,128)} %reshape.74, f32[16,16]{1,0:T(8,128)S(1)} %fusion.30, s32[]{:T(128)S(6)} %select_n.12), kind=kOutput, calls=%fused_computation.7 | convolution fusion | flops 50331648 | bytes 5244932 | tf_op jit(solution)/shard_map/dot_general | solution.py:90
  131.0 1.0 copy.9
  (36 shorter events, 3.2 us)
Async XLA Ops:
  7.2 7.6 %copy-start = (f32[4,2,2,128,128]{4,3,2,1,0:T(8,128)S(1)}, f32[4,2,2,128,128]{4,3,2,1,0:T(8,128)}, u32[]{:S(2)}) copy-start(f32[4,2,2,128,128]{4,3,2,1,0:T(8,128)} %param.2) | copy-start | bytes 3145732
  7.2 75.6 %all-gather.6.cloned.1.call-start = ((), (), s32[]{:S(2)}) async-start(), calls=%async_computation | async-start | bytes 2621440 | tf_op jit(solution)/shard_map/all_gather | solution.py:82
  8.7 15.4 %collective-permute-start = (bf16[4,2,1,128,128]{4,3,2,1,0:T(8,128)(2,1)S(1)}, bf16[4,2,1,128,128]{4,3,2,1,0:T(8,128)(2,1)S(1)}, u32[]{:S(2)}, u32[]{:S(2)}) collective-permute-start(bf16[4,2,1,128,128]{4,3,2,1,0:T(8,128)(2,1)S(1)} %get-tuple-element.48), channel_id=1, source_target_pairs={{0,1},{1,2},{2,3},{3,4},{4,5},{5,6},{6,7},{7,0},{8,9},{9,10},{10,1... | collective-permute-start | bytes 786440 | tf_op jit(solution)/shard_map/ppermute | solution.py:17
  11.7 3.3 %copy-start.1 = (bf16[3,4,2,32,128]{4,3,2,1,0:T(8,128)(2,1)S(1)}, bf16[3,4,2,32,128]{4,3,2,1,0:T(8,128)(2,1)}, u32[]{:S(2)}) copy-start(bf16[3,4,2,32,128]{4,3,2,1,0:T(8,128)(2,1)} %param.3) | copy-start | bytes 589828
  11.7 13.4 %collective-permute-start.1 = (bf16[4,2,1,128,128]{4,3,2,1,0:T(8,128)(2,1)S(1)}, bf16[4,2,1,128,128]{4,3,2,1,0:T(8,128)(2,1)S(1)}, u32[]{:S(2)}, u32[]{:S(2)}) collective-permute-start(bf16[4,2,1,128,128]{4,3,2,1,0:T(8,128)(2,1)S(1)} %get-tuple-element.49), channel_id=1, source_target_pairs={{1,0},{2,1},{3,2},{4,3},{5,4},{6,5},{7,6},{0,7},{9,8},{10,9},{11,1... | collective-permute-start | bytes 786440 | tf_op jit(solution)/shard_map/ppermute | solution.py:18
  26.9 11.1 %collective-permute-start.2 = (bf16[4,2,1,128,128]{4,3,2,1,0:T(8,128)(2,1)S(1)}, bf16[4,2,1,128,128]{4,3,2,1,0:T(8,128)(2,1)S(1)}, u32[]{:S(2)}, u32[]{:S(2)}) collective-permute-start(bf16[4,2,1,128,128]{4,3,2,1,0:T(8,128)(2,1)S(1)} %get-tuple-element.46), channel_id=1, source_target_pairs={{0,1},{1,2},{2,3},{3,4},{4,5},{5,6},{6,7},{7,0},{8,9},{9,10},{10,1... | collective-permute-start | bytes 786440 | tf_op jit(solution)/shard_map/ppermute | solution.py:17
  27.2 14.3 %collective-permute-start.3 = (bf16[4,2,1,128,128]{4,3,2,1,0:T(8,128)(2,1)S(1)}, bf16[4,2,1,128,128]{4,3,2,1,0:T(8,128)(2,1)S(1)}, u32[]{:S(2)}, u32[]{:S(2)}) collective-permute-start(bf16[4,2,1,128,128]{4,3,2,1,0:T(8,128)(2,1)S(1)} %get-tuple-element.47), channel_id=1, source_target_pairs={{1,0},{2,1},{3,2},{4,3},{5,4},{6,5},{7,6},{0,7},{9,8},{10,9},{11,1... | collective-permute-start | bytes 786440 | tf_op jit(solution)/shard_map/ppermute | solution.py:18
  43.4 10.9 %collective-permute-start.4 = (bf16[4,2,1,128,128]{4,3,2,1,0:T(8,128)(2,1)S(1)}, bf16[4,2,1,128,128]{4,3,2,1,0:T(8,128)(2,1)S(1)}, u32[]{:S(2)}, u32[]{:S(2)}) collective-permute-start(bf16[4,2,1,128,128]{4,3,2,1,0:T(8,128)(2,1)S(1)} %get-tuple-element.44), channel_id=1, source_target_pairs={{0,1},{1,2},{2,3},{3,4},{4,5},{5,6},{6,7},{7,0},{8,9},{9,10},{10,1... | collective-permute-start | bytes 786440 | tf_op jit(solution)/shard_map/ppermute | solution.py:17
  43.4 14.7 %collective-permute-start.5 = (bf16[4,2,1,128,128]{4,3,2,1,0:T(8,128)(2,1)S(1)}, bf16[4,2,1,128,128]{4,3,2,1,0:T(8,128)(2,1)S(1)}, u32[]{:S(2)}, u32[]{:S(2)}) collective-permute-start(bf16[4,2,1,128,128]{4,3,2,1,0:T(8,128)(2,1)S(1)} %get-tuple-element.45), channel_id=1, source_target_pairs={{1,0},{2,1},{3,2},{4,3},{5,4},{6,5},{7,6},{0,7},{9,8},{10,9},{11,1... | collective-permute-start | bytes 786440 | tf_op jit(solution)/shard_map/ppermute | solution.py:18
  61.5 60.7 %all-gather.8.cloned.1.call-start = ((), (), s32[]{:S(2)}) async-start(), calls=%async_computation.1 | async-start | bytes 5242880 | tf_op jit(solution)/shard_map/all_gather | solution.py:91
Sparse Core Ops, SparseCore 0:
  61.7 21.0 all-gather.5
  84.9 34.5 all-gather.7
where the time goes:
time: 139 us
  waiting for transfers between devices  40 us (29%)
  blocking collectives  35.4 us (25%)
  starting transfers between devices  15.7 us (11%)
  between operations  14.3 us (10%)
  local copies, waits for them, and re-layouts  13.3 us (10%)
  other arithmetic  11.2 us (8%)
  matrix products  8.91 us (6%)
    psum x1, blocking collectives, on_device(): summed = lax.psum(rows, 'space')  21.4 us
    all_gather x1, waiting for transfers between devices, on_device(): lax.all_gather(flat.astype(jnp.bfloat16), 'vec', axis=0, tiled=True)  19.7 us
    ppermute x3, starting transfers between devices, padded_2(): after = lax.ppermute(leading, axis, down)  12.3 us
    ppermute x3, waiting for transfers between devices, padded_2(): before = lax.ppermute(last, axis, up)  11.9 us
    unnamed x9, local copies, waits for them, and re-layouts  11.3 us
    all_gather x1, blocking collectives, on_device(): lax.all_gather(background, 'vec', axis=3, tiled=True).astype(jnp.float32)  8.74 us
    ppermute x3, waiting for transfers between devices, padded_2(): after = lax.ppermute(leading, axis, down)  8.41 us
    all_gather x1, blocking collectives, on_device(): gram = lax.all_gather(summed, 'vec', axis=0, tiled=True) / cells  5.35 us
  transfers between devices with their start and end apart: 8, of which 6 were waited for; matrix products, arithmetic and copies ran while one was open for 11% of the time, Pallas kernels for 0%

commit v1 on v0

v1 whole, which is shorter than its diff:
```python
import functools

import jax
import jax.numpy as jnp
from jax import lax
from jax.experimental import pallas as pl
from jax.experimental.pallas import tpu as pltpu
from jax.sharding import PartitionSpec as P

time_step = 0.1
diffusion = 0.5
VM = pl.BlockSpec(memory_space=pltpu.VMEM)
SM = pl.BlockSpec(memory_space=pltpu.SMEM)
PARAMS = pltpu.CompilerParams(vmem_limit_bytes=40 * 1024 * 1024)
PAD = 8
CHUNK = 16


def stage_rows(src, first, bgs, bg_first, alpha, beta, keep, keep_first, rows, vectors, store):
    columns = src.shape[2] - 2 * PAD
    levels = src.shape[3]
    h = beta * time_step
    lane = lax.broadcasted_iota(jnp.int32, (CHUNK, levels), 1)

    def one_row(row, carry):
        at = row + first
        for x in range(0, columns, CHUNK):
            quarter, inner = divmod(x, bgs.shape[3])
            u, v, r, s = (
                bgs[bg_first + row, f, quarter, inner : inner + CHUNK, :].astype(jnp.float32)
                for f in range(4)
            )
            hu, hv, hr, hs = (0.5 * h) * u, (0.5 * h) * v, (0.5 * h) * r, h * s
            lap = diffusion * h
            xn_c, xp_c = lap - hu, lap + hu
            yn_c, yp_c = lap - hv, lap + hv
            zn_c = jnp.where(lane == levels - 1, 0.0, lap - hr)
            zp_c = jnp.where(lane == 0, 0.0, lap + hr)
            mid = beta - 6.0 * lap
            lo = PAD + x
            for vector in range(vectors):
                centers = [src[at, 2 * vector + f, lo : lo + CHUNK, :] for f in range(2)]
                for f in range(2):
                    k = 2 * vector + f
                    c = centers[f]
                    total = xn_c * src[at, k, lo + 1 : lo + 1 + CHUNK, :]
                    total += xp_c * src[at, k, lo - 1 : lo - 1 + CHUNK, :]
                    total += yn_c * src[at + 1, k, lo : lo + CHUNK, :]
                    total += yp_c * src[at - 1, k, lo : lo + CHUNK, :]
                    total += zn_c * pltpu.roll(c, levels - 1, 1)
                    total += zp_c * pltpu.roll(c, 1, 1)
                    total += mid * c
                    if f == 0:
                        total += h * centers[1]
                    else:
                        total -= hs * centers[0]
                    if alpha:
                        total += alpha * keep[row + keep_first, k, lo : lo + CHUNK, :]
                    store(row, vector, f, x, total)
        return carry

    lax.fori_loop(0, rows, one_row, 0)


def wrap(ref, columns):
    ref[:, :, PAD - 1 : PAD, :] = ref[:, :, PAD + columns - 1 : PAD + columns, :]
    ref[:, :, PAD + columns : PAD + columns + 1, :] = ref[:, :, PAD : PAD + 1, :]


def advance_kernel(me, own, up1, dn1, up2, dn2, bg0, bg2, bg13, adv, q0, q1, q2, q3, p0, p1, p2, bgs):
    vectors, _, rows, columns, _ = own.shape
    position = me[0]
    bgs[:, :, position] = bg0[...]
    bgs[:, :, position ^ 2] = bg2[...]
    bgs[:, :, position ^ 1] = bg13[0]
    bgs[:, :, position ^ 3] = bg13[1]
    for vector in range(vectors):
        for f in range(2):
            k = 2 * vector + f
            cells = slice(PAD, PAD + columns)
            p0[0, k, cells, :] = up2[vector, f].astype(jnp.float32)
            p0[7, k, cells, :] = dn2[vector, f].astype(jnp.float32)
            for row in range(2):
                p0[1 + row, k, cells, :] = up1[vector, f, row].astype(jnp.float32)
                p0[3 + row, k, cells, :] = own[vector, f, row]
                p0[5 + row, k, cells, :] = dn1[vector, f, row].astype(jnp.float32)
    wrap(p0, columns)

    def to(ref):
        def store(row, vector, f, x, value):
            ref[row, 2 * vector + f, PAD + x : PAD + x + CHUNK, :] = value

        return store

    def to_out(row, vector, f, x, value):
        adv[vector, f, row, x : x + CHUNK, :] = value

    stage_rows(p0, 1, bgs, 0, 0.0, 1.0, None, 0, 6, vectors, to(p1))
    wrap(p1, columns)
    stage_rows(p1, 1, bgs, 6, 0.75, 0.25, p0, 2, 4, vectors, to(p2))
    wrap(p2, columns)
    stage_rows(p2, 1, bgs, 10, 1.0 / 3.0, 2.0 / 3.0, p0, 3, 2, vectors, to_out)
    for b, q in enumerate((q0, q1, q2, q3)):
        part = position ^ b
        for vector in range(vectors):
            q[vector] = adv[vector, part // 2, part % 2].astype(jnp.bfloat16)


def gram_kernel(me, q0, q1, q2, q3, out, flat):
    vectors, columns, levels = q0.shape
    position = me[0]
    for b, q in enumerate((q0, q1, q2, q3)):
        block = position ^ b
        for vector in range(vectors):
            flat[block * vectors + vector] = q[vector].astype(jnp.float32)
    count = vectors * 4
    rows = flat.reshape(count * columns, levels)
    total = jnp.zeros((count, count), jnp.float32)
    for x in range(0, columns, 2):
        part = jnp.concatenate(
            [rows[pl.ds(x + i, count, stride=columns), :].astype(jnp.bfloat16) for i in range(2)], 1
        )
        total += lax.dot_general(
            part, part, (((1,), (1,)), ((), ())), preferred_element_type=jnp.float32
        )
    out[...] = total


def final_kernel(scale, me, gram, own, r1, r2, r3, basis, growth, inv):
    vectors = own.shape[0]
    count = gram.shape[0]
    position = me[0]
    row = lax.broadcasted_iota(jnp.int32, (count, 2 * count), 0)
    lane = lax.broadcasted_iota(jnp.int32, (count, 2 * count), 1)
    unit = lane - count
    column = ((unit // vectors) ^ position) * vectors + unit % vectors
    eye = jnp.where((lane >= count) & (row == column), 1.0, 0.0)
    table = jnp.concatenate([gram[...] * scale, jnp.zeros((count, count), jnp.float32)], 1) + eye
    pivots = jnp.zeros((1, count), jnp.float32)
    wide = lax.broadcasted_iota(jnp.int32, (1, count), 1)
    for k in range(count):
        pivot = table[k : k + 1, k : k + 1]
        pivots = jnp.where(wide == k, pivot, pivots)
        scaled = table[k : k + 1, :] / jnp.sqrt(pivot)
        below = jnp.where(row[:, :1] > k, table[:, k : k + 1] / jnp.sqrt(pivot), 0.0)
        table = jnp.where(row == k, scaled, table - below * scaled)
    growth[...] = 0.5 * jnp.log(pivots)
    inv[...] = table
    for first in range(0, vectors, 2):
        weights = []
        for i in range(first, first + 2):
            line = inv[pl.ds(position * vectors + i, 1), :]
            weights.append(
                [
                    jnp.broadcast_to(line[:, count + j : count + j + 1], (8, own.shape[4]))
                    for j in range(count)
                ]
            )
        for f in range(own.shape[1]):
            for y in range(own.shape[2]):

                def tile(t, carry, f=f, y=y, first=first, weights=weights):
                    at = pl.ds(pl.multiple_of(t * 8, 8), 8)
                    values = [
                        ref[j, f, y, at, :] for ref in (own, r1, r2, r3) for j in range(vectors)
                    ]
                    for i in range(2):
                        parts = [w * value for w, value in zip(weights[i], values)]
                        while len(parts) > 1:
                            parts = [a + b for a, b in zip(parts[::2], parts[1::2])]
                        basis[first + i, f, y, at, :] = parts[0]
                    return carry

                lax.fori_loop(0, own.shape[3] // 8, tile, 0, unroll=4)


def shift(value, axis, step):
    count = lax.axis_size(axis)
    return lax.ppermute(value, axis, [(i, (i + step) % count) for i in range(count)])


def swap(value, axis, mask):
    return lax.ppermute(value, axis, [(i, i ^ mask) for i in range(lax.axis_size(axis))])


def summed(value):
    value = (value + swap(value, "vec", 1)) + (swap(value, "vec", 2) + swap(value, "vec", 3))
    mask = 1
    while mask < lax.axis_size("space"):
        value = value + swap(value, "space", mask)
        mask *= 2
    return value


def on_device(tangents, background):
    vectors, fields, rows, columns, levels = tangents.shape
    count = vectors * lax.axis_size("vec")
    cells = fields * rows * columns * levels * lax.axis_size("space")
    me = lax.axis_index("vec").astype(jnp.int32).reshape(1)

    narrow = tangents.astype(jnp.bfloat16)
    bg = jnp.swapaxes(background, 1, 2)
    bg_up = shift(jnp.concatenate([bg[0], bg[1, 1:]]), "space", 1)
    bg_dn = shift(jnp.concatenate([bg[0], bg[1, :1]]), "space", -1)
    up1 = shift(narrow, "space", 1)
    dn1 = shift(narrow, "space", -1)
    up2 = shift(narrow[:, :, 1], "space", 2)
    dn2 = shift(narrow[:, :, 0], "space", -2)
    bg0 = jnp.concatenate([bg_up[:2], bg[0], bg_dn[:2], bg_up[2:], bg[1], bg_dn[2:], bg[2]])
    bg2 = swap(bg0, "vec", 2)
    bg13 = swap(jnp.stack([bg0, bg2]), "vec", 1)

    quarter = jax.ShapeDtypeStruct((vectors, columns, levels), jnp.bfloat16)
    fields_all = 2 * vectors
    adv, q0, q1, q2, q3 = pl.pallas_call(
        advance_kernel,
        out_shape=[jax.ShapeDtypeStruct(tangents.shape, jnp.float32)] + [quarter] * 4,
        in_specs=[SM] + [VM] * 8,
        out_specs=[VM] * 5,
        scratch_shapes=[
            pltpu.VMEM((8, fields_all, columns + 2 * PAD, levels), jnp.float32),
            pltpu.VMEM((6, fields_all, columns + 2 * PAD, levels), jnp.float32),
            pltpu.VMEM((4, fields_all, columns + 2 * PAD, levels), jnp.float32),
            pltpu.VMEM((12, 4, 4, columns // 4, levels), jnp.bfloat16),
        ],
        compiler_params=PARAMS,
        name="advance",
    )(me, tangents, up1, dn1, up2, dn2, bg0, bg2, bg13)

    q1, q2, q3 = swap(q1, "vec", 1), swap(q2, "vec", 2), swap(q3, "vec", 3)
    r2 = lax.ppermute(adv, "vec", [(0, 2), (1, 3)])
    r1 = lax.ppermute(adv, "vec", [(0, 1), (2, 3)])
    r3 = lax.ppermute(r2, "vec", [(2, 3), (3, 2)])

    gram = pl.pallas_call(
        gram_kernel,
        out_shape=jax.ShapeDtypeStruct((count, count), jnp.float32),
        in_specs=[SM] + [VM] * 4,
        out_specs=VM,
        scratch_shapes=[pltpu.VMEM((count, columns, levels), jnp.float32)],
        compiler_params=PARAMS,
        name="gram",
    )(me, q0, q1, q2, q3)
    gram = summed(gram)

    basis, growth = pl.pallas_call(
        functools.partial(final_kernel, 1.0 / cells),
        out_shape=[
            jax.ShapeDtypeStruct(tangents.shape, jnp.float32),
            jax.ShapeDtypeStruct((1, count), jnp.float32),
        ],
        in_specs=[SM] + [VM] * 5,
        out_specs=[VM, VM],
        scratch_shapes=[pltpu.VMEM((count, 2 * count), jnp.float32)],
        compiler_params=PARAMS,
        name="final",
    )(me, gram, adv, r1, r2, r3)
    return basis, growth.reshape(count)


def solution(mesh):
    in_specs = (P("vec", None, "space", None, None), P(None, None, "space", "vec", None))
    out_specs = (P("vec", None, "space", None, None), P())
    return jax.shard_map(
        on_device, mesh=mesh, in_specs=in_specs, out_specs=out_specs, check_vma=False
    )
```

time: 139 us -> 118 us (0.85)
  blocking collectives: 35.4 us -> 0 us
  waiting for transfers between devices: 40 us -> 69.3 us
  starting transfers between devices: 15.7 us -> 31.3 us
  between operations: 14.3 us -> 0.78 us
  other arithmetic: 11.2 us -> 0.98 us
  Pallas kernels: 0 us -> 10.1 us
  matrix products: 8.91 us -> 0 us
  local copies, waits for them, and re-layouts: 13.3 us -> 4.91 us
    ppermute x6 -> x20, waiting for transfers between devices: 20.3 us -> 69.3 us  [the longest x11 25.8 us: swap(): lax.ppermute(value, axis, [(i, i ^ mask) for i in range(lax.axis_size(axi...]
    psum x1 -> x0, blocking collectives: 21.4 us -> none  [on_device(): summed = lax.psum(rows, 'space')]
    all_gather x2 -> x0, waiting for transfers between devices: 19.7 us -> none  [the longest x1 19.7 us: on_device(): lax.all_gather(flat.astype(jnp.bfloat16), 'vec', axis=0, tiled=True)]
    ppermute x6 -> x20, starting transfers between devices: 15.6 us -> 31.3 us  [the longest x11 12.9 us: swap(): lax.ppermute(value, axis, [(i, i ^ mask) for i in range(lax.axis_size(axi...]
    all_gather x2 -> x0, blocking collectives: 14.1 us -> none  [the longest x1 8.74 us: on_device(): lax.all_gather(background, 'vec', axis=3, tiled=True).astype(jnp.float32)]
    pallas_call x0 -> x3, Pallas kernels: none -> 10.1 us  [the longest x1 4.9 us: on_device(): pl.pallas_call(advance_kernel, out_shape=[jax.ShapeDtypeStruct(tangents.s...]
    unnamed x9 -> x10, local copies, waits for them, and re-layouts: 11.3 us -> 1.91 us
    dot_general x2 -> x0, matrix products: 8.72 us -> none  [the longest x1 4.45 us: on_device(): jnp.dot(flat, lax.all_gather(flat.astype(jnp.bfloat16), 'vec', axis=0, ti...]
  transfers between devices with their start and end apart: 8 -> 20, of which waited for: 6 -> 13; matrix products, arithmetic and copies ran while one was open for 11% -> 3% of each run, Pallas kernels for 0% -> 1%
where the time goes in v1:
time: 118 us; the launch traced here: 117 us
  waiting for transfers between devices  69.3 us (59%)
  starting transfers between devices  31.3 us (27%)
  Pallas kernels  10.1 us (9%)
  local copies, waits for them, and re-layouts  4.91 us (4%)
    ppermute x11, waiting for transfers between devices, swap(): lax.ppermute(value, axis, [(i, i ^ mask) for i in range(lax.axis_size(axi...  25.8 us
    ppermute x6, waiting for transfers between devices, shift(): lax.ppermute(value, axis, [(i, (i + step) % count) for i in range(count)])  22.6 us
    ppermute x1, waiting for transfers between devices, on_device(): r2 = lax.ppermute(adv, 'vec', [(0, 2), (1, 3)])  20.8 us
    ppermute x11, starting transfers between devices, swap(): lax.ppermute(value, axis, [(i, i ^ mask) for i in range(lax.axis_size(axi...  12.9 us
    ppermute x6, starting transfers between devices, shift(): lax.ppermute(value, axis, [(i, (i + step) % count) for i in range(count)])  12.6 us
    pallas_call x1, Pallas kernels, on_device(): pl.pallas_call(advance_kernel, out_shape=[jax.ShapeDtypeStruct(tangents.s...  4.9 us
    pallas_call x1, Pallas kernels, on_device(): pl.pallas_call(functools.partial(final_kernel, 1.0 / cells), out_shape=[j...  4.45 us
    ppermute x1, starting transfers between devices, on_device(): r2 = lax.ppermute(adv, 'vec', [(0, 2), (1, 3)])  3.49 us
  transfers between devices with their start and end apart: 20, of which 13 were waited for; matrix products, arithmetic and copies ran while one was open for 3% of the time, Pallas kernels for 1%

profile of v1, /device:TPU:0, one launch (start us, length us, event | category | flops | bytes accessed | tf_op | source)
XLA Modules:
  0.0 117.3 jit_solution(17433505609560929954)
XLA Ops:
  0.6 0.9 copy.13
  1.6 3.0 %collective-permute-start.4 = (bf16[3,4,32,128]{3,2,1,0:T(8,128)(2,1)S(1)}, bf16[3,4,32,128]{3,2,1,0:T(8,128)(2,1)S(1)}, u32[]{:S(2)}, u32[]{:S(2)}) collective-permute-start(bf16[3,4,32,128]{3,2,1,0:T(8,128)(2,1)S(1)} %get-tuple-element.21), channel_id=1, source_target_pairs={{0,1},{1,2},{2,3},{3,4},{4,5},{5,6},{6,7},{7,0},{8,9},{9,10},{10,1... | collective-permute-start | bytes 294920 | tf_op jit(solution)/shard_map/ppermute | solution.py:179
  4.6 3.1 %collective-permute-start.5 = (bf16[3,4,32,128]{3,2,1,0:T(8,128)(2,1)S(1)}, bf16[3,4,32,128]{3,2,1,0:T(8,128)(2,1)S(1)}, u32[]{:S(2)}, u32[]{:S(2)}) collective-permute-start(bf16[3,4,32,128]{3,2,1,0:T(8,128)(2,1)S(1)} %get-tuple-element.20), channel_id=1, source_target_pairs={{0,7},{1,0},{2,1},{3,2},{4,3},{5,4},{6,5},{7,6},{8,15},{9,8},{10,9... | collective-permute-start | bytes 294920 | tf_op jit(solution)/shard_map/ppermute | solution.py:179
  7.7 2.8 %collective-permute-done.4 = bf16[3,4,32,128]{3,2,1,0:T(8,128)(2,1)S(1)} collective-permute-done((bf16[3,4,32,128]{3,2,1,0:T(8,128)(2,1)S(1)}, bf16[3,4,32,128]{3,2,1,0:T(8,128)(2,1)S(1)}, u32[]{:S(2)}, u32[]{:S(2)}) %collective-permute-start.4) | collective-permute-done | bytes 98336 | tf_op jit(solution)/shard_map/ppermute | solution.py:179
  10.6 0.8 collective-permute-done.5
  11.4 1.6 %collective-permute-start.6 = (bf16[12,4,32,128]{3,2,1,0:T(8,128)(2,1)S(1)}, bf16[12,4,32,128]{3,2,1,0:T(8,128)(2,1)S(1)}, u32[]{:S(2)}, u32[]{:S(2)}) collective-permute-start(bf16[12,4,32,128]{3,2,1,0:T(8,128)(2,1)S(1)} %fusion.bg0), channel_id=1, source_target_pairs={{0,16},{8,24},{16,0},{24,8},{1,17},{9,25},{17,1},{25,9},{2,18},{10... | collective-permute-start | bytes 1179656 | tf_op jit(solution)/shard_map/ppermute | solution.py:183
  13.0 7.9 %collective-permute-done.6.bg2 = bf16[12,4,32,128]{3,2,1,0:T(8,128)(2,1)S(1)} collective-permute-done((bf16[12,4,32,128]{3,2,1,0:T(8,128)(2,1)S(1)}, bf16[12,4,32,128]{3,2,1,0:T(8,128)(2,1)S(1)}, u32[]{:S(2)}, u32[]{:S(2)}) %collective-permute-start.6) | collective-permute-done | bytes 393248 | tf_op jit(solution)/shard_map/ppermute | solution.py:183
  20.9 0.9 pad_maximum_fusion
  21.9 0.9 copy.10
  22.8 3.9 %collective-permute-start.1 = (bf16[4,2,2,128,128]{4,3,1,0,2:T(8,128)(2,1)}, bf16[4,2,2,128,128]{4,3,1,0,2:T(8,128)(2,1)}, u32[]{:S(2)}, u32[]{:S(2)}) collective-permute-start(bf16[4,2,2,128,128]{4,3,1,0,2:T(8,128)(2,1)} %copy.10), channel_id=1, source_target_pairs={{0,7},{1,0},{2,1},{3,2},{4,3},{5,4},{6,5},{7,6},{8,15},{9,8},{10,9... | collective-permute-start | bytes 1572872 | tf_op jit(solution)/shard_map/ppermute | solution.py:179
  26.7 0.8 slice_bitcast_fusion
  27.6 2.6 %collective-permute-start.3 = (bf16[4,2,128,128]{3,2,1,0:T(8,128)(2,1)}, bf16[4,2,128,128]{3,2,1,0:T(8,128)(2,1)S(1)}, u32[]{:S(2)}, u32[]{:S(2)}) collective-permute-start(bf16[4,2,128,128]{3,2,1,0:T(8,128)(2,1)} %get-tuple-element.16), channel_id=1, source_target_pairs={{0,6},{1,7},{2,0},{3,1},{4,2},{5,3},{6,4},{7,5},{8,14},{9,15},{10,... | collective-permute-start | bytes 786440 | tf_op jit(solution)/shard_map/ppermute | solution.py:179
  30.1 18.6 %collective-permute-done.1 = bf16[4,2,2,128,128]{4,3,1,0,2:T(8,128)(2,1)} collective-permute-done((bf16[4,2,2,128,128]{4,3,1,0,2:T(8,128)(2,1)}, bf16[4,2,2,128,128]{4,3,1,0,2:T(8,128)(2,1)}, u32[]{:S(2)}, u32[]{:S(2)}) %collective-permute-start.1) | collective-permute-done | bytes 524320 | tf_op jit(solution)/shard_map/ppermute | solution.py:179
  48.7 1.1 copy.7.dn1
  49.8 1.1 copy.6.up1
  51.4 4.9 %advance.1 = (f32[4,2,2,128,128]{4,3,2,1,0:T(8,128)S(1)}, bf16[4,128,128]{2,1,0:T(8,128)(2,1)S(1)}, bf16[4,128,128]{2,1,0:T(8,128)(2,1)S(1)}, bf16[4,128,128]{2,1,0:T(8,128)(2,1)S(1)}, bf16[4,128,128]{2,1,0:T(8,128)(2,1)S(1)}) custom-call(s32[1]{0:T(128)} %bitcast.me, f32[4,2,2,128,128]{4,3,2,1,0:T(8,128)S(1)} %copy-done, ...), custom_call_target="tpu_custom_call" | custom-call | tf_op jit(solution)/shard_map/advance/pallas_call | solution.py:215
  56.3 3.5 %collective-permute-start.18 = (f32[4,2,2,128,128]{4,3,2,1,0:T(8,128)S(1)}, f32[4,2,2,128,128]{4,3,2,1,0:T(8,128)S(1)}, u32[]{:S(2)}, u32[]{:S(2)}) collective-permute-start(f32[4,2,2,128,128]{4,3,2,1,0:T(8,128)S(1)} %get-tuple-element.13.own), channel_id=1, source_target_pairs={{0,16},{8,24},{1,17},{9,25},{2,18},{10,26},{3,19},{11,27},{4,20},{... | collective-permute-start | bytes 3145736 | tf_op jit(solution)/shard_map/ppermute | solution.py:231
  59.8 1.6 %collective-permute-start.17 = (f32[4,2,2,128,128]{4,3,2,1,0:T(8,128)S(1)}, f32[4,2,2,128,128]{4,3,2,1,0:T(8,128)S(1)}, u32[]{:S(2)}, u32[]{:S(2)}) collective-permute-start(f32[4,2,2,128,128]{4,3,2,1,0:T(8,128)S(1)} %get-tuple-element.13.own), channel_id=1, source_target_pairs={{0,8},{16,24},{1,9},{17,25},{2,10},{18,26},{3,11},{19,27},{4,12},{... | collective-permute-start | bytes 3145736 | tf_op jit(solution)/shard_map/ppermute | solution.py:232
  61.4 20.8 %collective-permute-done.18.r2 = f32[4,2,2,128,128]{4,3,2,1,0:T(8,128)S(1)} collective-permute-done((f32[4,2,2,128,128]{4,3,2,1,0:T(8,128)S(1)}, f32[4,2,2,128,128]{4,3,2,1,0:T(8,128)S(1)}, u32[]{:S(2)}, u32[]{:S(2)}) %collective-permute-start.18) | collective-permute-done | bytes 1048608 | tf_op jit(solution)/shard_map/ppermute | solution.py:231
  83.0 4.2 %collective-permute-start.9 = (bf16[4,128,128]{2,1,0:T(8,128)(2,1)S(1)}, bf16[4,128,128]{2,1,0:T(8,128)(2,1)S(1)}, u32[]{:S(2)}, u32[]{:S(2)}) collective-permute-start(bf16[4,128,128]{2,1,0:T(8,128)(2,1)S(1)} %get-tuple-element.11), channel_id=1, source_target_pairs={{0,16},{8,24},{16,0},{24,8},{1,17},{9,25},{17,1},{25,9},{2,18},{10... | collective-permute-start | bytes 393224 | tf_op jit(solution)/shard_map/ppermute | solution.py:183
  87.2 4.3 %collective-permute-done.9.q2 = bf16[4,128,128]{2,1,0:T(8,128)(2,1)S(1)} collective-permute-done((bf16[4,128,128]{2,1,0:T(8,128)(2,1)S(1)}, bf16[4,128,128]{2,1,0:T(8,128)(2,1)S(1)}, u32[]{:S(2)}, u32[]{:S(2)}) %collective-permute-start.9) | collective-permute-done | bytes 131104 | tf_op jit(solution)/shard_map/ppermute | solution.py:183
  91.4 1.7 %collective-permute-done.10.q3 = bf16[4,128,128]{2,1,0:T(8,128)(2,1)S(1)} collective-permute-done((bf16[4,128,128]{2,1,0:T(8,128)(2,1)S(1)}, bf16[4,128,128]{2,1,0:T(8,128)(2,1)S(1)}, u32[]{:S(2)}, u32[]{:S(2)}) %collective-permute-start.10) | collective-permute-done | bytes 131104 | tf_op jit(solution)/shard_map/ppermute | solution.py:183
  93.2 0.7 gram.1
  93.9 1.7 %collective-permute-start.13 = (f32[16,16]{1,0:T(8,128)S(1)}, f32[16,16]{1,0:T(8,128)S(1)}, u32[]{:S(2)}, u32[]{:S(2)}) collective-permute-start(f32[16,16]{1,0:T(8,128)S(1)} %gram.1), channel_id=1, source_target_pairs={{0,24},{8,16},{16,8},{24,0},{1,25},{9,17},{17,9},{25,1},{2,26},{10... | collective-permute-start | bytes 3080 | tf_op jit(solution)/shard_map/ppermute | solution.py:183
  95.9 1.1 collective-permute-done.13
  97.0 2.3 %collective-permute-done.12 = f32[16,16]{1,0:T(8,128)S(1)} collective-permute-done((f32[16,16]{1,0:T(8,128)S(1)}, f32[16,16]{1,0:T(8,128)S(1)}, u32[]{:S(2)}, u32[]{:S(2)}) %collective-permute-start.12) | collective-permute-done | bytes 1056 | tf_op jit(solution)/shard_map/ppermute | solution.py:183
  99.3 3.7 %collective-permute-start.14 = (f32[16,16]{1,0:T(8,128)S(1)}, f32[16,16]{1,0:T(8,128)S(1)}, u32[]{:S(2)}, u32[]{:S(2)}) collective-permute-start(f32[16,16]{1,0:T(8,128)S(1)} %add_add_fusion), channel_id=1, source_target_pairs={{0,1},{1,0},{2,3},{3,2},{4,5},{5,4},{6,7},{7,6},{8,9},{9,8},{10,11... | collective-permute-start | bytes 3080 | tf_op jit(solution)/shard_map/ppermute | solution.py:183
  103.0 1.6 %collective-permute-done.14 = f32[16,16]{1,0:T(8,128)S(1)} collective-permute-done((f32[16,16]{1,0:T(8,128)S(1)}, f32[16,16]{1,0:T(8,128)S(1)}, u32[]{:S(2)}, u32[]{:S(2)}) %collective-permute-start.14) | collective-permute-done | bytes 1056 | tf_op jit(solution)/shard_map/ppermute | solution.py:183
  104.8 3.5 %collective-permute-done.15 = f32[16,16]{1,0:T(8,128)S(1)} collective-permute-done((f32[16,16]{1,0:T(8,128)S(1)}, f32[16,16]{1,0:T(8,128)S(1)}, u32[]{:S(2)}, u32[]{:S(2)}) %collective-permute-start.15) | collective-permute-done | bytes 1056 | tf_op jit(solution)/shard_map/ppermute | solution.py:183
  108.3 1.2 collective-permute-start.16
  109.5 3.4 %collective-permute-done.16 = f32[16,16]{1,0:T(8,128)S(1)} collective-permute-done((f32[16,16]{1,0:T(8,128)S(1)}, f32[16,16]{1,0:T(8,128)S(1)}, u32[]{:S(2)}, u32[]{:S(2)}) %collective-permute-start.16) | collective-permute-done | bytes 1056 | tf_op jit(solution)/shard_map/ppermute | solution.py:183
  112.9 4.4 %final.1 = (f32[4,2,2,128,128]{4,3,2,1,0:T(8,128)}, f32[1,16]{1,0:T(1,128)}) custom-call(s32[1]{0:T(128)} %bitcast.me, f32[16,16]{1,0:T(8,128)S(1)} %add.23.gram, f32[4,2,2,128,128]{4,3,2,1,0:T(8,128)S(1)} %get-tuple-element.13.own, f32[4,2,2,128,128]{4,3,2,1,0:T(8,128)S(1)} %collective-permute-done.17.r1, ...), custom_call_target="tpu_custom_call" | custom-call | tf_op jit(solution)/shard_map/final/pallas_call | solution.py:246
  (33 shorter events, 1.9 us)
Async XLA Ops:
  1.6 8.9 %collective-permute-start.4 = (bf16[3,4,32,128]{3,2,1,0:T(8,128)(2,1)S(1)}, bf16[3,4,32,128]{3,2,1,0:T(8,128)(2,1)S(1)}, u32[]{:S(2)}, u32[]{:S(2)}) collective-permute-start(bf16[3,4,32,128]{3,2,1,0:T(8,128)(2,1)S(1)} %get-tuple-element.21), channel_id=1, source_target_pairs={{0,1},{1,2},{2,3},{3,4},{4,5},{5,6},{6,7},{7,0},{8,9},{9,10},{10,1... | collective-permute-start | bytes 294920 | tf_op jit(solution)/shard_map/ppermute | solution.py:179
  4.6 6.7 %collective-permute-start.5 = (bf16[3,4,32,128]{3,2,1,0:T(8,128)(2,1)S(1)}, bf16[3,4,32,128]{3,2,1,0:T(8,128)(2,1)S(1)}, u32[]{:S(2)}, u32[]{:S(2)}) collective-permute-start(bf16[3,4,32,128]{3,2,1,0:T(8,128)(2,1)S(1)} %get-tuple-element.20), channel_id=1, source_target_pairs={{0,7},{1,0},{2,1},{3,2},{4,3},{5,4},{6,5},{7,6},{8,15},{9,8},{10,9... | collective-permute-start | bytes 294920 | tf_op jit(solution)/shard_map/ppermute | solution.py:179
  10.6 11.3 %copy-start = (f32[4,2,2,128,128]{4,3,2,1,0:T(8,128)S(1)}, f32[4,2,2,128,128]{4,3,2,1,0:T(8,128)}, u32[]{:S(2)}) copy-start(f32[4,2,2,128,128]{4,3,2,1,0:T(8,128)} %own.1) | copy-start | bytes 3145732
  11.4 9.5 %collective-permute-start.6 = (bf16[12,4,32,128]{3,2,1,0:T(8,128)(2,1)S(1)}, bf16[12,4,32,128]{3,2,1,0:T(8,128)(2,1)S(1)}, u32[]{:S(2)}, u32[]{:S(2)}) collective-permute-start(bf16[12,4,32,128]{3,2,1,0:T(8,128)(2,1)S(1)} %fusion.bg0), channel_id=1, source_target_pairs={{0,16},{8,24},{16,0},{24,8},{1,17},{9,25},{17,1},{25,9},{2,18},{10... | collective-permute-start | bytes 1179656 | tf_op jit(solution)/shard_map/ppermute | solution.py:183
  21.9 29.5 %collective-permute-start.7 = (bf16[2,12,4,32,128]{4,3,2,1,0:T(8,128)(2,1)}, bf16[2,12,4,32,128]{4,3,2,1,0:T(8,128)(2,1)S(1)}, u32[]{:S(2)}, u32[]{:S(2)}) collective-permute-start(bf16[2,12,4,32,128]{4,3,2,1,0:T(8,128)(2,1)} %pad_maximum_fusion), channel_id=1, source_target_pairs={{0,8},{8,0},{16,24},{24,16},{1,9},{9,1},{17,25},{25,17},{2,10},{10... | collective-permute-start | bytes 2359304 | tf_op jit(solution)/shard_map/ppermute | solution.py:183
  22.8 25.9 %collective-permute-start.1 = (bf16[4,2,2,128,128]{4,3,1,0,2:T(8,128)(2,1)}, bf16[4,2,2,128,128]{4,3,1,0,2:T(8,128)(2,1)}, u32[]{:S(2)}, u32[]{:S(2)}) collective-permute-start(bf16[4,2,2,128,128]{4,3,1,0,2:T(8,128)(2,1)} %copy.10), channel_id=1, source_target_pairs={{0,7},{1,0},{2,1},{3,2},{4,3},{5,4},{6,5},{7,6},{8,15},{9,8},{10,9... | collective-permute-start | bytes 1572872 | tf_op jit(solution)/shard_map/ppermute | solution.py:179
  26.7 23.0 %collective-permute-start = (bf16[4,2,2,128,128]{4,3,1,0,2:T(8,128)(2,1)}, bf16[4,2,2,128,128]{4,3,1,0,2:T(8,128)(2,1)}, u32[]{:S(2)}, u32[]{:S(2)}) collective-permute-start(bf16[4,2,2,128,128]{4,3,1,0,2:T(8,128)(2,1)} %copy.10), channel_id=1, source_target_pairs={{0,1},{1,2},{2,3},{3,4},{4,5},{5,6},{6,7},{7,0},{8,9},{9,10},{10,1... | collective-permute-start | bytes 1572872 | tf_op jit(solution)/shard_map/ppermute | solution.py:179
  27.6 23.3 %collective-permute-start.3 = (bf16[4,2,128,128]{3,2,1,0:T(8,128)(2,1)}, bf16[4,2,128,128]{3,2,1,0:T(8,128)(2,1)S(1)}, u32[]{:S(2)}, u32[]{:S(2)}) collective-permute-start(bf16[4,2,128,128]{3,2,1,0:T(8,128)(2,1)} %get-tuple-element.16), channel_id=1, source_target_pairs={{0,6},{1,7},{2,0},{3,1},{4,2},{5,3},{6,4},{7,5},{8,14},{9,15},{10,... | collective-permute-start | bytes 786440 | tf_op jit(solution)/shard_map/ppermute | solution.py:179
  30.1 21.3 %collective-permute-start.2 = (bf16[4,2,128,128]{3,2,1,0:T(8,128)(2,1)S(1)}, bf16[4,2,128,128]{3,2,1,0:T(8,128)(2,1)S(1)}, u32[]{:S(2)}, u32[]{:S(2)}) collective-permute-start(bf16[4,2,128,128]{3,2,1,0:T(8,128)(2,1)S(1)} %get-tuple-element.17), channel_id=1, source_target_pairs={{0,2},{1,3},{2,4},{3,5},{4,6},{5,7},{6,0},{7,1},{8,10},{9,11},{10,... | collective-permute-start | bytes 786440 | tf_op jit(solution)/shard_map/ppermute | solution.py:179
  56.3 25.9 %collective-permute-start.18 = (f32[4,2,2,128,128]{4,3,2,1,0:T(8,128)S(1)}, f32[4,2,2,128,128]{4,3,2,1,0:T(8,128)S(1)}, u32[]{:S(2)}, u32[]{:S(2)}) collective-permute-start(f32[4,2,2,128,128]{4,3,2,1,0:T(8,128)S(1)} %get-tuple-element.13.own), channel_id=1, source_target_pairs={{0,16},{8,24},{1,17},{9,25},{2,18},{10,26},{3,19},{11,27},{4,20},{... | collective-permute-start | bytes 3145736 | tf_op jit(solution)/shard_map/ppermute | solution.py:231
  59.8 53.1 %collective-permute-start.17 = (f32[4,2,2,128,128]{4,3,2,1,0:T(8,128)S(1)}, f32[4,2,2,128,128]{4,3,2,1,0:T(8,128)S(1)}, u32[]{:S(2)}, u32[]{:S(2)}) collective-permute-start(f32[4,2,2,128,128]{4,3,2,1,0:T(8,128)S(1)} %get-tuple-element.13.own), channel_id=1, source_target_pairs={{0,8},{16,24},{1,9},{17,25},{2,10},{18,26},{3,11},{19,27},{4,12},{... | collective-permute-start | bytes 3145736 | tf_op jit(solution)/shard_map/ppermute | solution.py:232
  82.2 30.7 %collective-permute-start.19 = (f32[4,2,2,128,128]{4,3,2,1,0:T(8,128)S(1)}, f32[4,2,2,128,128]{4,3,2,1,0:T(8,128)S(1)}, u32[]{:S(2)}, u32[]{:S(2)}) collective-permute-start(f32[4,2,2,128,128]{4,3,2,1,0:T(8,128)S(1)} %collective-permute-done.18.r2), channel_id=1, source_target_pairs={{16,24},{24,16},{17,25},{25,17},{18,26},{26,18},{19,27},{27,19},{2... | collective-permute-start | bytes 3145736 | tf_op jit(solution)/shard_map/ppermute | solution.py:233
  82.9 4.2 %collective-permute-start.8 = (bf16[4,128,128]{2,1,0:T(8,128)(2,1)S(1)}, bf16[4,128,128]{2,1,0:T(8,128)(2,1)S(1)}, u32[]{:S(2)}, u32[]{:S(2)}) collective-permute-start(bf16[4,128,128]{2,1,0:T(8,128)(2,1)S(1)} %get-tuple-element.10), channel_id=1, source_target_pairs={{0,8},{8,0},{16,24},{24,16},{1,9},{9,1},{17,25},{25,17},{2,10},{10... | collective-permute-start | bytes 393224 | tf_op jit(solution)/shard_map/ppermute | solution.py:183
  83.0 8.4 %collective-permute-start.9 = (bf16[4,128,128]{2,1,0:T(8,128)(2,1)S(1)}, bf16[4,128,128]{2,1,0:T(8,128)(2,1)S(1)}, u32[]{:S(2)}, u32[]{:S(2)}) collective-permute-start(bf16[4,128,128]{2,1,0:T(8,128)(2,1)S(1)} %get-tuple-element.11), channel_id=1, source_target_pairs={{0,16},{8,24},{16,0},{24,8},{1,17},{9,25},{17,1},{25,9},{2,18},{10... | collective-permute-start | bytes 393224 | tf_op jit(solution)/shard_map/ppermute | solution.py:183
  87.2 6.0 %collective-permute-start.10 = (bf16[4,128,128]{2,1,0:T(8,128)(2,1)S(1)}, bf16[4,128,128]{2,1,0:T(8,128)(2,1)S(1)}, u32[]{:S(2)}, u32[]{:S(2)}) collective-permute-start(bf16[4,128,128]{2,1,0:T(8,128)(2,1)S(1)} %get-tuple-element.12), channel_id=1, source_target_pairs={{0,24},{8,16},{16,8},{24,0},{1,25},{9,17},{17,9},{25,1},{2,26},{10... | collective-permute-start | bytes 393224 | tf_op jit(solution)/shard_map/ppermute | solution.py:183
  93.9 3.1 %collective-permute-start.13 = (f32[16,16]{1,0:T(8,128)S(1)}, f32[16,16]{1,0:T(8,128)S(1)}, u32[]{:S(2)}, u32[]{:S(2)}) collective-permute-start(f32[16,16]{1,0:T(8,128)S(1)} %gram.1), channel_id=1, source_target_pairs={{0,24},{8,16},{16,8},{24,0},{1,25},{9,17},{17,9},{25,1},{2,26},{10... | collective-permute-start | bytes 3080 | tf_op jit(solution)/shard_map/ppermute | solution.py:183
  95.6 3.7 %collective-permute-start.12 = (f32[16,16]{1,0:T(8,128)S(1)}, f32[16,16]{1,0:T(8,128)S(1)}, u32[]{:S(2)}, u32[]{:S(2)}) collective-permute-start(f32[16,16]{1,0:T(8,128)S(1)} %gram.1), channel_id=1, source_target_pairs={{0,16},{8,24},{16,0},{24,8},{1,17},{9,25},{17,1},{25,9},{2,18},{10... | collective-permute-start | bytes 3080 | tf_op jit(solution)/shard_map/ppermute | solution.py:183
  95.9 3.4 %collective-permute-start.11 = (f32[16,16]{1,0:T(8,128)S(1)}, f32[16,16]{1,0:T(8,128)S(1)}, u32[]{:S(2)}, u32[]{:S(2)}) collective-permute-start(f32[16,16]{1,0:T(8,128)S(1)} %gram.1), channel_id=1, source_target_pairs={{0,8},{8,0},{16,24},{24,16},{1,9},{9,1},{17,25},{25,17},{2,10},{10... | collective-permute-start | bytes 3080 | tf_op jit(solution)/shard_map/ppermute | solution.py:183
  99.3 5.4 %collective-permute-start.14 = (f32[16,16]{1,0:T(8,128)S(1)}, f32[16,16]{1,0:T(8,128)S(1)}, u32[]{:S(2)}, u32[]{:S(2)}) collective-permute-start(f32[16,16]{1,0:T(8,128)S(1)} %add_add_fusion), channel_id=1, source_target_pairs={{0,1},{1,0},{2,3},{3,2},{4,5},{5,4},{6,7},{7,6},{8,9},{9,8},{10,11... | collective-permute-start | bytes 3080 | tf_op jit(solution)/shard_map/ppermute | solution.py:183
  104.6 3.7 %collective-permute-start.15 = (f32[16,16]{1,0:T(8,128)S(1)}, f32[16,16]{1,0:T(8,128)S(1)}, u32[]{:S(2)}, u32[]{:S(2)}) collective-permute-start(f32[16,16]{1,0:T(8,128)S(1)} %add.21), channel_id=1, source_target_pairs={{0,2},{1,3},{2,0},{3,1},{4,6},{5,7},{6,4},{7,5},{8,10},{9,11},{10,... | collective-permute-start | bytes 3080 | tf_op jit(solution)/shard_map/ppermute | solution.py:183
  108.3 4.5 %collective-permute-start.16 = (f32[16,16]{1,0:T(8,128)S(1)}, f32[16,16]{1,0:T(8,128)S(1)}, u32[]{:S(2)}, u32[]{:S(2)}) collective-permute-start(f32[16,16]{1,0:T(8,128)S(1)} %add.22), channel_id=1, source_target_pairs={{0,4},{1,5},{2,6},{3,7},{4,0},{5,1},{6,2},{7,3},{8,12},{9,13},{10,... | collective-permute-start | bytes 3080 | tf_op jit(solution)/shard_map/ppermute | solution.py:183

commit v2 on v1

--- a/solution.py
+++ b/solution.py
@@ -67,13 +67,26 @@
     ref[:, :, PAD + columns : PAD + columns + 1, :] = ref[:, :, PAD : PAD + 1, :]
 
 
-def advance_kernel(me, own, up1, dn1, up2, dn2, bg0, bg2, bg13, adv, q0, q1, q2, q3, p0, p1, p2, bgs):
+def prep_kernel(own, narrow, last, lead):
+    vectors, _, rows = own.shape[:3]
+    for vector in range(vectors):
+        for f in range(2):
+            for row in range(rows):
+                value = own[vector, f, row].astype(jnp.bfloat16)
+                narrow[row, vector, f] = value
+                if row == rows - 1:
+                    last[vector, f] = value
+                if row == 0:
+                    lead[vector, f] = value
+
+
+def advance_kernel(me, own, up1, dn1, up2, dn2, bg0, bg1, bg2, bg3, adv, q0, q1, q2, q3, p0, p1, p2, bgs):
     vectors, _, rows, columns, _ = own.shape
     position = me[0]
     bgs[:, :, position] = bg0[...]
     bgs[:, :, position ^ 2] = bg2[...]
-    bgs[:, :, position ^ 1] = bg13[0]
-    bgs[:, :, position ^ 3] = bg13[1]
+    bgs[:, :, position ^ 1] = bg1[...]
+    bgs[:, :, position ^ 3] = bg3[...]
     for vector in range(vectors):
         for f in range(2):
             k = 2 * vector + f
@@ -81,9 +94,9 @@
             p0[0, k, cells, :] = up2[vector, f].astype(jnp.float32)
             p0[7, k, cells, :] = dn2[vector, f].astype(jnp.float32)
             for row in range(2):
-                p0[1 + row, k, cells, :] = up1[vector, f, row].astype(jnp.float32)
+                p0[1 + row, k, cells, :] = up1[row, vector, f].astype(jnp.float32)
                 p0[3 + row, k, cells, :] = own[vector, f, row]
-                p0[5 + row, k, cells, :] = dn1[vector, f, row].astype(jnp.float32)
+                p0[5 + row, k, cells, :] = dn1[row, vector, f].astype(jnp.float32)
     wrap(p0, columns)
 
     def to(ref):
@@ -198,24 +211,31 @@
     cells = fields * rows * columns * levels * lax.axis_size("space")
     me = lax.axis_index("vec").astype(jnp.int32).reshape(1)
 
-    narrow = tangents.astype(jnp.bfloat16)
+    row_shape = jax.ShapeDtypeStruct((vectors, fields, columns, levels), jnp.bfloat16)
+    narrow, last, lead = pl.pallas_call(
+        prep_kernel,
+        out_shape=[jax.ShapeDtypeStruct((rows,) + row_shape.shape, jnp.bfloat16), row_shape, row_shape],
+        in_specs=[VM],
+        out_specs=[VM] * 3,
+        compiler_params=PARAMS,
+        name="prep",
+    )(tangents)
     bg = jnp.swapaxes(background, 1, 2)
     bg_up = shift(jnp.concatenate([bg[0], bg[1, 1:]]), "space", 1)
     bg_dn = shift(jnp.concatenate([bg[0], bg[1, :1]]), "space", -1)
     up1 = shift(narrow, "space", 1)
     dn1 = shift(narrow, "space", -1)
-    up2 = shift(narrow[:, :, 1], "space", 2)
-    dn2 = shift(narrow[:, :, 0], "space", -2)
+    up2 = shift(last, "space", 2)
+    dn2 = shift(lead, "space", -2)
     bg0 = jnp.concatenate([bg_up[:2], bg[0], bg_dn[:2], bg_up[2:], bg[1], bg_dn[2:], bg[2]])
-    bg2 = swap(bg0, "vec", 2)
-    bg13 = swap(jnp.stack([bg0, bg2]), "vec", 1)
+    bg1, bg2, bg3 = (swap(bg0, "vec", mask) for mask in (1, 2, 3))
 
     quarter = jax.ShapeDtypeStruct((vectors, columns, levels), jnp.bfloat16)
     fields_all = 2 * vectors
     adv, q0, q1, q2, q3 = pl.pallas_call(
         advance_kernel,
         out_shape=[jax.ShapeDtypeStruct(tangents.shape, jnp.float32)] + [quarter] * 4,
-        in_specs=[SM] + [VM] * 8,
+        in_specs=[SM] + [VM] * 9,
         out_specs=[VM] * 5,
         scratch_shapes=[
             pltpu.VMEM((8, fields_all, columns + 2 * PAD, levels), jnp.float32),
@@ -225,13 +245,11 @@
         ],
         compiler_params=PARAMS,
         name="advance",
-    )(me, tangents, up1, dn1, up2, dn2, bg0, bg2, bg13)
+    )(me, tangents, up1, dn1, up2, dn2, bg0, bg1, bg2, bg3)
 
     q1, q2, q3 = swap(q1, "vec", 1), swap(q2, "vec", 2), swap(q3, "vec", 3)
     r2 = lax.ppermute(adv, "vec", [(0, 2), (1, 3)])
     r1 = lax.ppermute(adv, "vec", [(0, 1), (2, 3)])
-    r3 = lax.ppermute(r2, "vec", [(2, 3), (3, 2)])
-
     gram = pl.pallas_call(
         gram_kernel,
         out_shape=jax.ShapeDtypeStruct((count, count), jnp.float32),
@@ -242,6 +260,8 @@
         name="gram",
     )(me, q0, q1, q2, q3)
     gram = summed(gram)
+    gram, r2 = lax.optimization_barrier((gram, r2))
+    r3 = lax.ppermute(r2, "vec", [(2, 3), (3, 2)])
 
     basis, growth = pl.pallas_call(
         functools.partial(final_kernel, 1.0 / cells),

time: 118 us -> 118 us (level)
  starting transfers between devices: 31.3 us -> 26.4 us
  waiting for transfers between devices: 69.3 us -> 73.8 us
  Pallas kernels: 10.1 us -> 11.9 us
    ppermute x11 -> x12, waiting for transfers between devices: 25.8 us -> 57.1 us  [swap(): lax.ppermute(value, axis, [(i, i ^ mask) for i in range(lax.axis_size(axi...]
    ppermute x1, waiting for transfers between devices: 20.8 us -> 0.01 us  [on_device(): r2 = lax.ppermute(adv, 'vec', [(0, 2), (1, 3)])]
    ppermute x11 -> x12, starting transfers between devices: 12.9 us -> 6.28 us  [swap(): lax.ppermute(value, axis, [(i, i ^ mask) for i in range(lax.axis_size(axi...]
    ppermute x6, waiting for transfers between devices: 22.6 us -> 16.7 us  [shift(): lax.ppermute(value, axis, [(i, (i + step) % count) for i in range(count)])]
    ppermute x2 -> x0, local copies, waits for them, and re-layouts: 2.16 us -> none  [shift(): lax.ppermute(value, axis, [(i, (i + step) % count) for i in range(count)])]
    ppermute x6, starting transfers between devices: 12.6 us -> 14.6 us  [shift(): lax.ppermute(value, axis, [(i, (i + step) % count) for i in range(count)])]
    unnamed x10 -> x15, local copies, waits for them, and re-layouts: 1.91 us -> 3.88 us
  transfers between devices with their start and end apart: 20 -> 21, of which waited for: 13 -> 10; matrix products, arithmetic and copies ran while one was open for 3% -> 0% of each run, Pallas kernels for 1% -> 1%
where the time goes in v2:
time: 118 us; the launch traced here: 117 us
  waiting for transfers between devices  73.8 us (63%)
  starting transfers between devices  26.4 us (22%)
  Pallas kernels  11.9 us (10%)
  local copies, waits for them, and re-layouts  3.91 us (3%)
    ppermute x12, waiting for transfers between devices, swap(): lax.ppermute(value, axis, [(i, i ^ mask) for i in range(lax.axis_size(axi...  57.1 us
    ppermute x6, waiting for transfers between devices, shift(): lax.ppermute(value, axis, [(i, (i + step) % count) for i in range(count)])  16.7 us
    ppermute x6, starting transfers between devices, shift(): lax.ppermute(value, axis, [(i, (i + step) % count) for i in range(count)])  14.6 us
    ppermute x12, starting transfers between devices, swap(): lax.ppermute(value, axis, [(i, i ^ mask) for i in range(lax.axis_size(axi...  6.28 us
    pallas_call x1, Pallas kernels, on_device(): pl.pallas_call(advance_kernel, out_shape=[jax.ShapeDtypeStruct(tangents.s...  5.88 us
    pallas_call x1, Pallas kernels, on_device(): pl.pallas_call(functools.partial(final_kernel, 1.0 / cells), out_shape=[j...  4.45 us
    unnamed x15, local copies, waits for them, and re-layouts  3.88 us
    ppermute x1, starting transfers between devices, on_device(): r2 = lax.ppermute(adv, 'vec', [(0, 2), (1, 3)])  3.49 us
  transfers between devices with their start and end apart: 21, of which 10 were waited for; matrix products, arithmetic and copies ran while one was open for 0% of the time, Pallas kernels for 1%

profile of v2, /device:TPU:0, one launch (start us, length us, event | category | flops | bytes accessed | tf_op | source)
XLA Modules:
  0.0 116.9 jit_solution(9751802221078234975)
XLA Ops:
  0.6 0.9 copy.6
  1.6 3.0 %collective-permute-start.4 = (bf16[3,4,32,128]{3,2,1,0:T(8,128)(2,1)S(1)}, bf16[3,4,32,128]{3,2,1,0:T(8,128)(2,1)S(1)}, u32[]{:S(2)}, u32[]{:S(2)}) collective-permute-start(bf16[3,4,32,128]{3,2,1,0:T(8,128)(2,1)S(1)} %get-tuple-element.29), channel_id=1, source_target_pairs={{0,1},{1,2},{2,3},{3,4},{4,5},{5,6},{6,7},{7,0},{8,9},{9,10},{10,1... | collective-permute-start | bytes 294920 | tf_op jit(solution)/shard_map/ppermute | solution.py:192
  4.6 1.2 %copy-done = f32[4,2,2,128,128]{4,3,2,1,0:T(8,128)S(1)} copy-done((f32[4,2,2,128,128]{4,3,2,1,0:T(8,128)S(1)}, f32[4,2,2,128,128]{4,3,2,1,0:T(8,128)}, u32[]{:S(2)}) %copy-start) | copy-done | bytes 1048600
  5.8 0.9 prep.1
  6.7 3.1 %collective-permute-start.1 = (bf16[2,4,2,128,128]{4,3,2,1,0:T(8,128)(2,1)}, bf16[2,4,2,128,128]{4,3,2,1,0:T(8,128)(2,1)S(1)}, u32[]{:S(2)}, u32[]{:S(2)}) collective-permute-start(bf16[2,4,2,128,128]{4,3,2,1,0:T(8,128)(2,1)} %get-tuple-element.14), channel_id=1, source_target_pairs={{0,7},{1,0},{2,1},{3,2},{4,3},{5,4},{6,5},{7,6},{8,15},{9,8},{10,9... | collective-permute-start | bytes 1572872 | tf_op jit(solution)/shard_map/ppermute | solution.py:192
  9.8 4.7 %collective-permute-start.5 = (bf16[3,4,32,128]{3,2,1,0:T(8,128)(2,1)S(1)}, bf16[3,4,32,128]{3,2,1,0:T(8,128)(2,1)S(1)}, u32[]{:S(2)}, u32[]{:S(2)}) collective-permute-start(bf16[3,4,32,128]{3,2,1,0:T(8,128)(2,1)S(1)} %get-tuple-element.28), channel_id=1, source_target_pairs={{0,7},{1,0},{2,1},{3,2},{4,3},{5,4},{6,5},{7,6},{8,15},{9,8},{10,9... | collective-permute-start | bytes 294920 | tf_op jit(solution)/shard_map/ppermute | solution.py:192
  14.5 3.8 %collective-permute-start.3 = (bf16[4,2,128,128]{3,2,1,0:T(8,128)(2,1)S(1)}, bf16[4,2,128,128]{3,2,1,0:T(8,128)(2,1)S(1)}, u32[]{:S(2)}, u32[]{:S(2)}) collective-permute-start(bf16[4,2,128,128]{3,2,1,0:T(8,128)(2,1)S(1)} %get-tuple-element.16), channel_id=1, source_target_pairs={{0,6},{1,7},{2,0},{3,1},{4,2},{5,3},{6,4},{7,5},{8,14},{9,15},{10,... | collective-permute-start | bytes 786440 | tf_op jit(solution)/shard_map/ppermute | solution.py:192
  18.3 16.7 %collective-permute-done.5 = bf16[3,4,32,128]{3,2,1,0:T(8,128)(2,1)S(1)} collective-permute-done((bf16[3,4,32,128]{3,2,1,0:T(8,128)(2,1)S(1)}, bf16[3,4,32,128]{3,2,1,0:T(8,128)(2,1)S(1)}, u32[]{:S(2)}, u32[]{:S(2)}) %collective-permute-start.5) | collective-permute-done | bytes 98336 | tf_op jit(solution)/shard_map/ppermute | solution.py:192
  35.1 1.2 %collective-permute-start.8 = (bf16[12,4,32,128]{3,2,1,0:T(8,128)(2,1)S(1)}, bf16[12,4,32,128]{3,2,1,0:T(8,128)(2,1)S(1)}, u32[]{:S(2)}, u32[]{:S(2)}) collective-permute-start(bf16[12,4,32,128]{3,2,1,0:T(8,128)(2,1)S(1)} %fusion.bg0), channel_id=1, source_target_pairs={{0,24},{8,16},{16,8},{24,0},{1,25},{9,17},{17,9},{25,1},{2,26},{10... | collective-permute-start | bytes 1179656 | tf_op jit(solution)/shard_map/ppermute | solution.py:196
  36.3 0.5 collective-permute-start.7
  36.8 0.7 copy-done.2
  37.5 0.2 collective-permute-start.6
  37.8 8.6 %collective-permute-done.8.bg3 = bf16[12,4,32,128]{3,2,1,0:T(8,128)(2,1)S(1)} collective-permute-done((bf16[12,4,32,128]{3,2,1,0:T(8,128)(2,1)S(1)}, bf16[12,4,32,128]{3,2,1,0:T(8,128)(2,1)S(1)}, u32[]{:S(2)}, u32[]{:S(2)}) %collective-permute-start.8) | collective-permute-done | bytes 393248 | tf_op jit(solution)/shard_map/ppermute | solution.py:196
  46.4 8.6 %collective-permute-done.7.bg2 = bf16[12,4,32,128]{3,2,1,0:T(8,128)(2,1)S(1)} collective-permute-done((bf16[12,4,32,128]{3,2,1,0:T(8,128)(2,1)S(1)}, bf16[12,4,32,128]{3,2,1,0:T(8,128)(2,1)S(1)}, u32[]{:S(2)}, u32[]{:S(2)}) %collective-permute-start.7) | collective-permute-done | bytes 393248 | tf_op jit(solution)/shard_map/ppermute | solution.py:196
  55.1 0.9 copy-done.3
  56.0 5.9 %advance.1 = (f32[4,2,2,128,128]{4,3,2,1,0:T(8,128)S(1)}, bf16[4,128,128]{2,1,0:T(8,128)(2,1)S(1)}, bf16[4,128,128]{2,1,0:T(8,128)(2,1)S(1)}, bf16[4,128,128]{2,1,0:T(8,128)(2,1)S(1)}, bf16[4,128,128]{2,1,0:T(8,128)(2,1)S(1)}) custom-call(s32[1]{0:T(128)} %bitcast.me, f32[4,2,2,128,128]{4,3,2,1,0:T(8,128)S(1)} %copy-done.1, ...), custom_call_target="tpu_custom_call" | custom-call | tf_op jit(solution)/shard_map/advance/pallas_call | solution.py:235
  61.9 3.5 %collective-permute-start.18 = (f32[4,2,2,128,128]{4,3,2,1,0:T(8,128)S(1)}, f32[4,2,2,128,128]{4,3,2,1,0:T(8,128)S(1)}, u32[]{:S(2)}, u32[]{:S(2)}) collective-permute-start(f32[4,2,2,128,128]{4,3,2,1,0:T(8,128)S(1)} %get-tuple-element.21.own), channel_id=1, source_target_pairs={{0,16},{8,24},{1,17},{9,25},{2,18},{10,26},{3,19},{11,27},{4,20},{... | collective-permute-start | bytes 3145736 | tf_op jit(solution)/shard_map/ppermute | solution.py:251
  65.5 1.8 %collective-permute-start.11 = (bf16[4,128,128]{2,1,0:T(8,128)(2,1)S(1)}, bf16[4,128,128]{2,1,0:T(8,128)(2,1)S(1)}, u32[]{:S(2)}, u32[]{:S(2)}) collective-permute-start(bf16[4,128,128]{2,1,0:T(8,128)(2,1)S(1)} %get-tuple-element.20), channel_id=1, source_target_pairs={{0,24},{8,16},{16,8},{24,0},{1,25},{9,17},{17,9},{25,1},{2,26},{10... | collective-permute-start | bytes 393224 | tf_op jit(solution)/shard_map/ppermute | solution.py:196
  67.3 24.3 %collective-permute-done.10.q2 = bf16[4,128,128]{2,1,0:T(8,128)(2,1)S(1)} collective-permute-done((bf16[4,128,128]{2,1,0:T(8,128)(2,1)S(1)}, bf16[4,128,128]{2,1,0:T(8,128)(2,1)S(1)}, u32[]{:S(2)}, u32[]{:S(2)}) %collective-permute-start.10) | collective-permute-done | bytes 131104 | tf_op jit(solution)/shard_map/ppermute | solution.py:196
  91.7 1.8 %collective-permute-done.11.q3 = bf16[4,128,128]{2,1,0:T(8,128)(2,1)S(1)} collective-permute-done((bf16[4,128,128]{2,1,0:T(8,128)(2,1)S(1)}, bf16[4,128,128]{2,1,0:T(8,128)(2,1)S(1)}, u32[]{:S(2)}, u32[]{:S(2)}) %collective-permute-start.11) | collective-permute-done | bytes 131104 | tf_op jit(solution)/shard_map/ppermute | solution.py:196
  93.4 0.7 gram.1
  94.1 1.9 %collective-permute-start.14 = (f32[16,16]{1,0:T(8,128)S(1)}, f32[16,16]{1,0:T(8,128)S(1)}, u32[]{:S(2)}, u32[]{:S(2)}) collective-permute-start(f32[16,16]{1,0:T(8,128)S(1)} %gram.1), channel_id=1, source_target_pairs={{0,24},{8,16},{16,8},{24,0},{1,25},{9,17},{17,9},{25,1},{2,26},{10... | collective-permute-start | bytes 3080 | tf_op jit(solution)/shard_map/ppermute | solution.py:196
  96.1 0.2 collective-permute-start.12
  96.2 1.2 %collective-permute-done.14 = f32[16,16]{1,0:T(8,128)S(1)} collective-permute-done((f32[16,16]{1,0:T(8,128)S(1)}, f32[16,16]{1,0:T(8,128)S(1)}, u32[]{:S(2)}, u32[]{:S(2)}) %collective-permute-start.14) | collective-permute-done | bytes 1056 | tf_op jit(solution)/shard_map/ppermute | solution.py:196
  97.4 2.3 %collective-permute-done.13 = f32[16,16]{1,0:T(8,128)S(1)} collective-permute-done((f32[16,16]{1,0:T(8,128)S(1)}, f32[16,16]{1,0:T(8,128)S(1)}, u32[]{:S(2)}, u32[]{:S(2)}) %collective-permute-start.13) | collective-permute-done | bytes 1056 | tf_op jit(solution)/shard_map/ppermute | solution.py:196
  99.8 3.6 %collective-permute-done.15 = f32[16,16]{1,0:T(8,128)S(1)} collective-permute-done((f32[16,16]{1,0:T(8,128)S(1)}, f32[16,16]{1,0:T(8,128)S(1)}, u32[]{:S(2)}, u32[]{:S(2)}) %collective-permute-start.15) | collective-permute-done | bytes 1056 | tf_op jit(solution)/shard_map/ppermute | solution.py:196
  103.4 3.7 %collective-permute-done.16 = f32[16,16]{1,0:T(8,128)S(1)} collective-permute-done((f32[16,16]{1,0:T(8,128)S(1)}, f32[16,16]{1,0:T(8,128)S(1)}, u32[]{:S(2)}, u32[]{:S(2)}) %collective-permute-start.16) | collective-permute-done | bytes 1056 | tf_op jit(solution)/shard_map/ppermute | solution.py:196
  107.1 0.3 collective-permute-start.17
  107.4 1.3 %collective-permute-start.19 = (f32[4,2,2,128,128]{4,3,2,1,0:T(8,128)S(1)}, f32[4,2,2,128,128]{4,3,2,1,0:T(8,128)S(1)}, u32[]{:S(2)}, u32[]{:S(2)}) collective-permute-start(f32[4,2,2,128,128]{4,3,2,1,0:T(8,128)S(1)} %get-tuple-element.21.own), channel_id=1, source_target_pairs={{0,8},{16,24},{1,9},{17,25},{2,10},{18,26},{3,11},{19,27},{4,12},{... | collective-permute-start | bytes 3145736 | tf_op jit(solution)/shard_map/ppermute | solution.py:252
  108.7 2.9 %collective-permute-done.17 = f32[16,16]{1,0:T(8,128)S(1)} collective-permute-done((f32[16,16]{1,0:T(8,128)S(1)}, f32[16,16]{1,0:T(8,128)S(1)}, u32[]{:S(2)}, u32[]{:S(2)}) %collective-permute-start.17) | collective-permute-done | bytes 1056 | tf_op jit(solution)/shard_map/ppermute | solution.py:196
  111.7 0.7 collective-permute-start.20
  112.4 4.4 %final.1 = (f32[4,2,2,128,128]{4,3,2,1,0:T(8,128)}, f32[1,16]{1,0:T(1,128)}) custom-call(s32[1]{0:T(128)} %bitcast.me, f32[16,16]{1,0:T(8,128)S(1)} %add.23.gram, f32[4,2,2,128,128]{4,3,2,1,0:T(8,128)S(1)} %get-tuple-element.21.own, f32[4,2,2,128,128]{4,3,2,1,0:T(8,128)S(1)} %collective-permute-done.19.r1, ...), custom_call_target="tpu_custom_call" | custom-call | tf_op jit(solution)/shard_map/final/pallas_call | solution.py:266
  (37 shorter events, 0.4 us)
Async XLA Ops:
  1.6 12.9 %collective-permute-start.4 = (bf16[3,4,32,128]{3,2,1,0:T(8,128)(2,1)S(1)}, bf16[3,4,32,128]{3,2,1,0:T(8,128)(2,1)S(1)}, u32[]{:S(2)}, u32[]{:S(2)}) collective-permute-start(bf16[3,4,32,128]{3,2,1,0:T(8,128)(2,1)S(1)} %get-tuple-element.29), channel_id=1, source_target_pairs={{0,1},{1,2},{2,3},{3,4},{4,5},{5,6},{6,7},{7,0},{8,9},{9,10},{10,1... | collective-permute-start | bytes 294920 | tf_op jit(solution)/shard_map/ppermute | solution.py:192
  4.6 1.2 %copy-start = (f32[4,2,2,128,128]{4,3,2,1,0:T(8,128)S(1)}, f32[4,2,2,128,128]{4,3,2,1,0:T(8,128)}, u32[]{:S(2)}) copy-start(f32[4,2,2,128,128]{4,3,2,1,0:T(8,128)} %own.3) | copy-start | bytes 3145732
  5.8 49.2 %copy-start.1 = (f32[4,2,2,128,128]{4,3,2,1,0:T(8,128)S(1)}, f32[4,2,2,128,128]{4,3,2,1,0:T(8,128)}, u32[]{:S(2)}) copy-start(f32[4,2,2,128,128]{4,3,2,1,0:T(8,128)} %own.3) | copy-start | bytes 3145732
  6.7 48.3 %collective-permute-start.1 = (bf16[2,4,2,128,128]{4,3,2,1,0:T(8,128)(2,1)}, bf16[2,4,2,128,128]{4,3,2,1,0:T(8,128)(2,1)S(1)}, u32[]{:S(2)}, u32[]{:S(2)}) collective-permute-start(bf16[2,4,2,128,128]{4,3,2,1,0:T(8,128)(2,1)} %get-tuple-element.14), channel_id=1, source_target_pairs={{0,7},{1,0},{2,1},{3,2},{4,3},{5,4},{6,5},{7,6},{8,15},{9,8},{10,9... | collective-permute-start | bytes 1572872 | tf_op jit(solution)/shard_map/ppermute | solution.py:192
  9.8 45.3 %collective-permute-start = (bf16[2,4,2,128,128]{4,3,2,1,0:T(8,128)(2,1)}, bf16[2,4,2,128,128]{4,3,2,1,0:T(8,128)(2,1)S(1)}, u32[]{:S(2)}, u32[]{:S(2)}) collective-permute-start(bf16[2,4,2,128,128]{4,3,2,1,0:T(8,128)(2,1)} %get-tuple-element.14), channel_id=1, source_target_pairs={{0,1},{1,2},{2,3},{3,4},{4,5},{5,6},{6,7},{7,0},{8,9},{9,10},{10,1... | collective-permute-start | bytes 1572872 | tf_op jit(solution)/shard_map/ppermute | solution.py:192
  9.8 25.3 %collective-permute-start.5 = (bf16[3,4,32,128]{3,2,1,0:T(8,128)(2,1)S(1)}, bf16[3,4,32,128]{3,2,1,0:T(8,128)(2,1)S(1)}, u32[]{:S(2)}, u32[]{:S(2)}) collective-permute-start(bf16[3,4,32,128]{3,2,1,0:T(8,128)(2,1)S(1)} %get-tuple-element.28), channel_id=1, source_target_pairs={{0,7},{1,0},{2,1},{3,2},{4,3},{5,4},{6,5},{7,6},{8,15},{9,8},{10,9... | collective-permute-start | bytes 294920 | tf_op jit(solution)/shard_map/ppermute | solution.py:192
  14.5 21.8 %collective-permute-start.2 = (bf16[4,2,128,128]{3,2,1,0:T(8,128)(2,1)S(1)}, bf16[4,2,128,128]{3,2,1,0:T(8,128)(2,1)S(1)}, u32[]{:S(2)}, u32[]{:S(2)}) collective-permute-start(bf16[4,2,128,128]{3,2,1,0:T(8,128)(2,1)S(1)} %get-tuple-element.15), channel_id=1, source_target_pairs={{0,2},{1,3},{2,4},{3,5},{4,6},{5,7},{6,0},{7,1},{8,10},{9,11},{10,... | collective-permute-start | bytes 786440 | tf_op jit(solution)/shard_map/ppermute | solution.py:192
  14.5 22.3 %collective-permute-start.3 = (bf16[4,2,128,128]{3,2,1,0:T(8,128)(2,1)S(1)}, bf16[4,2,128,128]{3,2,1,0:T(8,128)(2,1)S(1)}, u32[]{:S(2)}, u32[]{:S(2)}) collective-permute-start(bf16[4,2,128,128]{3,2,1,0:T(8,128)(2,1)S(1)} %get-tuple-element.16), channel_id=1, source_target_pairs={{0,6},{1,7},{2,0},{3,1},{4,2},{5,3},{6,4},{7,5},{8,14},{9,15},{10,... | collective-permute-start | bytes 786440 | tf_op jit(solution)/shard_map/ppermute | solution.py:192
  35.1 11.3 %collective-permute-start.8 = (bf16[12,4,32,128]{3,2,1,0:T(8,128)(2,1)S(1)}, bf16[12,4,32,128]{3,2,1,0:T(8,128)(2,1)S(1)}, u32[]{:S(2)}, u32[]{:S(2)}) collective-permute-start(bf16[12,4,32,128]{3,2,1,0:T(8,128)(2,1)S(1)} %fusion.bg0), channel_id=1, source_target_pairs={{0,24},{8,16},{16,8},{24,0},{1,25},{9,17},{17,9},{25,1},{2,26},{10... | collective-permute-start | bytes 1179656 | tf_op jit(solution)/shard_map/ppermute | solution.py:196
  36.3 18.7 %collective-permute-start.7 = (bf16[12,4,32,128]{3,2,1,0:T(8,128)(2,1)S(1)}, bf16[12,4,32,128]{3,2,1,0:T(8,128)(2,1)S(1)}, u32[]{:S(2)}, u32[]{:S(2)}) collective-permute-start(bf16[12,4,32,128]{3,2,1,0:T(8,128)(2,1)S(1)} %fusion.bg0), channel_id=1, source_target_pairs={{0,16},{8,24},{16,0},{24,8},{1,17},{9,25},{17,1},{25,9},{2,18},{10... | collective-permute-start | bytes 1179656 | tf_op jit(solution)/shard_map/ppermute | solution.py:196
  36.8 0.7 copy-start.2
  37.5 17.5 %collective-permute-start.6 = (bf16[12,4,32,128]{3,2,1,0:T(8,128)(2,1)S(1)}, bf16[12,4,32,128]{3,2,1,0:T(8,128)(2,1)}, u32[]{:S(2)}, u32[]{:S(2)}) collective-permute-start(bf16[12,4,32,128]{3,2,1,0:T(8,128)(2,1)S(1)} %fusion.bg0), channel_id=1, source_target_pairs={{0,8},{8,0},{16,24},{24,16},{1,9},{9,1},{17,25},{25,17},{2,10},{10... | collective-permute-start | bytes 1179656 | tf_op jit(solution)/shard_map/ppermute | solution.py:196
  55.0 1.0 copy-start.3
  61.9 49.8 %collective-permute-start.18 = (f32[4,2,2,128,128]{4,3,2,1,0:T(8,128)S(1)}, f32[4,2,2,128,128]{4,3,2,1,0:T(8,128)S(1)}, u32[]{:S(2)}, u32[]{:S(2)}) collective-permute-start(f32[4,2,2,128,128]{4,3,2,1,0:T(8,128)S(1)} %get-tuple-element.21.own), channel_id=1, source_target_pairs={{0,16},{8,24},{1,17},{9,25},{2,18},{10,26},{3,19},{11,27},{4,20},{... | collective-permute-start | bytes 3145736 | tf_op jit(solution)/shard_map/ppermute | solution.py:251
  65.4 1.9 %collective-permute-start.9 = (bf16[4,128,128]{2,1,0:T(8,128)(2,1)S(1)}, bf16[4,128,128]{2,1,0:T(8,128)(2,1)S(1)}, u32[]{:S(2)}, u32[]{:S(2)}) collective-permute-start(bf16[4,128,128]{2,1,0:T(8,128)(2,1)S(1)} %get-tuple-element.18), channel_id=1, source_target_pairs={{0,8},{8,0},{16,24},{24,16},{1,9},{9,1},{17,25},{25,17},{2,10},{10... | collective-permute-start | bytes 393224 | tf_op jit(solution)/shard_map/ppermute | solution.py:196
  65.5 26.2 %collective-permute-start.10 = (bf16[4,128,128]{2,1,0:T(8,128)(2,1)S(1)}, bf16[4,128,128]{2,1,0:T(8,128)(2,1)S(1)}, u32[]{:S(2)}, u32[]{:S(2)}) collective-permute-start(bf16[4,128,128]{2,1,0:T(8,128)(2,1)S(1)} %get-tuple-element.19), channel_id=1, source_target_pairs={{0,16},{8,24},{16,0},{24,8},{1,17},{9,25},{17,1},{25,9},{2,18},{10... | collective-permute-start | bytes 393224 | tf_op jit(solution)/shard_map/ppermute | solution.py:196
  65.5 27.9 %collective-permute-start.11 = (bf16[4,128,128]{2,1,0:T(8,128)(2,1)S(1)}, bf16[4,128,128]{2,1,0:T(8,128)(2,1)S(1)}, u32[]{:S(2)}, u32[]{:S(2)}) collective-permute-start(bf16[4,128,128]{2,1,0:T(8,128)(2,1)S(1)} %get-tuple-element.20), channel_id=1, source_target_pairs={{0,24},{8,16},{16,8},{24,0},{1,25},{9,17},{17,9},{25,1},{2,26},{10... | collective-permute-start | bytes 393224 | tf_op jit(solution)/shard_map/ppermute | solution.py:196
  94.1 3.3 %collective-permute-start.14 = (f32[16,16]{1,0:T(8,128)S(1)}, f32[16,16]{1,0:T(8,128)S(1)}, u32[]{:S(2)}, u32[]{:S(2)}) collective-permute-start(f32[16,16]{1,0:T(8,128)S(1)} %gram.1), channel_id=1, source_target_pairs={{0,24},{8,16},{16,8},{24,0},{1,25},{9,17},{17,9},{25,1},{2,26},{10... | collective-permute-start | bytes 3080 | tf_op jit(solution)/shard_map/ppermute | solution.py:196
  96.1 3.7 %collective-permute-start.13 = (f32[16,16]{1,0:T(8,128)S(1)}, f32[16,16]{1,0:T(8,128)S(1)}, u32[]{:S(2)}, u32[]{:S(2)}) collective-permute-start(f32[16,16]{1,0:T(8,128)S(1)} %gram.1), channel_id=1, source_target_pairs={{0,16},{8,24},{16,0},{24,8},{1,17},{9,25},{17,1},{25,9},{2,18},{10... | collective-permute-start | bytes 3080 | tf_op jit(solution)/shard_map/ppermute | solution.py:196
  96.1 3.7 %collective-permute-start.12 = (f32[16,16]{1,0:T(8,128)S(1)}, f32[16,16]{1,0:T(8,128)S(1)}, u32[]{:S(2)}, u32[]{:S(2)}) collective-permute-start(f32[16,16]{1,0:T(8,128)S(1)} %gram.1), channel_id=1, source_target_pairs={{0,8},{8,0},{16,24},{24,16},{1,9},{9,1},{17,25},{25,17},{2,10},{10... | collective-permute-start | bytes 3080 | tf_op jit(solution)/shard_map/ppermute | solution.py:196
  99.7 3.7 %collective-permute-start.15 = (f32[16,16]{1,0:T(8,128)S(1)}, f32[16,16]{1,0:T(8,128)S(1)}, u32[]{:S(2)}, u32[]{:S(2)}) collective-permute-start(f32[16,16]{1,0:T(8,128)S(1)} %add_add_fusion), channel_id=1, source_target_pairs={{0,1},{1,0},{2,3},{3,2},{4,5},{5,4},{6,7},{7,6},{8,9},{9,8},{10,11... | collective-permute-start | bytes 3080 | tf_op jit(solution)/shard_map/ppermute | solution.py:196
  103.4 3.7 %collective-permute-start.16 = (f32[16,16]{1,0:T(8,128)S(1)}, f32[16,16]{1,0:T(8,128)S(1)}, u32[]{:S(2)}, u32[]{:S(2)}) collective-permute-start(f32[16,16]{1,0:T(8,128)S(1)} %add.21), channel_id=1, source_target_pairs={{0,2},{1,3},{2,0},{3,1},{4,6},{5,7},{6,4},{7,5},{8,10},{9,11},{10,... | collective-permute-start | bytes 3080 | tf_op jit(solution)/shard_map/ppermute | solution.py:196
  107.1 4.5 %collective-permute-start.17 = (f32[16,16]{1,0:T(8,128)S(1)}, f32[16,16]{1,0:T(8,128)S(1)}, u32[]{:S(2)}, u32[]{:S(2)}) collective-permute-start(f32[16,16]{1,0:T(8,128)S(1)} %add.22), channel_id=1, source_target_pairs={{0,4},{1,5},{2,6},{3,7},{4,0},{5,1},{6,2},{7,3},{8,12},{9,13},{10,... | collective-permute-start | bytes 3080 | tf_op jit(solution)/shard_map/ppermute | solution.py:196
  107.4 5.0 %collective-permute-start.19 = (f32[4,2,2,128,128]{4,3,2,1,0:T(8,128)S(1)}, f32[4,2,2,128,128]{4,3,2,1,0:T(8,128)S(1)}, u32[]{:S(2)}, u32[]{:S(2)}) collective-permute-start(f32[4,2,2,128,128]{4,3,2,1,0:T(8,128)S(1)} %get-tuple-element.21.own), channel_id=1, source_target_pairs={{0,8},{16,24},{1,9},{17,25},{2,10},{18,26},{3,11},{19,27},{4,12},{... | collective-permute-start | bytes 3145736 | tf_op jit(solution)/shard_map/ppermute | solution.py:252
  111.7 0.7 collective-permute-start.20

commit v3 on v2

--- a/solution.py
+++ b/solution.py
@@ -80,7 +80,28 @@
                     lead[vector, f] = value
 
 
-def advance_kernel(me, own, up1, dn1, up2, dn2, bg0, bg1, bg2, bg3, adv, q0, q1, q2, q3, p0, p1, p2, bgs):
+def edges_kernel(background, up, dn):
+    for f in range(4):
+        for row in range(2):
+            up[row, f] = background[0, f, row]
+            dn[row, f] = background[0, f, row]
+        up[2, f] = background[1, f, 1]
+        dn[2, f] = background[1, f, 0]
+
+
+def pack_kernel(background, up, dn, packed):
+    for f in range(4):
+        for row in range(2):
+            packed[row, f] = up[row, f]
+            packed[2 + row, f] = background[0, f, row]
+            packed[4 + row, f] = dn[row, f]
+            packed[7 + row, f] = background[1, f, row]
+            packed[10 + row, f] = background[2, f, row]
+        packed[6, f] = up[2, f]
+        packed[9, f] = dn[2, f]
+
+
+def advance_kernel(me, own, up1, dn1, up2, dn2, bg0, bg1, bg2, bg3, adv, hi, lo, p0, p1, p2, bgs):
     vectors, _, rows, columns, _ = own.shape
     position = me[0]
     bgs[:, :, position] = bg0[...]
@@ -107,39 +128,50 @@
 
     def to_out(row, vector, f, x, value):
         adv[vector, f, row, x : x + CHUNK, :] = value
+        top = value.astype(jnp.bfloat16)
+        hi[vector, f, row, x : x + CHUNK, :] = top
+        lo[vector, f, row, x : x + CHUNK, :] = (value - top.astype(jnp.float32)).astype(jnp.bfloat16)
 
     stage_rows(p0, 1, bgs, 0, 0.0, 1.0, None, 0, 6, vectors, to(p1))
     wrap(p1, columns)
     stage_rows(p1, 1, bgs, 6, 0.75, 0.25, p0, 2, 4, vectors, to(p2))
     wrap(p2, columns)
     stage_rows(p2, 1, bgs, 10, 1.0 / 3.0, 2.0 / 3.0, p0, 3, 2, vectors, to_out)
-    for b, q in enumerate((q0, q1, q2, q3)):
-        part = position ^ b
-        for vector in range(vectors):
-            q[vector] = adv[vector, part // 2, part % 2].astype(jnp.bfloat16)
-
-
-def gram_kernel(me, q0, q1, q2, q3, out, flat):
-    vectors, columns, levels = q0.shape
+
+
+def gram_kernel(me, h0, h1, h2, h3, out, lines):
+    vectors, fields, rows, columns, levels = h0.shape
+    count = 4 * vectors
+    size = count * CHUNK
     position = me[0]
-    for b, q in enumerate((q0, q1, q2, q3)):
-        block = position ^ b
-        for vector in range(vectors):
-            flat[block * vectors + vector] = q[vector].astype(jnp.float32)
-    count = vectors * 4
-    rows = flat.reshape(count * columns, levels)
-    total = jnp.zeros((count, count), jnp.float32)
-    for x in range(0, columns, 2):
-        part = jnp.concatenate(
-            [rows[pl.ds(x + i, count, stride=columns), :].astype(jnp.bfloat16) for i in range(2)], 1
-        )
-        total += lax.dot_general(
-            part, part, (((1,), (1,)), ((), ())), preferred_element_type=jnp.float32
-        )
-    out[...] = total
-
-
-def final_kernel(scale, me, gram, own, r1, r2, r3, basis, growth, inv):
+    parts = []
+    for f in range(fields):
+        for y in range(rows):
+            for x in range(0, columns, CHUNK):
+                parts.append(
+                    jnp.concatenate(
+                        [h[j, f, y, x : x + CHUNK, :] for h in (h0, h1, h2, h3) for j in range(vectors)]
+                    )
+                )
+    flat = jnp.concatenate(parts, 1)
+    full = lax.dot_general(flat, flat, (((1,), (1,)), ((), ())), preferred_element_type=jnp.float32)
+    row = lax.broadcasted_iota(jnp.int32, (size, size), 0)
+    lane = lax.broadcasted_iota(jnp.int32, (size, size), 1)
+    full = jnp.where(row % CHUNK == lane % CHUNK, full, 0.0)
+    full = jnp.sum(full.reshape(count, CHUNK, size), axis=1)
+    for b in range(4):
+        for j in range(vectors):
+            k = b * vectors + j
+            lines[pl.ds((position ^ b) * vectors + j, 1), :] = full[k : k + 1, :]
+    group = lax.broadcasted_iota(jnp.int32, (size, count), 0) // CHUNK
+    target = ((group // vectors) ^ position) * vectors + group % vectors
+    pick = jnp.where(target == lax.broadcasted_iota(jnp.int32, (size, count), 1), 1.0, 0.0)
+    out[...] = jnp.dot(
+        lines[...], pick, precision=lax.Precision.HIGHEST, preferred_element_type=jnp.float32
+    )
+
+
+def final_kernel(scale, me, gram, own, h1, h2, h3, l1, l2, l3, basis, growth, inv):
     vectors = own.shape[0]
     count = gram.shape[0]
     position = me[0]
@@ -165,7 +197,7 @@
             line = inv[pl.ds(position * vectors + i, 1), :]
             weights.append(
                 [
-                    jnp.broadcast_to(line[:, count + j : count + j + 1], (8, own.shape[4]))
+                    jnp.broadcast_to(line[:, count + j : count + j + 1], (CHUNK, own.shape[4]))
                     for j in range(count)
                 ]
             )
@@ -173,10 +205,14 @@
             for y in range(own.shape[2]):
 
                 def tile(t, carry, f=f, y=y, first=first, weights=weights):
-                    at = pl.ds(pl.multiple_of(t * 8, 8), 8)
-                    values = [
-                        ref[j, f, y, at, :] for ref in (own, r1, r2, r3) for j in range(vectors)
-                    ]
+                    at = pl.ds(pl.multiple_of(t * CHUNK, CHUNK), CHUNK)
+                    values = [own[j, f, y, at, :] for j in range(vectors)]
+                    for h, l in ((h1, l1), (h2, l2), (h3, l3)):
+                        for j in range(vectors):
+                            values.append(
+                                h[j, f, y, at, :].astype(jnp.float32)
+                                + l[j, f, y, at, :].astype(jnp.float32)
+                            )
                     for i in range(2):
                         parts = [w * value for w, value in zip(weights[i], values)]
                         while len(parts) > 1:
@@ -184,7 +220,7 @@
                         basis[first + i, f, y, at, :] = parts[0]
                     return carry
 
-                lax.fori_loop(0, own.shape[3] // 8, tile, 0, unroll=4)
+                lax.fori_loop(0, own.shape[3] // CHUNK, tile, 0, unroll=2)
 
 
 def shift(value, axis, step):
@@ -197,11 +233,14 @@
 
 
 def summed(value):
-    value = (value + swap(value, "vec", 1)) + (swap(value, "vec", 2) + swap(value, "vec", 3))
-    mask = 1
-    while mask < lax.axis_size("space"):
-        value = value + swap(value, "space", mask)
-        mask *= 2
+    mask, size = 2, lax.axis_size("space")
+    while mask < size:
+        if 2 * mask < size:
+            one, two, three = (swap(value, "space", k) for k in (mask, 2 * mask, 3 * mask))
+            value = (value + one) + (two + three)
+        else:
+            value = value + swap(value, "space", mask)
+        mask *= 4
     return value
 
 
@@ -220,23 +259,39 @@
         compiler_params=PARAMS,
         name="prep",
     )(tangents)
-    bg = jnp.swapaxes(background, 1, 2)
-    bg_up = shift(jnp.concatenate([bg[0], bg[1, 1:]]), "space", 1)
-    bg_dn = shift(jnp.concatenate([bg[0], bg[1, :1]]), "space", -1)
+    edge = jax.ShapeDtypeStruct((3, 4) + background.shape[3:], jnp.bfloat16)
+    bg_up, bg_dn = pl.pallas_call(
+        edges_kernel,
+        out_shape=[edge, edge],
+        in_specs=[VM],
+        out_specs=[VM] * 2,
+        compiler_params=PARAMS,
+        name="edges",
+    )(background)
+    bg_up = shift(bg_up, "space", 1)
+    bg_dn = shift(bg_dn, "space", -1)
+    narrow, last, lead, bg_up, bg_dn = lax.optimization_barrier((narrow, last, lead, bg_up, bg_dn))
     up1 = shift(narrow, "space", 1)
     dn1 = shift(narrow, "space", -1)
     up2 = shift(last, "space", 2)
     dn2 = shift(lead, "space", -2)
-    bg0 = jnp.concatenate([bg_up[:2], bg[0], bg_dn[:2], bg_up[2:], bg[1], bg_dn[2:], bg[2]])
+    bg0 = pl.pallas_call(
+        pack_kernel,
+        out_shape=jax.ShapeDtypeStruct((12, 4) + background.shape[3:], jnp.bfloat16),
+        in_specs=[VM] * 3,
+        out_specs=VM,
+        compiler_params=PARAMS,
+        name="pack",
+    )(background, bg_up, bg_dn)
     bg1, bg2, bg3 = (swap(bg0, "vec", mask) for mask in (1, 2, 3))
 
-    quarter = jax.ShapeDtypeStruct((vectors, columns, levels), jnp.bfloat16)
+    half = jax.ShapeDtypeStruct(tangents.shape, jnp.bfloat16)
     fields_all = 2 * vectors
-    adv, q0, q1, q2, q3 = pl.pallas_call(
+    adv, hi, lo = pl.pallas_call(
         advance_kernel,
-        out_shape=[jax.ShapeDtypeStruct(tangents.shape, jnp.float32)] + [quarter] * 4,
+        out_shape=[jax.ShapeDtypeStruct(tangents.shape, jnp.float32), half, half],
         in_specs=[SM] + [VM] * 9,
-        out_specs=[VM] * 5,
+        out_specs=[VM] * 3,
         scratch_shapes=[
             pltpu.VMEM((8, fields_all, columns + 2 * PAD, levels), jnp.float32),
             pltpu.VMEM((6, fields_all, columns + 2 * PAD, levels), jnp.float32),
@@ -247,21 +302,23 @@
         name="advance",
     )(me, tangents, up1, dn1, up2, dn2, bg0, bg1, bg2, bg3)
 
-    q1, q2, q3 = swap(q1, "vec", 1), swap(q2, "vec", 2), swap(q3, "vec", 3)
-    r2 = lax.ppermute(adv, "vec", [(0, 2), (1, 3)])
-    r1 = lax.ppermute(adv, "vec", [(0, 1), (2, 3)])
+    h2, h1 = swap(hi, "vec", 2), swap(hi, "vec", 1)
+    l2, l1 = swap(lo, "vec", 2), swap(lo, "vec", 1)
+    h3 = swap(h2, "vec", 1)
+
     gram = pl.pallas_call(
         gram_kernel,
         out_shape=jax.ShapeDtypeStruct((count, count), jnp.float32),
         in_specs=[SM] + [VM] * 4,
         out_specs=VM,
-        scratch_shapes=[pltpu.VMEM((count, columns, levels), jnp.float32)],
+        scratch_shapes=[pltpu.VMEM((count, count * CHUNK), jnp.float32)],
         compiler_params=PARAMS,
         name="gram",
-    )(me, q0, q1, q2, q3)
+    )(me, hi, h1, h2, h3)
+    gram = gram + swap(gram, "space", 1)
+    gram, l2 = lax.optimization_barrier((gram, l2))
+    l3 = swap(l2, "vec", 1)
     gram = summed(gram)
-    gram, r2 = lax.optimization_barrier((gram, r2))
-    r3 = lax.ppermute(r2, "vec", [(2, 3), (3, 2)])
 
     basis, growth = pl.pallas_call(
         functools.partial(final_kernel, 1.0 / cells),
@@ -269,12 +326,12 @@
             jax.ShapeDtypeStruct(tangents.shape, jnp.float32),
             jax.ShapeDtypeStruct((1, count), jnp.float32),
         ],
-        in_specs=[SM] + [VM] * 5,
+        in_specs=[SM] + [VM] * 8,
         out_specs=[VM, VM],
         scratch_shapes=[pltpu.VMEM((count, 2 * count), jnp.float32)],
         compiler_params=PARAMS,
         name="final",
-    )(me, gram, adv, r1, r2, r3)
+    )(me, gram, adv, h1, h2, h3, l1, l2, l3)
     return basis, growth.reshape(count)
 
 

time: 118 us -> 88.4 us (0.75)
  waiting for transfers between devices: 73.8 us -> 46.9 us
  starting transfers between devices: 26.4 us -> 24 us
    ppermute x12 -> x13, waiting for transfers between devices: 57.1 us -> 35.6 us  [swap(): lax.ppermute(value, axis, [(i, i ^ mask) for i in range(lax.axis_size(axi...]
    ppermute x12 -> x13, starting transfers between devices: 6.28 us -> 12 us  [swap(): lax.ppermute(value, axis, [(i, i ^ mask) for i in range(lax.axis_size(axi...]
    ppermute x3 -> x0, starting transfers between devices: 5.55 us -> none  [the longest x1 3.49 us: on_device(): r2 = lax.ppermute(adv, 'vec', [(0, 2), (1, 3)])]
    ppermute x6, waiting for transfers between devices: 16.7 us -> 11.3 us  [shift(): lax.ppermute(value, axis, [(i, (i + step) % count) for i in range(count)])]
    ppermute x6, starting transfers between devices: 14.6 us -> 11.9 us  [shift(): lax.ppermute(value, axis, [(i, (i + step) % count) for i in range(count)])]
    unnamed x15 -> x12, local copies, waits for them, and re-layouts: 3.88 us -> 3.8 us
  transfers between devices with their start and end apart: 21 -> 19, of which waited for: 10 -> 13; matrix products, arithmetic and copies ran while one was open for 0% -> 0% of each run, Pallas kernels for 1% -> 2%
where the time goes in v3:
time: 88.4 us; the launch traced here: 88.1 us
  waiting for transfers between devices  46.9 us (53%)
  starting transfers between devices  24 us (27%)
  Pallas kernels  12.8 us (14%)
  local copies, waits for them, and re-layouts  3.8 us (4%)
    ppermute x13, waiting for transfers between devices, swap(): lax.ppermute(value, axis, [(i, i ^ mask) for i in range(lax.axis_size(axi...  35.6 us
    ppermute x13, starting transfers between devices, swap(): lax.ppermute(value, axis, [(i, i ^ mask) for i in range(lax.axis_size(axi...  12 us
    ppermute x6, starting transfers between devices, shift(): lax.ppermute(value, axis, [(i, (i + step) % count) for i in range(count)])  11.9 us
    ppermute x6, waiting for transfers between devices, shift(): lax.ppermute(value, axis, [(i, (i + step) % count) for i in range(count)])  11.3 us
    pallas_call x1, Pallas kernels, on_device(): pl.pallas_call(advance_kernel, out_shape=[jax.ShapeDtypeStruct(tangents.s...  5.9 us
    pallas_call x1, Pallas kernels, on_device(): pl.pallas_call(functools.partial(final_kernel, 1.0 / cells), out_shape=[j...  4.95 us
    unnamed x12, local copies, waits for them, and re-layouts  3.8 us
  transfers between devices with their start and end apart: 19, of which 13 were waited for; matrix products, arithmetic and copies ran while one was open for 0% of the time, Pallas kernels for 2%

profile of v3, /device:TPU:0, one launch (start us, length us, event | category | flops | bytes accessed | tf_op | source)
XLA Modules:
  0.0 88.1 jit_solution(16066347745823720887)
XLA Ops:
  0.6 0.9 %copy-done.2 = bf16[3,4,2,32,128]{4,3,2,1,0:T(8,128)(2,1)S(1)} copy-done((bf16[3,4,2,32,128]{4,3,2,1,0:T(8,128)(2,1)S(1)}, bf16[3,4,2,32,128]{4,3,2,1,0:T(8,128)(2,1)}, u32[]{:S(2)}) %copy-start.2) | copy-done | bytes 196632
  1.6 3.0 %collective-permute-start = (bf16[3,4,32,128]{3,2,1,0:T(8,128)(2,1)S(1)}, bf16[3,4,32,128]{3,2,1,0:T(8,128)(2,1)S(1)}, u32[]{:S(2)}, u32[]{:S(2)}) collective-permute-start(bf16[3,4,32,128]{3,2,1,0:T(8,128)(2,1)S(1)} %get-tuple-element.22), channel_id=1, source_target_pairs={{0,1},{1,2},{2,3},{3,4},{4,5},{5,6},{6,7},{7,0},{8,9},{9,10},{10,1... | collective-permute-start | bytes 294920 | tf_op jit(solution)/shard_map/ppermute | solution.py:228
  4.6 3.1 %collective-permute-start.1 = (bf16[3,4,32,128]{3,2,1,0:T(8,128)(2,1)S(1)}, bf16[3,4,32,128]{3,2,1,0:T(8,128)(2,1)S(1)}, u32[]{:S(2)}, u32[]{:S(2)}) collective-permute-start(bf16[3,4,32,128]{3,2,1,0:T(8,128)(2,1)S(1)} %get-tuple-element.23), channel_id=1, source_target_pairs={{0,7},{1,0},{2,1},{3,2},{4,3},{5,4},{6,5},{7,6},{8,15},{9,8},{10,9... | collective-permute-start | bytes 294920 | tf_op jit(solution)/shard_map/ppermute | solution.py:228
  7.7 1.2 %copy-done = f32[4,2,2,128,128]{4,3,2,1,0:T(8,128)S(1)} copy-done((f32[4,2,2,128,128]{4,3,2,1,0:T(8,128)S(1)}, f32[4,2,2,128,128]{4,3,2,1,0:T(8,128)}, u32[]{:S(2)}) %copy-start) | copy-done | bytes 1048600
  8.9 0.9 prep.1
  9.8 0.7 collective-permute-done.up
  10.5 0.8 collective-permute-done.1.dn
  11.3 0.9 %collective-permute-start.4 = (bf16[4,2,128,128]{3,2,1,0:T(8,128)(2,1)S(1)}, bf16[4,2,128,128]{3,2,1,0:T(8,128)(2,1)S(1)}, u32[]{:S(2)}, u32[]{:S(2)}) collective-permute-start(bf16[4,2,128,128]{3,2,1,0:T(8,128)(2,1)S(1)} %get-tuple-element.25), channel_id=1, source_target_pairs={{0,2},{1,3},{2,4},{3,5},{4,6},{5,7},{6,0},{7,1},{8,10},{9,11},{10,... | collective-permute-start | bytes 786440 | tf_op jit(solution)/shard_map/ppermute | solution.py:228
  12.2 2.9 %collective-permute-start.5 = (bf16[4,2,128,128]{3,2,1,0:T(8,128)(2,1)S(1)}, bf16[4,2,128,128]{3,2,1,0:T(8,128)(2,1)S(1)}, u32[]{:S(2)}, u32[]{:S(2)}) collective-permute-start(bf16[4,2,128,128]{3,2,1,0:T(8,128)(2,1)S(1)} %get-tuple-element.26), channel_id=1, source_target_pairs={{0,6},{1,7},{2,0},{3,1},{4,2},{5,3},{6,4},{7,5},{8,14},{9,15},{10,... | collective-permute-start | bytes 786440 | tf_op jit(solution)/shard_map/ppermute | solution.py:228
  15.1 1.9 %collective-permute-start.3 = (bf16[2,4,2,128,128]{4,3,2,1,0:T(8,128)(2,1)}, bf16[2,4,2,128,128]{4,3,2,1,0:T(8,128)(2,1)S(1)}, u32[]{:S(2)}, u32[]{:S(2)}) collective-permute-start(bf16[2,4,2,128,128]{4,3,2,1,0:T(8,128)(2,1)} %get-tuple-element.24), channel_id=1, source_target_pairs={{0,7},{1,0},{2,1},{3,2},{4,3},{5,4},{6,5},{7,6},{8,15},{9,8},{10,9... | collective-permute-start | bytes 1572872 | tf_op jit(solution)/shard_map/ppermute | solution.py:228
  17.3 5.1 %collective-permute-done.4.up2 = bf16[4,2,128,128]{3,2,1,0:T(8,128)(2,1)S(1)} collective-permute-done((bf16[4,2,128,128]{3,2,1,0:T(8,128)(2,1)S(1)}, bf16[4,2,128,128]{3,2,1,0:T(8,128)(2,1)S(1)}, u32[]{:S(2)}, u32[]{:S(2)}) %collective-permute-start.4) | collective-permute-done | bytes 262176 | tf_op jit(solution)/shard_map/ppermute | solution.py:228
  22.4 1.5 %collective-permute-start.7 = (bf16[12,4,32,128]{3,2,1,0:T(8,128)(2,1)S(1)}, bf16[12,4,32,128]{3,2,1,0:T(8,128)(2,1)S(1)}, u32[]{:S(2)}, u32[]{:S(2)}) collective-permute-start(bf16[12,4,32,128]{3,2,1,0:T(8,128)(2,1)S(1)} %pack.1.bg0), channel_id=1, source_target_pairs={{0,16},{8,24},{16,0},{24,8},{1,17},{9,25},{17,1},{25,9},{2,18},{10... | collective-permute-start | bytes 1179656 | tf_op jit(solution)/shard_map/ppermute | solution.py:232
  23.9 2.5 %collective-permute-done.5.dn2 = bf16[4,2,128,128]{3,2,1,0:T(8,128)(2,1)S(1)} collective-permute-done((bf16[4,2,128,128]{3,2,1,0:T(8,128)(2,1)S(1)}, bf16[4,2,128,128]{3,2,1,0:T(8,128)(2,1)S(1)}, u32[]{:S(2)}, u32[]{:S(2)}) %collective-permute-start.5) | collective-permute-done | bytes 262176 | tf_op jit(solution)/shard_map/ppermute | solution.py:228
  26.4 0.7 copy-done.4
  27.1 1.5 %collective-permute-done.8.bg3 = bf16[12,4,32,128]{3,2,1,0:T(8,128)(2,1)S(1)} collective-permute-done((bf16[12,4,32,128]{3,2,1,0:T(8,128)(2,1)S(1)}, bf16[12,4,32,128]{3,2,1,0:T(8,128)(2,1)S(1)}, u32[]{:S(2)}, u32[]{:S(2)}) %collective-permute-start.8) | collective-permute-done | bytes 393248 | tf_op jit(solution)/shard_map/ppermute | solution.py:232
  28.6 8.5 %collective-permute-done.7.bg2 = bf16[12,4,32,128]{3,2,1,0:T(8,128)(2,1)S(1)} collective-permute-done((bf16[12,4,32,128]{3,2,1,0:T(8,128)(2,1)S(1)}, bf16[12,4,32,128]{3,2,1,0:T(8,128)(2,1)S(1)}, u32[]{:S(2)}, u32[]{:S(2)}) %collective-permute-start.7) | collective-permute-done | bytes 393248 | tf_op jit(solution)/shard_map/ppermute | solution.py:232
  37.1 2.1 %collective-permute-done.3.dn1 = bf16[2,4,2,128,128]{4,3,2,1,0:T(8,128)(2,1)S(1)} collective-permute-done((bf16[2,4,2,128,128]{4,3,2,1,0:T(8,128)(2,1)}, bf16[2,4,2,128,128]{4,3,2,1,0:T(8,128)(2,1)S(1)}, u32[]{:S(2)}, u32[]{:S(2)}) %collective-permute-start.3) | collective-permute-done | bytes 524320 | tf_op jit(solution)/shard_map/ppermute | solution.py:228
  39.2 0.9 %copy-done.5 = bf16[4,2,128,128]{3,2,1,0:T(8,128)(2,1)S(1)} copy-done((bf16[4,2,128,128]{3,2,1,0:T(8,128)(2,1)S(1)}, bf16[4,2,128,128]{3,2,1,0:T(8,128)(2,1)}, u32[]{:S(2)}) %copy-start.5) | copy-done | bytes 262168
  40.2 5.9 %advance.1 = (f32[4,2,2,128,128]{4,3,2,1,0:T(8,128)S(1)}, bf16[4,2,2,128,128]{4,3,2,1,0:T(8,128)(2,1)S(1)}, bf16[4,2,2,128,128]{4,3,2,1,0:T(8,128)(2,1)S(1)}) custom-call(s32[1]{0:T(128)} %bitcast.me, f32[4,2,2,128,128]{4,3,2,1,0:T(8,128)S(1)} %copy-done.1, bf16[2,4,2,128,128]{4,3,2,1,0:T(8,128)(2,1)S(1)} %collective-permute-done.2.up1, ...), custom_call_target="tpu_custom_call" | custom-call | tf_op jit(solution)/shard_map/advance/pallas_call | solution.py:290
  46.1 1.6 %collective-permute-start.10 = (bf16[4,2,2,128,128]{4,3,2,1,0:T(8,128)(2,1)S(1)}, bf16[4,2,2,128,128]{4,3,2,1,0:T(8,128)(2,1)S(1)}, u32[]{:S(2)}, u32[]{:S(2)}) collective-permute-start(bf16[4,2,2,128,128]{4,3,2,1,0:T(8,128)(2,1)S(1)} %get-tuple-element.29.h0), channel_id=1, source_target_pairs={{0,16},{8,24},{16,0},{24,8},{1,17},{9,25},{17,1},{25,9},{2,18},{10... | collective-permute-start | bytes 1572872 | tf_op jit(solution)/shard_map/ppermute | solution.py:232
  47.7 10.2 %collective-permute-done.10.h2 = bf16[4,2,2,128,128]{4,3,2,1,0:T(8,128)(2,1)S(1)} collective-permute-done((bf16[4,2,2,128,128]{4,3,2,1,0:T(8,128)(2,1)S(1)}, bf16[4,2,2,128,128]{4,3,2,1,0:T(8,128)(2,1)S(1)}, u32[]{:S(2)}, u32[]{:S(2)}) %collective-permute-start.10) | collective-permute-done | bytes 524320 | tf_op jit(solution)/shard_map/ppermute | solution.py:232
  57.9 0.7 collective-permute-start.13
  58.6 1.2 %collective-permute-done.11.h3 = bf16[4,2,2,128,128]{4,3,2,1,0:T(8,128)(2,1)S(1)} collective-permute-done((bf16[4,2,2,128,128]{4,3,2,1,0:T(8,128)(2,1)S(1)}, bf16[4,2,2,128,128]{4,3,2,1,0:T(8,128)(2,1)S(1)}, u32[]{:S(2)}, u32[]{:S(2)}) %collective-permute-start.11) | collective-permute-done | bytes 524320 | tf_op jit(solution)/shard_map/ppermute | solution.py:232
  59.8 1.0 %gram.1 = f32[16,16]{1,0:T(8,128)S(1)} custom-call(s32[1]{0:T(128)} %bitcast.me, bf16[4,2,2,128,128]{4,3,2,1,0:T(8,128)(2,1)S(1)} %get-tuple-element.29.h0, bf16[4,2,2,128,128]{4,3,2,1,0:T(8,128)(2,1)S(1)} %collective-permute-done.9.h1, bf16[4,2,2,128,128]{4,3,2,1,0:T(8,128)(2,1)S(1)} %collective-permute-done.10.h2, ...), custom_call_target="tpu_custom_call" | custom-call | tf_op jit(solution)/shard_map/gram/pallas_call | solution.py:309
  60.8 1.3 %collective-permute-start.12 = (f32[16,16]{1,0:T(8,128)S(1)}, f32[16,16]{1,0:T(8,128)S(1)}, u32[]{:S(2)}, u32[]{:S(2)}) collective-permute-start(f32[16,16]{1,0:T(8,128)S(1)} %gram.1), channel_id=1, source_target_pairs={{0,1},{1,0},{2,3},{3,2},{4,5},{5,4},{6,7},{7,6},{8,9},{9,8},{10,11... | collective-permute-start | bytes 3080 | tf_op jit(solution)/shard_map/ppermute | solution.py:232
  62.1 2.4 %collective-permute-done.12 = f32[16,16]{1,0:T(8,128)S(1)} collective-permute-done((f32[16,16]{1,0:T(8,128)S(1)}, f32[16,16]{1,0:T(8,128)S(1)}, u32[]{:S(2)}, u32[]{:S(2)}) %collective-permute-start.12) | collective-permute-done | bytes 1056 | tf_op jit(solution)/shard_map/ppermute | solution.py:232
  64.5 7.7 %collective-permute-done.13.l2 = bf16[4,2,2,128,128]{4,3,2,1,0:T(8,128)(2,1)S(1)} collective-permute-done((bf16[4,2,2,128,128]{4,3,2,1,0:T(8,128)(2,1)S(1)}, bf16[4,2,2,128,128]{4,3,2,1,0:T(8,128)(2,1)S(1)}, u32[]{:S(2)}, u32[]{:S(2)}) %collective-permute-start.13) | collective-permute-done | bytes 524320 | tf_op jit(solution)/shard_map/ppermute | solution.py:232
  72.2 6.4 %collective-permute-start.16 = (f32[16,16]{1,0:T(8,128)S(1)}, f32[16,16]{1,0:T(8,128)S(1)}, u32[]{:S(2)}, u32[]{:S(2)}) collective-permute-start(f32[16,16]{1,0:T(8,128)S(1)} %add.12), channel_id=1, source_target_pairs={{0,6},{1,7},{2,4},{3,5},{4,2},{5,3},{6,0},{7,1},{8,14},{9,15},{10,... | collective-permute-start | bytes 3080 | tf_op jit(solution)/shard_map/ppermute | solution.py:232
  78.6 0.6 collective-permute-start.14
  79.2 1.1 %collective-permute-done.16 = f32[16,16]{1,0:T(8,128)S(1)} collective-permute-done((f32[16,16]{1,0:T(8,128)S(1)}, f32[16,16]{1,0:T(8,128)S(1)}, u32[]{:S(2)}, u32[]{:S(2)}) %collective-permute-start.16) | collective-permute-done | bytes 1056 | tf_op jit(solution)/shard_map/ppermute | solution.py:232
  80.2 2.9 %collective-permute-done.15 = f32[16,16]{1,0:T(8,128)S(1)} collective-permute-done((f32[16,16]{1,0:T(8,128)S(1)}, f32[16,16]{1,0:T(8,128)S(1)}, u32[]{:S(2)}, u32[]{:S(2)}) %collective-permute-start.15) | collective-permute-done | bytes 1056 | tf_op jit(solution)/shard_map/ppermute | solution.py:232
  83.2 4.9 %final.1 = (f32[4,2,2,128,128]{4,3,2,1,0:T(8,128)}, f32[1,16]{1,0:T(1,128)}) custom-call(s32[1]{0:T(128)} %bitcast.me, f32[16,16]{1,0:T(8,128)S(1)} %add_add_fusion.gram, f32[4,2,2,128,128]{4,3,2,1,0:T(8,128)S(1)} %get-tuple-element.32.own, bf16[4,2,2,128,128]{4,3,2,1,0:T(8,128)(2,1)S(1)} %collective-permute-done.9.h1, ...), custom_call_target="tpu_custom_call" | custom-call | tf_op jit(solution)/shard_map/final/pallas_call | solution.py:323
  (26 shorter events, 0.3 us)
Async XLA Ops:
  0.6 0.9 %copy-start.2 = (bf16[3,4,2,32,128]{4,3,2,1,0:T(8,128)(2,1)S(1)}, bf16[3,4,2,32,128]{4,3,2,1,0:T(8,128)(2,1)}, u32[]{:S(2)}) copy-start(bf16[3,4,2,32,128]{4,3,2,1,0:T(8,128)(2,1)} %background.3) | copy-start | bytes 589828
  1.6 15.6 %copy-start.3 = (bf16[3,4,2,32,128]{4,3,2,1,0:T(8,128)(2,1)S(1)}, bf16[3,4,2,32,128]{4,3,2,1,0:T(8,128)(2,1)}, u32[]{:S(2)}) copy-start(bf16[3,4,2,32,128]{4,3,2,1,0:T(8,128)(2,1)} %background.3) | copy-start | bytes 589828
  1.6 8.9 %collective-permute-start = (bf16[3,4,32,128]{3,2,1,0:T(8,128)(2,1)S(1)}, bf16[3,4,32,128]{3,2,1,0:T(8,128)(2,1)S(1)}, u32[]{:S(2)}, u32[]{:S(2)}) collective-permute-start(bf16[3,4,32,128]{3,2,1,0:T(8,128)(2,1)S(1)} %get-tuple-element.22), channel_id=1, source_target_pairs={{0,1},{1,2},{2,3},{3,4},{4,5},{5,6},{6,7},{7,0},{8,9},{9,10},{10,1... | collective-permute-start | bytes 294920 | tf_op jit(solution)/shard_map/ppermute | solution.py:228
  4.6 6.7 %collective-permute-start.1 = (bf16[3,4,32,128]{3,2,1,0:T(8,128)(2,1)S(1)}, bf16[3,4,32,128]{3,2,1,0:T(8,128)(2,1)S(1)}, u32[]{:S(2)}, u32[]{:S(2)}) collective-permute-start(bf16[3,4,32,128]{3,2,1,0:T(8,128)(2,1)S(1)} %get-tuple-element.23), channel_id=1, source_target_pairs={{0,7},{1,0},{2,1},{3,2},{4,3},{5,4},{6,5},{7,6},{8,15},{9,8},{10,9... | collective-permute-start | bytes 294920 | tf_op jit(solution)/shard_map/ppermute | solution.py:228
  7.7 1.2 %copy-start = (f32[4,2,2,128,128]{4,3,2,1,0:T(8,128)S(1)}, f32[4,2,2,128,128]{4,3,2,1,0:T(8,128)}, u32[]{:S(2)}) copy-start(f32[4,2,2,128,128]{4,3,2,1,0:T(8,128)} %own.3) | copy-start | bytes 3145732
  8.9 30.3 %copy-start.1 = (f32[4,2,2,128,128]{4,3,2,1,0:T(8,128)S(1)}, f32[4,2,2,128,128]{4,3,2,1,0:T(8,128)}, u32[]{:S(2)}) copy-start(f32[4,2,2,128,128]{4,3,2,1,0:T(8,128)} %own.3) | copy-start | bytes 3145732
  11.3 11.1 %collective-permute-start.4 = (bf16[4,2,128,128]{3,2,1,0:T(8,128)(2,1)S(1)}, bf16[4,2,128,128]{3,2,1,0:T(8,128)(2,1)S(1)}, u32[]{:S(2)}, u32[]{:S(2)}) collective-permute-start(bf16[4,2,128,128]{3,2,1,0:T(8,128)(2,1)S(1)} %get-tuple-element.25), channel_id=1, source_target_pairs={{0,2},{1,3},{2,4},{3,5},{4,6},{5,7},{6,0},{7,1},{8,10},{9,11},{10,... | collective-permute-start | bytes 786440 | tf_op jit(solution)/shard_map/ppermute | solution.py:228
  12.2 14.2 %collective-permute-start.5 = (bf16[4,2,128,128]{3,2,1,0:T(8,128)(2,1)S(1)}, bf16[4,2,128,128]{3,2,1,0:T(8,128)(2,1)S(1)}, u32[]{:S(2)}, u32[]{:S(2)}) collective-permute-start(bf16[4,2,128,128]{3,2,1,0:T(8,128)(2,1)S(1)} %get-tuple-element.26), channel_id=1, source_target_pairs={{0,6},{1,7},{2,0},{3,1},{4,2},{5,3},{6,4},{7,5},{8,14},{9,15},{10,... | collective-permute-start | bytes 786440 | tf_op jit(solution)/shard_map/ppermute | solution.py:228
  15.1 24.1 %collective-permute-start.3 = (bf16[2,4,2,128,128]{4,3,2,1,0:T(8,128)(2,1)}, bf16[2,4,2,128,128]{4,3,2,1,0:T(8,128)(2,1)S(1)}, u32[]{:S(2)}, u32[]{:S(2)}) collective-permute-start(bf16[2,4,2,128,128]{4,3,2,1,0:T(8,128)(2,1)} %get-tuple-element.24), channel_id=1, source_target_pairs={{0,7},{1,0},{2,1},{3,2},{4,3},{5,4},{6,5},{7,6},{8,15},{9,8},{10,9... | collective-permute-start | bytes 1572872 | tf_op jit(solution)/shard_map/ppermute | solution.py:228
  17.0 22.2 %collective-permute-start.2 = (bf16[2,4,2,128,128]{4,3,2,1,0:T(8,128)(2,1)}, bf16[2,4,2,128,128]{4,3,2,1,0:T(8,128)(2,1)S(1)}, u32[]{:S(2)}, u32[]{:S(2)}) collective-permute-start(bf16[2,4,2,128,128]{4,3,2,1,0:T(8,128)(2,1)} %get-tuple-element.24), channel_id=1, source_target_pairs={{0,1},{1,2},{2,3},{3,4},{4,5},{5,6},{6,7},{7,0},{8,9},{9,10},{10,1... | collective-permute-start | bytes 1572872 | tf_op jit(solution)/shard_map/ppermute | solution.py:228
  17.2 11.4 %collective-permute-start.8 = (bf16[12,4,32,128]{3,2,1,0:T(8,128)(2,1)S(1)}, bf16[12,4,32,128]{3,2,1,0:T(8,128)(2,1)S(1)}, u32[]{:S(2)}, u32[]{:S(2)}) collective-permute-start(bf16[12,4,32,128]{3,2,1,0:T(8,128)(2,1)S(1)} %pack.1.bg0), channel_id=1, source_target_pairs={{0,24},{8,16},{16,8},{24,0},{1,25},{9,17},{17,9},{25,1},{2,26},{10... | collective-permute-start | bytes 1179656 | tf_op jit(solution)/shard_map/ppermute | solution.py:232
  22.4 14.7 %collective-permute-start.7 = (bf16[12,4,32,128]{3,2,1,0:T(8,128)(2,1)S(1)}, bf16[12,4,32,128]{3,2,1,0:T(8,128)(2,1)S(1)}, u32[]{:S(2)}, u32[]{:S(2)}) collective-permute-start(bf16[12,4,32,128]{3,2,1,0:T(8,128)(2,1)S(1)} %pack.1.bg0), channel_id=1, source_target_pairs={{0,16},{8,24},{16,0},{24,8},{1,17},{9,25},{17,1},{25,9},{2,18},{10... | collective-permute-start | bytes 1179656 | tf_op jit(solution)/shard_map/ppermute | solution.py:232
  26.4 0.7 copy-start.4
  27.1 10.0 %collective-permute-start.6 = (bf16[12,4,32,128]{3,2,1,0:T(8,128)(2,1)S(1)}, bf16[12,4,32,128]{3,2,1,0:T(8,128)(2,1)}, u32[]{:S(2)}, u32[]{:S(2)}) collective-permute-start(bf16[12,4,32,128]{3,2,1,0:T(8,128)(2,1)S(1)} %pack.1.bg0), channel_id=1, source_target_pairs={{0,8},{8,0},{16,24},{24,16},{1,9},{9,1},{17,25},{25,17},{2,10},{10... | collective-permute-start | bytes 1179656 | tf_op jit(solution)/shard_map/ppermute | solution.py:232
  39.2 1.0 %copy-start.5 = (bf16[4,2,128,128]{3,2,1,0:T(8,128)(2,1)S(1)}, bf16[4,2,128,128]{3,2,1,0:T(8,128)(2,1)}, u32[]{:S(2)}) copy-start(bf16[4,2,128,128]{3,2,1,0:T(8,128)(2,1)} %copy-done.4) | copy-start | bytes 786436
  46.1 11.8 %collective-permute-start.10 = (bf16[4,2,2,128,128]{4,3,2,1,0:T(8,128)(2,1)S(1)}, bf16[4,2,2,128,128]{4,3,2,1,0:T(8,128)(2,1)S(1)}, u32[]{:S(2)}, u32[]{:S(2)}) collective-permute-start(bf16[4,2,2,128,128]{4,3,2,1,0:T(8,128)(2,1)S(1)} %get-tuple-element.29.h0), channel_id=1, source_target_pairs={{0,16},{8,24},{16,0},{24,8},{1,17},{9,25},{17,1},{25,9},{2,18},{10... | collective-permute-start | bytes 1572872 | tf_op jit(solution)/shard_map/ppermute | solution.py:232
  47.7 10.9 %collective-permute-start.9 = (bf16[4,2,2,128,128]{4,3,2,1,0:T(8,128)(2,1)S(1)}, bf16[4,2,2,128,128]{4,3,2,1,0:T(8,128)(2,1)S(1)}, u32[]{:S(2)}, u32[]{:S(2)}) collective-permute-start(bf16[4,2,2,128,128]{4,3,2,1,0:T(8,128)(2,1)S(1)} %get-tuple-element.29.h0), channel_id=1, source_target_pairs={{0,8},{8,0},{16,24},{24,16},{1,9},{9,1},{17,25},{25,17},{2,10},{10... | collective-permute-start | bytes 1572872 | tf_op jit(solution)/shard_map/ppermute | solution.py:232
  57.9 1.9 %collective-permute-start.11 = (bf16[4,2,2,128,128]{4,3,2,1,0:T(8,128)(2,1)S(1)}, bf16[4,2,2,128,128]{4,3,2,1,0:T(8,128)(2,1)S(1)}, u32[]{:S(2)}, u32[]{:S(2)}) collective-permute-start(bf16[4,2,2,128,128]{4,3,2,1,0:T(8,128)(2,1)S(1)} %collective-permute-done.10.h2), channel_id=1, source_target_pairs={{0,8},{8,0},{16,24},{24,16},{1,9},{9,1},{17,25},{25,17},{2,10},{10... | collective-permute-start | bytes 1572872 | tf_op jit(solution)/shard_map/ppermute | solution.py:232
  57.9 14.3 %collective-permute-start.13 = (bf16[4,2,2,128,128]{4,3,2,1,0:T(8,128)(2,1)S(1)}, bf16[4,2,2,128,128]{4,3,2,1,0:T(8,128)(2,1)S(1)}, u32[]{:S(2)}, u32[]{:S(2)}) collective-permute-start(bf16[4,2,2,128,128]{4,3,2,1,0:T(8,128)(2,1)S(1)} %get-tuple-element.30), channel_id=1, source_target_pairs={{0,16},{8,24},{16,0},{24,8},{1,17},{9,25},{17,1},{25,9},{2,18},{10... | collective-permute-start | bytes 1572872 | tf_op jit(solution)/shard_map/ppermute | solution.py:232
  60.8 3.7 %collective-permute-start.12 = (f32[16,16]{1,0:T(8,128)S(1)}, f32[16,16]{1,0:T(8,128)S(1)}, u32[]{:S(2)}, u32[]{:S(2)}) collective-permute-start(f32[16,16]{1,0:T(8,128)S(1)} %gram.1), channel_id=1, source_target_pairs={{0,1},{1,0},{2,3},{3,2},{4,5},{5,4},{6,7},{7,6},{8,9},{9,8},{10,11... | collective-permute-start | bytes 3080 | tf_op jit(solution)/shard_map/ppermute | solution.py:232
  62.1 21.1 %collective-permute-start.17 = (bf16[4,2,2,128,128]{4,3,2,1,0:T(8,128)(2,1)S(1)}, bf16[4,2,2,128,128]{4,3,2,1,0:T(8,128)(2,1)S(1)}, u32[]{:S(2)}, u32[]{:S(2)}) collective-permute-start(bf16[4,2,2,128,128]{4,3,2,1,0:T(8,128)(2,1)S(1)} %get-tuple-element.30), channel_id=1, source_target_pairs={{0,8},{8,0},{16,24},{24,16},{1,9},{9,1},{17,25},{25,17},{2,10},{10... | collective-permute-start | bytes 1572872 | tf_op jit(solution)/shard_map/ppermute | solution.py:232
  72.2 10.9 %collective-permute-start.18 = (bf16[4,2,2,128,128]{4,3,2,1,0:T(8,128)(2,1)S(1)}, bf16[4,2,2,128,128]{4,3,2,1,0:T(8,128)(2,1)S(1)}, u32[]{:S(2)}, u32[]{:S(2)}) collective-permute-start(bf16[4,2,2,128,128]{4,3,2,1,0:T(8,128)(2,1)S(1)} %collective-permute-done.13.l2), channel_id=1, source_target_pairs={{0,8},{8,0},{16,24},{24,16},{1,9},{9,1},{17,25},{25,17},{2,10},{10... | collective-permute-start | bytes 1572872 | tf_op jit(solution)/shard_map/ppermute | solution.py:232
  72.2 8.0 %collective-permute-start.16 = (f32[16,16]{1,0:T(8,128)S(1)}, f32[16,16]{1,0:T(8,128)S(1)}, u32[]{:S(2)}, u32[]{:S(2)}) collective-permute-start(f32[16,16]{1,0:T(8,128)S(1)} %add.12), channel_id=1, source_target_pairs={{0,6},{1,7},{2,4},{3,5},{4,2},{5,3},{6,0},{7,1},{8,14},{9,15},{10,... | collective-permute-start | bytes 3080 | tf_op jit(solution)/shard_map/ppermute | solution.py:232
  78.6 4.5 %collective-permute-start.15 = (f32[16,16]{1,0:T(8,128)S(1)}, f32[16,16]{1,0:T(8,128)S(1)}, u32[]{:S(2)}, u32[]{:S(2)}) collective-permute-start(f32[16,16]{1,0:T(8,128)S(1)} %add.12), channel_id=1, source_target_pairs={{0,4},{1,5},{2,6},{3,7},{4,0},{5,1},{6,2},{7,3},{8,12},{9,13},{10,... | collective-permute-start | bytes 3080 | tf_op jit(solution)/shard_map/ppermute | solution.py:232
  78.6 4.5 %collective-permute-start.14 = (f32[16,16]{1,0:T(8,128)S(1)}, f32[16,16]{1,0:T(8,128)S(1)}, u32[]{:S(2)}, u32[]{:S(2)}) collective-permute-start(f32[16,16]{1,0:T(8,128)S(1)} %add.12), channel_id=1, source_target_pairs={{0,2},{1,3},{2,0},{3,1},{4,6},{5,7},{6,4},{7,5},{8,10},{9,11},{10,... | collective-permute-start | bytes 3080 | tf_op jit(solution)/shard_map/ppermute | solution.py:232

commit v4 on v3

--- a/solution.py
+++ b/solution.py
@@ -11,7 +11,8 @@
 diffusion = 0.5
 VM = pl.BlockSpec(memory_space=pltpu.VMEM)
 SM = pl.BlockSpec(memory_space=pltpu.SMEM)
-PARAMS = pltpu.CompilerParams(vmem_limit_bytes=40 * 1024 * 1024)
+SMALL = pltpu.CompilerParams(vmem_limit_bytes=12 * 1024 * 1024)
+PARAMS = pltpu.CompilerParams(vmem_limit_bytes=20 * 1024 * 1024)
 PAD = 8
 CHUNK = 16
 
@@ -27,7 +28,7 @@
         for x in range(0, columns, CHUNK):
             quarter, inner = divmod(x, bgs.shape[3])
             u, v, r, s = (
-                bgs[bg_first + row, f, quarter, inner : inner + CHUNK, :].astype(jnp.float32)
+                bgs[quarter, bg_first + row, f, inner : inner + CHUNK, :].astype(jnp.float32)
                 for f in range(4)
             )
             hu, hv, hr, hs = (0.5 * h) * u, (0.5 * h) * v, (0.5 * h) * r, h * s
@@ -101,13 +102,10 @@
         packed[9, f] = dn[2, f]
 
 
-def advance_kernel(me, own, up1, dn1, up2, dn2, bg0, bg1, bg2, bg3, adv, hi, lo, p0, p1, p2, bgs):
+def advance_kernel(me, own, up1, dn1, up2, dn2, bg0, bg1, bg2, bg3, adv, hia, hib, lo, p0, p1, p2, bg):
     vectors, _, rows, columns, _ = own.shape
-    position = me[0]
-    bgs[:, :, position] = bg0[...]
-    bgs[:, :, position ^ 2] = bg2[...]
-    bgs[:, :, position ^ 1] = bg1[...]
-    bgs[:, :, position ^ 3] = bg3[...]
+    for mask, part in enumerate((bg0, bg1, bg2, bg3)):
+        bg[me[0] ^ mask] = part[...]
     for vector in range(vectors):
         for f in range(2):
             k = 2 * vector + f
@@ -129,49 +127,73 @@
     def to_out(row, vector, f, x, value):
         adv[vector, f, row, x : x + CHUNK, :] = value
         top = value.astype(jnp.bfloat16)
-        hi[vector, f, row, x : x + CHUNK, :] = top
+        hi = (hia, hib)[vector // 2]
+        hi[vector % 2, f, row, x : x + CHUNK, :] = top
         lo[vector, f, row, x : x + CHUNK, :] = (value - top.astype(jnp.float32)).astype(jnp.bfloat16)
 
-    stage_rows(p0, 1, bgs, 0, 0.0, 1.0, None, 0, 6, vectors, to(p1))
+    stage_rows(p0, 1, bg, 0, 0.0, 1.0, None, 0, 6, vectors, to(p1))
     wrap(p1, columns)
-    stage_rows(p1, 1, bgs, 6, 0.75, 0.25, p0, 2, 4, vectors, to(p2))
+    stage_rows(p1, 1, bg, 6, 0.75, 0.25, p0, 2, 4, vectors, to(p2))
     wrap(p2, columns)
-    stage_rows(p2, 1, bgs, 10, 1.0 / 3.0, 2.0 / 3.0, p0, 3, 2, vectors, to_out)
-
-
-def gram_kernel(me, h0, h1, h2, h3, out, lines):
-    vectors, fields, rows, columns, levels = h0.shape
-    count = 4 * vectors
-    size = count * CHUNK
-    position = me[0]
+    stage_rows(p2, 1, bg, 10, 1.0 / 3.0, 2.0 / 3.0, p0, 3, 2, vectors, to_out)
+
+
+def stacked(blocks):
+    vectors, fields, rows, columns, _ = blocks[0].shape
     parts = []
     for f in range(fields):
         for y in range(rows):
             for x in range(0, columns, CHUNK):
                 parts.append(
                     jnp.concatenate(
-                        [h[j, f, y, x : x + CHUNK, :] for h in (h0, h1, h2, h3) for j in range(vectors)]
+                        [h[j, f, y, x : x + CHUNK, :] for h in blocks for j in range(vectors)]
                     )
                 )
-    flat = jnp.concatenate(parts, 1)
-    full = lax.dot_general(flat, flat, (((1,), (1,)), ((), ())), preferred_element_type=jnp.float32)
-    row = lax.broadcasted_iota(jnp.int32, (size, size), 0)
-    lane = lax.broadcasted_iota(jnp.int32, (size, size), 1)
+    return jnp.concatenate(parts, 1)
+
+
+def pairs(left, right):
+    full = lax.dot_general(left, right, (((1,), (1,)), ((), ())), preferred_element_type=jnp.float32)
+    row = lax.broadcasted_iota(jnp.int32, full.shape, 0)
+    lane = lax.broadcasted_iota(jnp.int32, full.shape, 1)
     full = jnp.where(row % CHUNK == lane % CHUNK, full, 0.0)
-    full = jnp.sum(full.reshape(count, CHUNK, size), axis=1)
-    for b in range(4):
+    return jnp.sum(full.reshape(full.shape[0] // CHUNK, CHUNK, full.shape[1]), axis=1)
+
+
+def gram_own_kernel(h0a, h0b, h1a, h1b, out):
+    flat = stacked((h0a, h0b, h1a, h1b))
+    out[...] = pairs(flat, flat)
+
+
+def gram_kernel(me, near, h0a, h0b, h1a, h1b, h2a, h2b, h3a, h3b, out, lines):
+    vectors = 2 * h0a.shape[0]
+    count = 4 * vectors
+    size = count * CHUNK
+    position = me[0]
+    flat, other = stacked((h0a, h0b, h1a, h1b)), stacked((h2a, h2b, h3a, h3b))
+    cross = pairs(flat, other)
+    far = pairs(other, other)
+    for b in range(2):
         for j in range(vectors):
             k = b * vectors + j
-            lines[pl.ds((position ^ b) * vectors + j, 1), :] = full[k : k + 1, :]
+            lines[pl.ds((position ^ b) * vectors + j, 1), :] = jnp.concatenate(
+                [near[k : k + 1, :], cross[k : k + 1, :]], 1
+            )
+            lines[pl.ds((position ^ (2 + b)) * vectors + j, 1), :] = jnp.concatenate(
+                [jnp.zeros_like(far[k : k + 1, :]), far[k : k + 1, :]], 1
+            )
     group = lax.broadcasted_iota(jnp.int32, (size, count), 0) // CHUNK
     target = ((group // vectors) ^ position) * vectors + group % vectors
     pick = jnp.where(target == lax.broadcasted_iota(jnp.int32, (size, count), 1), 1.0, 0.0)
-    out[...] = jnp.dot(
+    half = jnp.dot(
         lines[...], pick, precision=lax.Precision.HIGHEST, preferred_element_type=jnp.float32
     )
-
-
-def final_kernel(scale, me, gram, own, h1, h2, h3, l1, l2, l3, basis, growth, inv):
+    row = lax.broadcasted_iota(jnp.int32, (count, count), 0) // (2 * vectors)
+    lane = lax.broadcasted_iota(jnp.int32, (count, count), 1) // (2 * vectors)
+    out[...] = half + jnp.where(row == lane, 0.0, half.T)
+
+
+def final_kernel(scale, me, gram, own, h1a, h1b, h2a, h2b, h3a, h3b, l1, l2, l3, basis, growth, inv):
     vectors = own.shape[0]
     count = gram.shape[0]
     position = me[0]
@@ -207,10 +229,10 @@
                 def tile(t, carry, f=f, y=y, first=first, weights=weights):
                     at = pl.ds(pl.multiple_of(t * CHUNK, CHUNK), CHUNK)
                     values = [own[j, f, y, at, :] for j in range(vectors)]
-                    for h, l in ((h1, l1), (h2, l2), (h3, l3)):
+                    for h, l in (((h1a, h1b), l1), ((h2a, h2b), l2), ((h3a, h3b), l3)):
                         for j in range(vectors):
                             values.append(
-                                h[j, f, y, at, :].astype(jnp.float32)
+                                h[j // 2][j % 2, f, y, at, :].astype(jnp.float32)
                                 + l[j, f, y, at, :].astype(jnp.float32)
                             )
                     for i in range(2):
@@ -256,7 +278,7 @@
         out_shape=[jax.ShapeDtypeStruct((rows,) + row_shape.shape, jnp.bfloat16), row_shape, row_shape],
         in_specs=[VM],
         out_specs=[VM] * 3,
-        compiler_params=PARAMS,
+        compiler_params=SMALL,
         name="prep",
     )(tangents)
     edge = jax.ShapeDtypeStruct((3, 4) + background.shape[3:], jnp.bfloat16)
@@ -265,7 +287,7 @@
         out_shape=[edge, edge],
         in_specs=[VM],
         out_specs=[VM] * 2,
-        compiler_params=PARAMS,
+        compiler_params=SMALL,
         name="edges",
     )(background)
     bg_up = shift(bg_up, "space", 1)
@@ -275,46 +297,60 @@
     dn1 = shift(narrow, "space", -1)
     up2 = shift(last, "space", 2)
     dn2 = shift(lead, "space", -2)
-    bg0 = pl.pallas_call(
+    packed = pl.pallas_call(
         pack_kernel,
         out_shape=jax.ShapeDtypeStruct((12, 4) + background.shape[3:], jnp.bfloat16),
         in_specs=[VM] * 3,
         out_specs=VM,
-        compiler_params=PARAMS,
+        compiler_params=SMALL,
         name="pack",
     )(background, bg_up, bg_dn)
-    bg1, bg2, bg3 = (swap(bg0, "vec", mask) for mask in (1, 2, 3))
-
-    half = jax.ShapeDtypeStruct(tangents.shape, jnp.bfloat16)
+    bg2 = swap(packed, "vec", 2)
+    near_bg, far_bg, up2, dn2 = lax.optimization_barrier((packed, bg2, up2, dn2))
+    bgs = [packed, swap(near_bg, "vec", 1), bg2, swap(far_bg, "vec", 1)]
+
+    low = jax.ShapeDtypeStruct(tangents.shape, jnp.bfloat16)
+    pair = jax.ShapeDtypeStruct((vectors // 2,) + tangents.shape[1:], jnp.bfloat16)
     fields_all = 2 * vectors
-    adv, hi, lo = pl.pallas_call(
+    adv, hia, hib, lo = pl.pallas_call(
         advance_kernel,
-        out_shape=[jax.ShapeDtypeStruct(tangents.shape, jnp.float32), half, half],
+        out_shape=[jax.ShapeDtypeStruct(tangents.shape, jnp.float32), pair, pair, low],
         in_specs=[SM] + [VM] * 9,
-        out_specs=[VM] * 3,
+        out_specs=[VM] * 4,
         scratch_shapes=[
             pltpu.VMEM((8, fields_all, columns + 2 * PAD, levels), jnp.float32),
             pltpu.VMEM((6, fields_all, columns + 2 * PAD, levels), jnp.float32),
             pltpu.VMEM((4, fields_all, columns + 2 * PAD, levels), jnp.float32),
-            pltpu.VMEM((12, 4, 4, columns // 4, levels), jnp.bfloat16),
-        ],
+            pltpu.VMEM((4,) + packed.shape, jnp.bfloat16),
+            ],
         compiler_params=PARAMS,
         name="advance",
-    )(me, tangents, up1, dn1, up2, dn2, bg0, bg1, bg2, bg3)
-
-    h2, h1 = swap(hi, "vec", 2), swap(hi, "vec", 1)
+    )(me, tangents, up1, dn1, up2, dn2, *bgs)
+
+    h2a, h1a = swap(hia, "vec", 2), swap(hia, "vec", 1)
+    h2b, h1b = swap(hib, "vec", 2), swap(hib, "vec", 1)
+    near = pl.pallas_call(
+        gram_own_kernel,
+        out_shape=jax.ShapeDtypeStruct((2 * vectors, 2 * vectors * CHUNK), jnp.float32),
+        in_specs=[VM] * 4,
+        out_specs=VM,
+        compiler_params=SMALL,
+        name="gram_own",
+    )(hia, hib, h1a, h1b)
+    lo, near = lax.optimization_barrier((lo, near))
     l2, l1 = swap(lo, "vec", 2), swap(lo, "vec", 1)
-    h3 = swap(h2, "vec", 1)
+    h3a, h3b = swap(h2a, "vec", 1), swap(h2b, "vec", 1)
+    high = (hia, hib, h1a, h1b, h2a, h2b, h3a, h3b)
 
     gram = pl.pallas_call(
         gram_kernel,
         out_shape=jax.ShapeDtypeStruct((count, count), jnp.float32),
-        in_specs=[SM] + [VM] * 4,
+        in_specs=[SM] + [VM] * 9,
         out_specs=VM,
         scratch_shapes=[pltpu.VMEM((count, count * CHUNK), jnp.float32)],
-        compiler_params=PARAMS,
+        compiler_params=SMALL,
         name="gram",
-    )(me, hi, h1, h2, h3)
+    )(me, near, *high)
     gram = gram + swap(gram, "space", 1)
     gram, l2 = lax.optimization_barrier((gram, l2))
     l3 = swap(l2, "vec", 1)
@@ -326,12 +362,12 @@
             jax.ShapeDtypeStruct(tangents.shape, jnp.float32),
             jax.ShapeDtypeStruct((1, count), jnp.float32),
         ],
-        in_specs=[SM] + [VM] * 8,
+        in_specs=[SM] + [VM] * 11,
         out_specs=[VM, VM],
         scratch_shapes=[pltpu.VMEM((count, 2 * count), jnp.float32)],
-        compiler_params=PARAMS,
+        compiler_params=SMALL,
         name="final",
-    )(me, gram, adv, h1, h2, h3, l1, l2, l3)
+    )(me, gram, adv, *high[2:], l1, l2, l3)
     return basis, growth.reshape(count)
 
 

time: 88.4 us -> 86.1 us (0.974)
  waiting for transfers between devices: 46.9 us -> 44.9 us
    ppermute x13 -> x16, waiting for transfers between devices: 35.6 us -> 22.8 us  [swap(): lax.ppermute(value, axis, [(i, i ^ mask) for i in range(lax.axis_size(axi...]
    ppermute x6, waiting for transfers between devices: 11.3 us -> 22.1 us  [shift(): lax.ppermute(value, axis, [(i, (i + step) % count) for i in range(count)])]
    ppermute x13 -> x16, starting transfers between devices: 12 us -> 11.4 us  [swap(): lax.ppermute(value, axis, [(i, i ^ mask) for i in range(lax.axis_size(axi...]
  transfers between devices with their start and end apart: 19 -> 22, of which waited for: 13 -> 12; matrix products, arithmetic and copies ran while one was open for 0% -> 0% of each run, Pallas kernels for 2% -> 3%
where the time goes in v4:
time: 86.1 us; the launch traced here: 85.9 us
  waiting for transfers between devices  44.9 us (52%)
  starting transfers between devices  23.3 us (27%)
  Pallas kernels  13.1 us (15%)
  local copies, waits for them, and re-layouts  3.79 us (4%)
    ppermute x16, waiting for transfers between devices, swap(): lax.ppermute(value, axis, [(i, i ^ mask) for i in range(lax.axis_size(axi...  22.8 us
    ppermute x6, waiting for transfers between devices, shift(): lax.ppermute(value, axis, [(i, (i + step) % count) for i in range(count)])  22.1 us
    ppermute x6, starting transfers between devices, shift(): lax.ppermute(value, axis, [(i, (i + step) % count) for i in range(count)])  11.9 us
    ppermute x16, starting transfers between devices, swap(): lax.ppermute(value, axis, [(i, i ^ mask) for i in range(lax.axis_size(axi...  11.4 us
    pallas_call x1, Pallas kernels, on_device(): pl.pallas_call(advance_kernel, out_shape=[jax.ShapeDtypeStruct(tangents.s...  5.87 us
    pallas_call x1, Pallas kernels, on_device(): pl.pallas_call(functools.partial(final_kernel, 1.0 / cells), out_shape=[j...  4.96 us
    unnamed x12, local copies, waits for them, and re-layouts  3.79 us
  transfers between devices with their start and end apart: 22, of which 12 were waited for; matrix products, arithmetic and copies ran while one was open for 0% of the time, Pallas kernels for 3%

profile of v4, /device:TPU:0, one launch (start us, length us, event | category | flops | bytes accessed | tf_op | source)
XLA Modules:
  0.0 85.9 jit_solution(11056939186143271209)
XLA Ops:
  0.6 0.9 %copy-done.2 = bf16[3,4,2,32,128]{4,3,2,1,0:T(8,128)(2,1)S(1)} copy-done((bf16[3,4,2,32,128]{4,3,2,1,0:T(8,128)(2,1)S(1)}, bf16[3,4,2,32,128]{4,3,2,1,0:T(8,128)(2,1)}, u32[]{:S(2)}) %copy-start.2) | copy-done | bytes 196632
  1.6 3.0 %collective-permute-start = (bf16[3,4,32,128]{3,2,1,0:T(8,128)(2,1)S(1)}, bf16[3,4,32,128]{3,2,1,0:T(8,128)(2,1)S(1)}, u32[]{:S(2)}, u32[]{:S(2)}) collective-permute-start(bf16[3,4,32,128]{3,2,1,0:T(8,128)(2,1)S(1)} %get-tuple-element.29), channel_id=1, source_target_pairs={{0,1},{1,2},{2,3},{3,4},{4,5},{5,6},{6,7},{7,0},{8,9},{9,10},{10,1... | collective-permute-start | bytes 294920 | tf_op jit(solution)/shard_map/ppermute | solution.py:250
  4.6 3.1 %collective-permute-start.1 = (bf16[3,4,32,128]{3,2,1,0:T(8,128)(2,1)S(1)}, bf16[3,4,32,128]{3,2,1,0:T(8,128)(2,1)S(1)}, u32[]{:S(2)}, u32[]{:S(2)}) collective-permute-start(bf16[3,4,32,128]{3,2,1,0:T(8,128)(2,1)S(1)} %get-tuple-element.30), channel_id=1, source_target_pairs={{0,7},{1,0},{2,1},{3,2},{4,3},{5,4},{6,5},{7,6},{8,15},{9,8},{10,9... | collective-permute-start | bytes 294920 | tf_op jit(solution)/shard_map/ppermute | solution.py:250
  7.7 1.2 %copy-done = f32[4,2,2,128,128]{4,3,2,1,0:T(8,128)S(1)} copy-done((f32[4,2,2,128,128]{4,3,2,1,0:T(8,128)S(1)}, f32[4,2,2,128,128]{4,3,2,1,0:T(8,128)}, u32[]{:S(2)}) %copy-start) | copy-done | bytes 1048600
  8.9 0.9 %prep.1 = (bf16[2,4,2,128,128]{4,3,2,1,0:T(8,128)(2,1)}, bf16[4,2,128,128]{3,2,1,0:T(8,128)(2,1)S(1)}, bf16[4,2,128,128]{3,2,1,0:T(8,128)(2,1)S(1)}) custom-call(f32[4,2,2,128,128]{4,3,2,1,0:T(8,128)S(1)} %copy-done), custom_call_target="tpu_custom_call" | custom-call | tf_op jit(solution)/shard_map/prep/pallas_call | solution.py:276
  9.8 0.7 collective-permute-done.up
  10.5 0.8 collective-permute-done.1.dn
  11.3 1.6 %collective-permute-start.4 = (bf16[12,4,32,128]{3,2,1,0:T(8,128)(2,1)S(1)}, bf16[12,4,32,128]{3,2,1,0:T(8,128)(2,1)S(1)}, u32[]{:S(2)}, u32[]{:S(2)}) collective-permute-start(bf16[12,4,32,128]{3,2,1,0:T(8,128)(2,1)S(1)} %pack.1.bg0), channel_id=1, source_target_pairs={{0,16},{8,24},{16,0},{24,8},{1,17},{9,25},{17,1},{25,9},{2,18},{10... | collective-permute-start | bytes 1179656 | tf_op jit(solution)/shard_map/ppermute | solution.py:254
  12.9 0.9 %collective-permute-start.5 = (bf16[4,2,128,128]{3,2,1,0:T(8,128)(2,1)S(1)}, bf16[4,2,128,128]{3,2,1,0:T(8,128)(2,1)S(1)}, u32[]{:S(2)}, u32[]{:S(2)}) collective-permute-start(bf16[4,2,128,128]{3,2,1,0:T(8,128)(2,1)S(1)} %get-tuple-element.34), channel_id=1, source_target_pairs={{0,2},{1,3},{2,4},{3,5},{4,6},{5,7},{6,0},{7,1},{8,10},{9,11},{10,... | collective-permute-start | bytes 786440 | tf_op jit(solution)/shard_map/ppermute | solution.py:250
  13.8 2.9 %collective-permute-start.6 = (bf16[4,2,128,128]{3,2,1,0:T(8,128)(2,1)S(1)}, bf16[4,2,128,128]{3,2,1,0:T(8,128)(2,1)S(1)}, u32[]{:S(2)}, u32[]{:S(2)}) collective-permute-start(bf16[4,2,128,128]{3,2,1,0:T(8,128)(2,1)S(1)} %get-tuple-element.35), channel_id=1, source_target_pairs={{0,6},{1,7},{2,0},{3,1},{4,2},{5,3},{6,4},{7,5},{8,14},{9,15},{10,... | collective-permute-start | bytes 786440 | tf_op jit(solution)/shard_map/ppermute | solution.py:250
  16.7 2.0 %collective-permute-start.3 = (bf16[2,4,2,128,128]{4,3,2,1,0:T(8,128)(2,1)}, bf16[2,4,2,128,128]{4,3,2,1,0:T(8,128)(2,1)S(1)}, u32[]{:S(2)}, u32[]{:S(2)}) collective-permute-start(bf16[2,4,2,128,128]{4,3,2,1,0:T(8,128)(2,1)} %get-tuple-element.31), channel_id=1, source_target_pairs={{0,7},{1,0},{2,1},{3,2},{4,3},{5,4},{6,5},{7,6},{8,15},{9,8},{10,9... | collective-permute-start | bytes 1572872 | tf_op jit(solution)/shard_map/ppermute | solution.py:250
  18.8 5.2 %collective-permute-done.5.up2 = bf16[4,2,128,128]{3,2,1,0:T(8,128)(2,1)S(1)} collective-permute-done((bf16[4,2,128,128]{3,2,1,0:T(8,128)(2,1)S(1)}, bf16[4,2,128,128]{3,2,1,0:T(8,128)(2,1)S(1)}, u32[]{:S(2)}, u32[]{:S(2)}) %collective-permute-start.5) | collective-permute-done | bytes 262176 | tf_op jit(solution)/shard_map/ppermute | solution.py:250
  24.0 3.8 %collective-permute-done.6.dn2 = bf16[4,2,128,128]{3,2,1,0:T(8,128)(2,1)S(1)} collective-permute-done((bf16[4,2,128,128]{3,2,1,0:T(8,128)(2,1)S(1)}, bf16[4,2,128,128]{3,2,1,0:T(8,128)(2,1)S(1)}, u32[]{:S(2)}, u32[]{:S(2)}) %collective-permute-start.6) | collective-permute-done | bytes 262176 | tf_op jit(solution)/shard_map/ppermute | solution.py:250
  27.8 0.7 copy-done.4
  28.5 0.5 collective-permute-start.8
  29.0 11.5 %collective-permute-done.3.dn1 = bf16[2,4,2,128,128]{4,3,2,1,0:T(8,128)(2,1)S(1)} collective-permute-done((bf16[2,4,2,128,128]{4,3,2,1,0:T(8,128)(2,1)}, bf16[2,4,2,128,128]{4,3,2,1,0:T(8,128)(2,1)S(1)}, u32[]{:S(2)}, u32[]{:S(2)}) %collective-permute-start.3) | collective-permute-done | bytes 524320 | tf_op jit(solution)/shard_map/ppermute | solution.py:250
  40.6 0.9 %copy-done.5 = bf16[4,2,128,128]{3,2,1,0:T(8,128)(2,1)S(1)} copy-done((bf16[4,2,128,128]{3,2,1,0:T(8,128)(2,1)S(1)}, bf16[4,2,128,128]{3,2,1,0:T(8,128)(2,1)}, u32[]{:S(2)}) %copy-start.5) | copy-done | bytes 262168
  41.5 5.9 %advance.1 = (f32[4,2,2,128,128]{4,3,2,1,0:T(8,128)S(1)}, bf16[2,2,2,128,128]{4,3,2,1,0:T(8,128)(2,1)S(1)}, bf16[2,2,2,128,128]{4,3,2,1,0:T(8,128)(2,1)S(1)}, bf16[4,2,2,128,128]{4,3,2,1,0:T(8,128)(2,1)S(1)}) custom-call(s32[1]{0:T(128)} %bitcast.me, f32[4,2,2,128,128]{4,3,2,1,0:T(8,128)S(1)} %copy-done.1, ...), custom_call_target="tpu_custom_call" | custom-call | tf_op jit(solution)/shard_map/advance/pallas_call | solution.py:315
  48.5 1.5 %collective-permute-start.12 = (bf16[2,2,2,128,128]{4,3,2,1,0:T(8,128)(2,1)S(1)}, bf16[2,2,2,128,128]{4,3,2,1,0:T(8,128)(2,1)S(1)}, u32[]{:S(2)}, u32[]{:S(2)}) collective-permute-start(bf16[2,2,2,128,128]{4,3,2,1,0:T(8,128)(2,1)S(1)} %get-tuple-element.42.h0b), channel_id=1, source_target_pairs={{0,16},{8,24},{16,0},{24,8},{1,17},{9,25},{17,1},{25,9},{2,18},{10... | collective-permute-start | bytes 786440 | tf_op jit(solution)/shard_map/ppermute | solution.py:254
  50.5 0.6 collective-permute-start.16
  51.0 6.1 %collective-permute-done.11.h2a = bf16[2,2,2,128,128]{4,3,2,1,0:T(8,128)(2,1)S(1)} collective-permute-done((bf16[2,2,2,128,128]{4,3,2,1,0:T(8,128)(2,1)S(1)}, bf16[2,2,2,128,128]{4,3,2,1,0:T(8,128)(2,1)S(1)}, u32[]{:S(2)}, u32[]{:S(2)}) %collective-permute-start.11) | collective-permute-done | bytes 262176 | tf_op jit(solution)/shard_map/ppermute | solution.py:254
  57.1 5.6 %collective-permute-done.12.h2b = bf16[2,2,2,128,128]{4,3,2,1,0:T(8,128)(2,1)S(1)} collective-permute-done((bf16[2,2,2,128,128]{4,3,2,1,0:T(8,128)(2,1)S(1)}, bf16[2,2,2,128,128]{4,3,2,1,0:T(8,128)(2,1)S(1)}, u32[]{:S(2)}, u32[]{:S(2)}) %collective-permute-start.12) | collective-permute-done | bytes 262176 | tf_op jit(solution)/shard_map/ppermute | solution.py:254
  62.8 1.5 %collective-permute-done.14.h3b = bf16[2,2,2,128,128]{4,3,2,1,0:T(8,128)(2,1)S(1)} collective-permute-done((bf16[2,2,2,128,128]{4,3,2,1,0:T(8,128)(2,1)S(1)}, bf16[2,2,2,128,128]{4,3,2,1,0:T(8,128)(2,1)S(1)}, u32[]{:S(2)}, u32[]{:S(2)}) %collective-permute-start.14) | collective-permute-done | bytes 262176 | tf_op jit(solution)/shard_map/ppermute | solution.py:254
  64.3 0.9 %gram.1 = f32[16,16]{1,0:T(8,128)S(1)} custom-call(s32[1]{0:T(128)} %bitcast.me, f32[8,128]{1,0:T(8,128)S(1)} %gram_own.1.near, bf16[2,2,2,128,128]{4,3,2,1,0:T(8,128)(2,1)S(1)} %get-tuple-element.41.h0a, bf16[2,2,2,128,128]{4,3,2,1,0:T(8,128)(2,1)S(1)} %get-tuple-element.42.h0b, bf16[2,2,2,128,128]{4,3,2,1,0:T(8,128)(2,1)S(1)} %collective-permute-done.9.h1a, ...), custom_call_target="tpu_custom_call" | custom-call | tf_op jit(solution)/shard_map/gram/pallas_call | solution.py:345
  65.2 1.7 %collective-permute-start.15 = (f32[16,16]{1,0:T(8,128)S(1)}, f32[16,16]{1,0:T(8,128)S(1)}, u32[]{:S(2)}, u32[]{:S(2)}) collective-permute-start(f32[16,16]{1,0:T(8,128)S(1)} %gram.1), channel_id=1, source_target_pairs={{0,1},{1,0},{2,3},{3,2},{4,5},{5,4},{6,7},{7,6},{8,9},{9,8},{10,11... | collective-permute-start | bytes 3080 | tf_op jit(solution)/shard_map/ppermute | solution.py:254
  67.0 1.9 %collective-permute-done.15 = f32[16,16]{1,0:T(8,128)S(1)} collective-permute-done((f32[16,16]{1,0:T(8,128)S(1)}, f32[16,16]{1,0:T(8,128)S(1)}, u32[]{:S(2)}, u32[]{:S(2)}) %collective-permute-start.15) | collective-permute-done | bytes 1056 | tf_op jit(solution)/shard_map/ppermute | solution.py:254
  68.9 4.2 %collective-permute-done.16.l2 = bf16[4,2,2,128,128]{4,3,2,1,0:T(8,128)(2,1)S(1)} collective-permute-done((bf16[4,2,2,128,128]{4,3,2,1,0:T(8,128)(2,1)S(1)}, bf16[4,2,2,128,128]{4,3,2,1,0:T(8,128)(2,1)S(1)}, u32[]{:S(2)}, u32[]{:S(2)}) %collective-permute-start.16) | collective-permute-done | bytes 524320 | tf_op jit(solution)/shard_map/ppermute | solution.py:254
  73.1 3.2 %collective-permute-start.19 = (f32[16,16]{1,0:T(8,128)S(1)}, f32[16,16]{1,0:T(8,128)S(1)}, u32[]{:S(2)}, u32[]{:S(2)}) collective-permute-start(f32[16,16]{1,0:T(8,128)S(1)} %add.12), channel_id=1, source_target_pairs={{0,6},{1,7},{2,4},{3,5},{4,2},{5,3},{6,0},{7,1},{8,14},{9,15},{10,... | collective-permute-start | bytes 3080 | tf_op jit(solution)/shard_map/ppermute | solution.py:254
  76.4 1.2 %collective-permute-start.17 = (f32[16,16]{1,0:T(8,128)S(1)}, f32[16,16]{1,0:T(8,128)S(1)}, u32[]{:S(2)}, u32[]{:S(2)}) collective-permute-start(f32[16,16]{1,0:T(8,128)S(1)} %add.12), channel_id=1, source_target_pairs={{0,2},{1,3},{2,0},{3,1},{4,6},{5,7},{6,4},{7,5},{8,10},{9,11},{10,... | collective-permute-start | bytes 3080 | tf_op jit(solution)/shard_map/ppermute | solution.py:254
  77.5 1.1 %collective-permute-done.19 = f32[16,16]{1,0:T(8,128)S(1)} collective-permute-done((f32[16,16]{1,0:T(8,128)S(1)}, f32[16,16]{1,0:T(8,128)S(1)}, u32[]{:S(2)}, u32[]{:S(2)}) %collective-permute-start.19) | collective-permute-done | bytes 1056 | tf_op jit(solution)/shard_map/ppermute | solution.py:254
  78.6 2.3 %collective-permute-done.18 = f32[16,16]{1,0:T(8,128)S(1)} collective-permute-done((f32[16,16]{1,0:T(8,128)S(1)}, f32[16,16]{1,0:T(8,128)S(1)}, u32[]{:S(2)}, u32[]{:S(2)}) %collective-permute-start.18) | collective-permute-done | bytes 1056 | tf_op jit(solution)/shard_map/ppermute | solution.py:254
  80.9 5.0 %final.1 = (f32[4,2,2,128,128]{4,3,2,1,0:T(8,128)}, f32[1,16]{1,0:T(1,128)}) custom-call(s32[1]{0:T(128)} %bitcast.me, f32[16,16]{1,0:T(8,128)S(1)} %add_add_fusion.gram, f32[4,2,2,128,128]{4,3,2,1,0:T(8,128)S(1)} %get-tuple-element.46.own, bf16[2,2,2,128,128]{4,3,2,1,0:T(8,128)(2,1)S(1)} %collective-permute-done.9.h1a, ...), custom_call_target="tpu_custom_call" | custom-call | tf_op jit(solution)/shard_map/final/pallas_call | solution.py:359
  (33 shorter events, 1.6 us)
Async XLA Ops:
  0.6 0.9 %copy-start.2 = (bf16[3,4,2,32,128]{4,3,2,1,0:T(8,128)(2,1)S(1)}, bf16[3,4,2,32,128]{4,3,2,1,0:T(8,128)(2,1)}, u32[]{:S(2)}) copy-start(bf16[3,4,2,32,128]{4,3,2,1,0:T(8,128)(2,1)} %background.3) | copy-start | bytes 589828
  1.6 9.7 %copy-start.3 = (bf16[3,4,2,32,128]{4,3,2,1,0:T(8,128)(2,1)S(1)}, bf16[3,4,2,32,128]{4,3,2,1,0:T(8,128)(2,1)}, u32[]{:S(2)}) copy-start(bf16[3,4,2,32,128]{4,3,2,1,0:T(8,128)(2,1)} %background.3) | copy-start | bytes 589828
  1.6 8.9 %collective-permute-start = (bf16[3,4,32,128]{3,2,1,0:T(8,128)(2,1)S(1)}, bf16[3,4,32,128]{3,2,1,0:T(8,128)(2,1)S(1)}, u32[]{:S(2)}, u32[]{:S(2)}) collective-permute-start(bf16[3,4,32,128]{3,2,1,0:T(8,128)(2,1)S(1)} %get-tuple-element.29), channel_id=1, source_target_pairs={{0,1},{1,2},{2,3},{3,4},{4,5},{5,6},{6,7},{7,0},{8,9},{9,10},{10,1... | collective-permute-start | bytes 294920 | tf_op jit(solution)/shard_map/ppermute | solution.py:250
  4.6 6.7 %collective-permute-start.1 = (bf16[3,4,32,128]{3,2,1,0:T(8,128)(2,1)S(1)}, bf16[3,4,32,128]{3,2,1,0:T(8,128)(2,1)S(1)}, u32[]{:S(2)}, u32[]{:S(2)}) collective-permute-start(bf16[3,4,32,128]{3,2,1,0:T(8,128)(2,1)S(1)} %get-tuple-element.30), channel_id=1, source_target_pairs={{0,7},{1,0},{2,1},{3,2},{4,3},{5,4},{6,5},{7,6},{8,15},{9,8},{10,9... | collective-permute-start | bytes 294920 | tf_op jit(solution)/shard_map/ppermute | solution.py:250
  7.7 1.2 %copy-start = (f32[4,2,2,128,128]{4,3,2,1,0:T(8,128)S(1)}, f32[4,2,2,128,128]{4,3,2,1,0:T(8,128)}, u32[]{:S(2)}) copy-start(f32[4,2,2,128,128]{4,3,2,1,0:T(8,128)} %own.3) | copy-start | bytes 3145732
  8.9 31.7 %copy-start.1 = (f32[4,2,2,128,128]{4,3,2,1,0:T(8,128)S(1)}, f32[4,2,2,128,128]{4,3,2,1,0:T(8,128)}, u32[]{:S(2)}) copy-start(f32[4,2,2,128,128]{4,3,2,1,0:T(8,128)} %own.3) | copy-start | bytes 3145732
  11.3 17.2 %collective-permute-start.4 = (bf16[12,4,32,128]{3,2,1,0:T(8,128)(2,1)S(1)}, bf16[12,4,32,128]{3,2,1,0:T(8,128)(2,1)S(1)}, u32[]{:S(2)}, u32[]{:S(2)}) collective-permute-start(bf16[12,4,32,128]{3,2,1,0:T(8,128)(2,1)S(1)} %pack.1.bg0), channel_id=1, source_target_pairs={{0,16},{8,24},{16,0},{24,8},{1,17},{9,25},{17,1},{25,9},{2,18},{10... | collective-permute-start | bytes 1179656 | tf_op jit(solution)/shard_map/ppermute | solution.py:254
  12.9 11.1 %collective-permute-start.5 = (bf16[4,2,128,128]{3,2,1,0:T(8,128)(2,1)S(1)}, bf16[4,2,128,128]{3,2,1,0:T(8,128)(2,1)S(1)}, u32[]{:S(2)}, u32[]{:S(2)}) collective-permute-start(bf16[4,2,128,128]{3,2,1,0:T(8,128)(2,1)S(1)} %get-tuple-element.34), channel_id=1, source_target_pairs={{0,2},{1,3},{2,4},{3,5},{4,6},{5,7},{6,0},{7,1},{8,10},{9,11},{10,... | collective-permute-start | bytes 786440 | tf_op jit(solution)/shard_map/ppermute | solution.py:250
  13.8 14.0 %collective-permute-start.6 = (bf16[4,2,128,128]{3,2,1,0:T(8,128)(2,1)S(1)}, bf16[4,2,128,128]{3,2,1,0:T(8,128)(2,1)S(1)}, u32[]{:S(2)}, u32[]{:S(2)}) collective-permute-start(bf16[4,2,128,128]{3,2,1,0:T(8,128)(2,1)S(1)} %get-tuple-element.35), channel_id=1, source_target_pairs={{0,6},{1,7},{2,0},{3,1},{4,2},{5,3},{6,4},{7,5},{8,14},{9,15},{10,... | collective-permute-start | bytes 786440 | tf_op jit(solution)/shard_map/ppermute | solution.py:250
  16.7 23.8 %collective-permute-start.3 = (bf16[2,4,2,128,128]{4,3,2,1,0:T(8,128)(2,1)}, bf16[2,4,2,128,128]{4,3,2,1,0:T(8,128)(2,1)S(1)}, u32[]{:S(2)}, u32[]{:S(2)}) collective-permute-start(bf16[2,4,2,128,128]{4,3,2,1,0:T(8,128)(2,1)} %get-tuple-element.31), channel_id=1, source_target_pairs={{0,7},{1,0},{2,1},{3,2},{4,3},{5,4},{6,5},{7,6},{8,15},{9,8},{10,9... | collective-permute-start | bytes 1572872 | tf_op jit(solution)/shard_map/ppermute | solution.py:250
  18.8 21.8 %collective-permute-start.2 = (bf16[2,4,2,128,128]{4,3,2,1,0:T(8,128)(2,1)}, bf16[2,4,2,128,128]{4,3,2,1,0:T(8,128)(2,1)S(1)}, u32[]{:S(2)}, u32[]{:S(2)}) collective-permute-start(bf16[2,4,2,128,128]{4,3,2,1,0:T(8,128)(2,1)} %get-tuple-element.31), channel_id=1, source_target_pairs={{0,1},{1,2},{2,3},{3,4},{4,5},{5,6},{6,7},{7,0},{8,9},{9,10},{10,1... | collective-permute-start | bytes 1572872 | tf_op jit(solution)/shard_map/ppermute | solution.py:250
  27.8 0.7 copy-start.4
  28.5 12.1 %collective-permute-start.7 = (bf16[12,4,32,128]{3,2,1,0:T(8,128)(2,1)S(1)}, bf16[12,4,32,128]{3,2,1,0:T(8,128)(2,1)S(1)}, u32[]{:S(2)}, u32[]{:S(2)}) collective-permute-start(bf16[12,4,32,128]{3,2,1,0:T(8,128)(2,1)S(1)} %pack.1.bg0), channel_id=1, source_target_pairs={{0,8},{8,0},{16,24},{24,16},{1,9},{9,1},{17,25},{25,17},{2,10},{10... | collective-permute-start | bytes 1179656 | tf_op jit(solution)/shard_map/ppermute | solution.py:254
  28.5 12.1 %collective-permute-start.8 = (bf16[12,4,32,128]{3,2,1,0:T(8,128)(2,1)S(1)}, bf16[12,4,32,128]{3,2,1,0:T(8,128)(2,1)}, u32[]{:S(2)}, u32[]{:S(2)}) collective-permute-start(bf16[12,4,32,128]{3,2,1,0:T(8,128)(2,1)S(1)} %collective-permute-done.4.bg2), channel_id=1, source_target_pairs={{0,8},{8,0},{16,24},{24,16},{1,9},{9,1},{17,25},{25,17},{2,10},{10... | collective-permute-start | bytes 1179656 | tf_op jit(solution)/shard_map/ppermute | solution.py:254
  40.6 1.0 %copy-start.5 = (bf16[4,2,128,128]{3,2,1,0:T(8,128)(2,1)S(1)}, bf16[4,2,128,128]{3,2,1,0:T(8,128)(2,1)}, u32[]{:S(2)}) copy-start(bf16[4,2,128,128]{3,2,1,0:T(8,128)(2,1)} %copy-done.4) | copy-start | bytes 786436
  47.4 2.6 %collective-permute-start.9 = (bf16[2,2,2,128,128]{4,3,2,1,0:T(8,128)(2,1)S(1)}, bf16[2,2,2,128,128]{4,3,2,1,0:T(8,128)(2,1)S(1)}, u32[]{:S(2)}, u32[]{:S(2)}) collective-permute-start(bf16[2,2,2,128,128]{4,3,2,1,0:T(8,128)(2,1)S(1)} %get-tuple-element.41.h0a), channel_id=1, source_target_pairs={{0,8},{8,0},{16,24},{24,16},{1,9},{9,1},{17,25},{25,17},{2,10},{10... | collective-permute-start | bytes 786440 | tf_op jit(solution)/shard_map/ppermute | solution.py:254
  47.5 2.5 %collective-permute-start.10 = (bf16[2,2,2,128,128]{4,3,2,1,0:T(8,128)(2,1)S(1)}, bf16[2,2,2,128,128]{4,3,2,1,0:T(8,128)(2,1)S(1)}, u32[]{:S(2)}, u32[]{:S(2)}) collective-permute-start(bf16[2,2,2,128,128]{4,3,2,1,0:T(8,128)(2,1)S(1)} %get-tuple-element.42.h0b), channel_id=1, source_target_pairs={{0,8},{8,0},{16,24},{24,16},{1,9},{9,1},{17,25},{25,17},{2,10},{10... | collective-permute-start | bytes 786440 | tf_op jit(solution)/shard_map/ppermute | solution.py:254
  48.0 9.2 %collective-permute-start.11 = (bf16[2,2,2,128,128]{4,3,2,1,0:T(8,128)(2,1)S(1)}, bf16[2,2,2,128,128]{4,3,2,1,0:T(8,128)(2,1)S(1)}, u32[]{:S(2)}, u32[]{:S(2)}) collective-permute-start(bf16[2,2,2,128,128]{4,3,2,1,0:T(8,128)(2,1)S(1)} %get-tuple-element.41.h0a), channel_id=1, source_target_pairs={{0,16},{8,24},{16,0},{24,8},{1,17},{9,25},{17,1},{25,9},{2,18},{10... | collective-permute-start | bytes 786440 | tf_op jit(solution)/shard_map/ppermute | solution.py:254
  48.5 14.3 %collective-permute-start.12 = (bf16[2,2,2,128,128]{4,3,2,1,0:T(8,128)(2,1)S(1)}, bf16[2,2,2,128,128]{4,3,2,1,0:T(8,128)(2,1)S(1)}, u32[]{:S(2)}, u32[]{:S(2)}) collective-permute-start(bf16[2,2,2,128,128]{4,3,2,1,0:T(8,128)(2,1)S(1)} %get-tuple-element.42.h0b), channel_id=1, source_target_pairs={{0,16},{8,24},{16,0},{24,8},{1,17},{9,25},{17,1},{25,9},{2,18},{10... | collective-permute-start | bytes 786440 | tf_op jit(solution)/shard_map/ppermute | solution.py:254
  50.5 22.6 %collective-permute-start.16 = (bf16[4,2,2,128,128]{4,3,2,1,0:T(8,128)(2,1)S(1)}, bf16[4,2,2,128,128]{4,3,2,1,0:T(8,128)(2,1)S(1)}, u32[]{:S(2)}, u32[]{:S(2)}) collective-permute-start(bf16[4,2,2,128,128]{4,3,2,1,0:T(8,128)(2,1)S(1)} %get-tuple-element.44), channel_id=1, source_target_pairs={{0,16},{8,24},{16,0},{24,8},{1,17},{9,25},{17,1},{25,9},{2,18},{10... | collective-permute-start | bytes 1572872 | tf_op jit(solution)/shard_map/ppermute | solution.py:254
  57.1 5.6 %collective-permute-start.13 = (bf16[2,2,2,128,128]{4,3,2,1,0:T(8,128)(2,1)S(1)}, bf16[2,2,2,128,128]{4,3,2,1,0:T(8,128)(2,1)S(1)}, u32[]{:S(2)}, u32[]{:S(2)}) collective-permute-start(bf16[2,2,2,128,128]{4,3,2,1,0:T(8,128)(2,1)S(1)} %collective-permute-done.11.h2a), channel_id=1, source_target_pairs={{0,8},{8,0},{16,24},{24,16},{1,9},{9,1},{17,25},{25,17},{2,10},{10... | collective-permute-start | bytes 786440 | tf_op jit(solution)/shard_map/ppermute | solution.py:254
  62.8 1.5 %collective-permute-start.14 = (bf16[2,2,2,128,128]{4,3,2,1,0:T(8,128)(2,1)S(1)}, bf16[2,2,2,128,128]{4,3,2,1,0:T(8,128)(2,1)S(1)}, u32[]{:S(2)}, u32[]{:S(2)}) collective-permute-start(bf16[2,2,2,128,128]{4,3,2,1,0:T(8,128)(2,1)S(1)} %collective-permute-done.12.h2b), channel_id=1, source_target_pairs={{0,8},{8,0},{16,24},{24,16},{1,9},{9,1},{17,25},{25,17},{2,10},{10... | collective-permute-start | bytes 786440 | tf_op jit(solution)/shard_map/ppermute | solution.py:254
  65.2 3.7 %collective-permute-start.15 = (f32[16,16]{1,0:T(8,128)S(1)}, f32[16,16]{1,0:T(8,128)S(1)}, u32[]{:S(2)}, u32[]{:S(2)}) collective-permute-start(f32[16,16]{1,0:T(8,128)S(1)} %gram.1), channel_id=1, source_target_pairs={{0,1},{1,0},{2,3},{3,2},{4,5},{5,4},{6,7},{7,6},{8,9},{9,8},{10,11... | collective-permute-start | bytes 3080 | tf_op jit(solution)/shard_map/ppermute | solution.py:254
  67.0 13.9 %collective-permute-start.20 = (bf16[4,2,2,128,128]{4,3,2,1,0:T(8,128)(2,1)S(1)}, bf16[4,2,2,128,128]{4,3,2,1,0:T(8,128)(2,1)S(1)}, u32[]{:S(2)}, u32[]{:S(2)}) collective-permute-start(bf16[4,2,2,128,128]{4,3,2,1,0:T(8,128)(2,1)S(1)} %get-tuple-element.44), channel_id=1, source_target_pairs={{0,8},{8,0},{16,24},{24,16},{1,9},{9,1},{17,25},{25,17},{2,10},{10... | collective-permute-start | bytes 1572872 | tf_op jit(solution)/shard_map/ppermute | solution.py:254
  73.1 7.8 %collective-permute-start.21 = (bf16[4,2,2,128,128]{4,3,2,1,0:T(8,128)(2,1)S(1)}, bf16[4,2,2,128,128]{4,3,2,1,0:T(8,128)(2,1)S(1)}, u32[]{:S(2)}, u32[]{:S(2)}) collective-permute-start(bf16[4,2,2,128,128]{4,3,2,1,0:T(8,128)(2,1)S(1)} %collective-permute-done.16.l2), channel_id=1, source_target_pairs={{0,8},{8,0},{16,24},{24,16},{1,9},{9,1},{17,25},{25,17},{2,10},{10... | collective-permute-start | bytes 1572872 | tf_op jit(solution)/shard_map/ppermute | solution.py:254
  73.1 5.4 %collective-permute-start.19 = (f32[16,16]{1,0:T(8,128)S(1)}, f32[16,16]{1,0:T(8,128)S(1)}, u32[]{:S(2)}, u32[]{:S(2)}) collective-permute-start(f32[16,16]{1,0:T(8,128)S(1)} %add.12), channel_id=1, source_target_pairs={{0,6},{1,7},{2,4},{3,5},{4,2},{5,3},{6,0},{7,1},{8,14},{9,15},{10,... | collective-permute-start | bytes 3080 | tf_op jit(solution)/shard_map/ppermute | solution.py:254
  76.4 4.5 %collective-permute-start.18 = (f32[16,16]{1,0:T(8,128)S(1)}, f32[16,16]{1,0:T(8,128)S(1)}, u32[]{:S(2)}, u32[]{:S(2)}) collective-permute-start(f32[16,16]{1,0:T(8,128)S(1)} %add.12), channel_id=1, source_target_pairs={{0,4},{1,5},{2,6},{3,7},{4,0},{5,1},{6,2},{7,3},{8,12},{9,13},{10,... | collective-permute-start | bytes 3080 | tf_op jit(solution)/shard_map/ppermute | solution.py:254
  76.4 4.5 %collective-permute-start.17 = (f32[16,16]{1,0:T(8,128)S(1)}, f32[16,16]{1,0:T(8,128)S(1)}, u32[]{:S(2)}, u32[]{:S(2)}) collective-permute-start(f32[16,16]{1,0:T(8,128)S(1)} %add.12), channel_id=1, source_target_pairs={{0,2},{1,3},{2,0},{3,1},{4,6},{5,7},{6,4},{7,5},{8,10},{9,11},{10,... | collective-permute-start | bytes 3080 | tf_op jit(solution)/shard_map/ppermute | solution.py:254

commit v5 on v4

--- a/solution.py
+++ b/solution.py
@@ -208,8 +208,10 @@
     for k in range(count):
         pivot = table[k : k + 1, k : k + 1]
         pivots = jnp.where(wide == k, pivot, pivots)
-        scaled = table[k : k + 1, :] / jnp.sqrt(pivot)
-        below = jnp.where(row[:, :1] > k, table[:, k : k + 1] / jnp.sqrt(pivot), 0.0)
+        root = lax.rsqrt(pivot)
+        root = root * (1.5 - 0.5 * pivot * root * root)
+        scaled = table[k : k + 1, :] * root
+        below = jnp.where(row[:, :1] > k, table[:, k : k + 1] * root, 0.0)
         table = jnp.where(row == k, scaled, table - below * scaled)
     growth[...] = 0.5 * jnp.log(pivots)
     inv[...] = table
@@ -252,18 +254,6 @@
 
 def swap(value, axis, mask):
     return lax.ppermute(value, axis, [(i, i ^ mask) for i in range(lax.axis_size(axis))])
-
-
-def summed(value):
-    mask, size = 2, lax.axis_size("space")
-    while mask < size:
-        if 2 * mask < size:
-            one, two, three = (swap(value, "space", k) for k in (mask, 2 * mask, 3 * mask))
-            value = (value + one) + (two + three)
-        else:
-            value = value + swap(value, "space", mask)
-        mask *= 4
-    return value
 
 
 def on_device(tangents, background):
@@ -351,10 +341,13 @@
         compiler_params=SMALL,
         name="gram",
     )(me, near, *high)
-    gram = gram + swap(gram, "space", 1)
-    gram, l2 = lax.optimization_barrier((gram, l2))
-    l3 = swap(l2, "vec", 1)
-    gram = summed(gram)
+    mask, size = 1, lax.axis_size("space")
+    while mask < size:
+        if 2 * mask >= size:
+            gram, l2 = lax.optimization_barrier((gram, l2))
+            l3 = swap(l2, "vec", 1)
+        gram = gram + swap(gram, "space", mask)
+        mask *= 2
 
     basis, growth = pl.pallas_call(
         functools.partial(final_kernel, 1.0 / cells),

time: 86.1 us -> 82.8 us (0.962)
  starting transfers between devices: 23.3 us -> 20.2 us
    ppermute x16 -> x15, starting transfers between devices: 11.4 us -> 8.23 us  [swap(): lax.ppermute(value, axis, [(i, i ^ mask) for i in range(lax.axis_size(axi...]
    ppermute x16 -> x15, waiting for transfers between devices: 22.8 us -> 22.7 us  [swap(): lax.ppermute(value, axis, [(i, i ^ mask) for i in range(lax.axis_size(axi...]
  transfers between devices with their start and end apart: 22 -> 21, of which waited for: 12 -> 12; matrix products, arithmetic and copies ran while one was open for 0% -> 0% of each run, Pallas kernels for 3% -> 3%
where the time goes in v5:
time: 82.8 us; the launch traced here: 82.5 us
  waiting for transfers between devices  44.8 us (54%)
  starting transfers between devices  20.2 us (24%)
  Pallas kernels  13 us (16%)
  local copies, waits for them, and re-layouts  3.79 us (5%)
    ppermute x15, waiting for transfers between devices, swap(): lax.ppermute(value, axis, [(i, i ^ mask) for i in range(lax.axis_size(axi...  22.7 us
    ppermute x6, waiting for transfers between devices, shift(): lax.ppermute(value, axis, [(i, (i + step) % count) for i in range(count)])  22.1 us
    ppermute x6, starting transfers between devices, shift(): lax.ppermute(value, axis, [(i, (i + step) % count) for i in range(count)])  11.9 us
    ppermute x15, starting transfers between devices, swap(): lax.ppermute(value, axis, [(i, i ^ mask) for i in range(lax.axis_size(axi...  8.23 us
    pallas_call x1, Pallas kernels, on_device(): pl.pallas_call(advance_kernel, out_shape=[jax.ShapeDtypeStruct(tangents.s...  5.87 us
    pallas_call x1, Pallas kernels, on_device(): pl.pallas_call(functools.partial(final_kernel, 1.0 / cells), out_shape=[j...  4.86 us
    unnamed x12, local copies, waits for them, and re-layouts  3.79 us
  transfers between devices with their start and end apart: 21, of which 12 were waited for; matrix products, arithmetic and copies ran while one was open for 0% of the time, Pallas kernels for 3%

profile of v5, /device:TPU:0, one launch (start us, length us, event | category | flops | bytes accessed | tf_op | source)
XLA Modules:
  0.0 82.5 jit_solution(17965944142861177103)
XLA Ops:
  0.6 0.9 %copy-done.2 = bf16[3,4,2,32,128]{4,3,2,1,0:T(8,128)(2,1)S(1)} copy-done((bf16[3,4,2,32,128]{4,3,2,1,0:T(8,128)(2,1)S(1)}, bf16[3,4,2,32,128]{4,3,2,1,0:T(8,128)(2,1)}, u32[]{:S(2)}) %copy-start.2) | copy-done | bytes 196632
  1.6 3.0 %collective-permute-start = (bf16[3,4,32,128]{3,2,1,0:T(8,128)(2,1)S(1)}, bf16[3,4,32,128]{3,2,1,0:T(8,128)(2,1)S(1)}, u32[]{:S(2)}, u32[]{:S(2)}) collective-permute-start(bf16[3,4,32,128]{3,2,1,0:T(8,128)(2,1)S(1)} %get-tuple-element.29), channel_id=1, source_target_pairs={{0,1},{1,2},{2,3},{3,4},{4,5},{5,6},{6,7},{7,0},{8,9},{9,10},{10,1... | collective-permute-start | bytes 294920 | tf_op jit(solution)/shard_map/ppermute | solution.py:252
  4.6 3.1 %collective-permute-start.1 = (bf16[3,4,32,128]{3,2,1,0:T(8,128)(2,1)S(1)}, bf16[3,4,32,128]{3,2,1,0:T(8,128)(2,1)S(1)}, u32[]{:S(2)}, u32[]{:S(2)}) collective-permute-start(bf16[3,4,32,128]{3,2,1,0:T(8,128)(2,1)S(1)} %get-tuple-element.30), channel_id=1, source_target_pairs={{0,7},{1,0},{2,1},{3,2},{4,3},{5,4},{6,5},{7,6},{8,15},{9,8},{10,9... | collective-permute-start | bytes 294920 | tf_op jit(solution)/shard_map/ppermute | solution.py:252
  7.7 1.2 %copy-done = f32[4,2,2,128,128]{4,3,2,1,0:T(8,128)S(1)} copy-done((f32[4,2,2,128,128]{4,3,2,1,0:T(8,128)S(1)}, f32[4,2,2,128,128]{4,3,2,1,0:T(8,128)}, u32[]{:S(2)}) %copy-start) | copy-done | bytes 1048600
  8.9 0.9 %prep.1 = (bf16[2,4,2,128,128]{4,3,2,1,0:T(8,128)(2,1)}, bf16[4,2,128,128]{3,2,1,0:T(8,128)(2,1)S(1)}, bf16[4,2,128,128]{3,2,1,0:T(8,128)(2,1)S(1)}) custom-call(f32[4,2,2,128,128]{4,3,2,1,0:T(8,128)S(1)} %copy-done), custom_call_target="tpu_custom_call" | custom-call | tf_op jit(solution)/shard_map/prep/pallas_call | solution.py:266
  9.8 0.7 collective-permute-done.up
  10.5 0.8 collective-permute-done.1.dn
  11.3 1.6 %collective-permute-start.4 = (bf16[12,4,32,128]{3,2,1,0:T(8,128)(2,1)S(1)}, bf16[12,4,32,128]{3,2,1,0:T(8,128)(2,1)S(1)}, u32[]{:S(2)}, u32[]{:S(2)}) collective-permute-start(bf16[12,4,32,128]{3,2,1,0:T(8,128)(2,1)S(1)} %pack.1.bg0), channel_id=1, source_target_pairs={{0,16},{8,24},{16,0},{24,8},{1,17},{9,25},{17,1},{25,9},{2,18},{10... | collective-permute-start | bytes 1179656 | tf_op jit(solution)/shard_map/ppermute | solution.py:256
  12.9 0.9 %collective-permute-start.5 = (bf16[4,2,128,128]{3,2,1,0:T(8,128)(2,1)S(1)}, bf16[4,2,128,128]{3,2,1,0:T(8,128)(2,1)S(1)}, u32[]{:S(2)}, u32[]{:S(2)}) collective-permute-start(bf16[4,2,128,128]{3,2,1,0:T(8,128)(2,1)S(1)} %get-tuple-element.34), channel_id=1, source_target_pairs={{0,2},{1,3},{2,4},{3,5},{4,6},{5,7},{6,0},{7,1},{8,10},{9,11},{10,... | collective-permute-start | bytes 786440 | tf_op jit(solution)/shard_map/ppermute | solution.py:252
  13.8 2.9 %collective-permute-start.6 = (bf16[4,2,128,128]{3,2,1,0:T(8,128)(2,1)S(1)}, bf16[4,2,128,128]{3,2,1,0:T(8,128)(2,1)S(1)}, u32[]{:S(2)}, u32[]{:S(2)}) collective-permute-start(bf16[4,2,128,128]{3,2,1,0:T(8,128)(2,1)S(1)} %get-tuple-element.35), channel_id=1, source_target_pairs={{0,6},{1,7},{2,0},{3,1},{4,2},{5,3},{6,4},{7,5},{8,14},{9,15},{10,... | collective-permute-start | bytes 786440 | tf_op jit(solution)/shard_map/ppermute | solution.py:252
  16.7 2.0 %collective-permute-start.3 = (bf16[2,4,2,128,128]{4,3,2,1,0:T(8,128)(2,1)}, bf16[2,4,2,128,128]{4,3,2,1,0:T(8,128)(2,1)S(1)}, u32[]{:S(2)}, u32[]{:S(2)}) collective-permute-start(bf16[2,4,2,128,128]{4,3,2,1,0:T(8,128)(2,1)} %get-tuple-element.31), channel_id=1, source_target_pairs={{0,7},{1,0},{2,1},{3,2},{4,3},{5,4},{6,5},{7,6},{8,15},{9,8},{10,9... | collective-permute-start | bytes 1572872 | tf_op jit(solution)/shard_map/ppermute | solution.py:252
  18.8 5.2 %collective-permute-done.5.up2 = bf16[4,2,128,128]{3,2,1,0:T(8,128)(2,1)S(1)} collective-permute-done((bf16[4,2,128,128]{3,2,1,0:T(8,128)(2,1)S(1)}, bf16[4,2,128,128]{3,2,1,0:T(8,128)(2,1)S(1)}, u32[]{:S(2)}, u32[]{:S(2)}) %collective-permute-start.5) | collective-permute-done | bytes 262176 | tf_op jit(solution)/shard_map/ppermute | solution.py:252
  24.0 3.8 %collective-permute-done.6.dn2 = bf16[4,2,128,128]{3,2,1,0:T(8,128)(2,1)S(1)} collective-permute-done((bf16[4,2,128,128]{3,2,1,0:T(8,128)(2,1)S(1)}, bf16[4,2,128,128]{3,2,1,0:T(8,128)(2,1)S(1)}, u32[]{:S(2)}, u32[]{:S(2)}) %collective-permute-start.6) | collective-permute-done | bytes 262176 | tf_op jit(solution)/shard_map/ppermute | solution.py:252
  27.8 0.7 copy-done.4
  28.5 0.5 collective-permute-start.8
  29.0 11.5 %collective-permute-done.3.dn1 = bf16[2,4,2,128,128]{4,3,2,1,0:T(8,128)(2,1)S(1)} collective-permute-done((bf16[2,4,2,128,128]{4,3,2,1,0:T(8,128)(2,1)}, bf16[2,4,2,128,128]{4,3,2,1,0:T(8,128)(2,1)S(1)}, u32[]{:S(2)}, u32[]{:S(2)}) %collective-permute-start.3) | collective-permute-done | bytes 524320 | tf_op jit(solution)/shard_map/ppermute | solution.py:252
  40.6 0.9 %copy-done.5 = bf16[4,2,128,128]{3,2,1,0:T(8,128)(2,1)S(1)} copy-done((bf16[4,2,128,128]{3,2,1,0:T(8,128)(2,1)S(1)}, bf16[4,2,128,128]{3,2,1,0:T(8,128)(2,1)}, u32[]{:S(2)}) %copy-start.5) | copy-done | bytes 262168
  41.5 5.9 %advance.1 = (f32[4,2,2,128,128]{4,3,2,1,0:T(8,128)S(1)}, bf16[2,2,2,128,128]{4,3,2,1,0:T(8,128)(2,1)S(1)}, bf16[2,2,2,128,128]{4,3,2,1,0:T(8,128)(2,1)S(1)}, bf16[4,2,2,128,128]{4,3,2,1,0:T(8,128)(2,1)S(1)}) custom-call(s32[1]{0:T(128)} %bitcast.me, f32[4,2,2,128,128]{4,3,2,1,0:T(8,128)S(1)} %copy-done.1, ...), custom_call_target="tpu_custom_call" | custom-call | tf_op jit(solution)/shard_map/advance/pallas_call | solution.py:305
  48.0 0.5 collective-permute-start.11
  48.5 1.5 %collective-permute-start.12 = (bf16[2,2,2,128,128]{4,3,2,1,0:T(8,128)(2,1)S(1)}, bf16[2,2,2,128,128]{4,3,2,1,0:T(8,128)(2,1)S(1)}, u32[]{:S(2)}, u32[]{:S(2)}) collective-permute-start(bf16[2,2,2,128,128]{4,3,2,1,0:T(8,128)(2,1)S(1)} %get-tuple-element.42.h0b), channel_id=1, source_target_pairs={{0,16},{8,24},{16,0},{24,8},{1,17},{9,25},{17,1},{25,9},{2,18},{10... | collective-permute-start | bytes 786440 | tf_op jit(solution)/shard_map/ppermute | solution.py:256
  50.5 0.6 collective-permute-start.17
  51.0 6.1 %collective-permute-done.11.h2a = bf16[2,2,2,128,128]{4,3,2,1,0:T(8,128)(2,1)S(1)} collective-permute-done((bf16[2,2,2,128,128]{4,3,2,1,0:T(8,128)(2,1)S(1)}, bf16[2,2,2,128,128]{4,3,2,1,0:T(8,128)(2,1)S(1)}, u32[]{:S(2)}, u32[]{:S(2)}) %collective-permute-start.11) | collective-permute-done | bytes 262176 | tf_op jit(solution)/shard_map/ppermute | solution.py:256
  57.1 5.6 %collective-permute-done.12.h2b = bf16[2,2,2,128,128]{4,3,2,1,0:T(8,128)(2,1)S(1)} collective-permute-done((bf16[2,2,2,128,128]{4,3,2,1,0:T(8,128)(2,1)S(1)}, bf16[2,2,2,128,128]{4,3,2,1,0:T(8,128)(2,1)S(1)}, u32[]{:S(2)}, u32[]{:S(2)}) %collective-permute-start.12) | collective-permute-done | bytes 262176 | tf_op jit(solution)/shard_map/ppermute | solution.py:256
  62.8 1.5 %collective-permute-done.14.h3b = bf16[2,2,2,128,128]{4,3,2,1,0:T(8,128)(2,1)S(1)} collective-permute-done((bf16[2,2,2,128,128]{4,3,2,1,0:T(8,128)(2,1)S(1)}, bf16[2,2,2,128,128]{4,3,2,1,0:T(8,128)(2,1)S(1)}, u32[]{:S(2)}, u32[]{:S(2)}) %collective-permute-start.14) | collective-permute-done | bytes 262176 | tf_op jit(solution)/shard_map/ppermute | solution.py:256
  64.3 0.9 %gram.1 = f32[16,16]{1,0:T(8,128)S(1)} custom-call(s32[1]{0:T(128)} %bitcast.me, f32[8,128]{1,0:T(8,128)S(1)} %gram_own.1.near, bf16[2,2,2,128,128]{4,3,2,1,0:T(8,128)(2,1)S(1)} %get-tuple-element.41.h0a, bf16[2,2,2,128,128]{4,3,2,1,0:T(8,128)(2,1)S(1)} %get-tuple-element.42.h0b, bf16[2,2,2,128,128]{4,3,2,1,0:T(8,128)(2,1)S(1)} %collective-permute-done.9.h1a, ...), custom_call_target="tpu_custom_call" | custom-call | tf_op jit(solution)/shard_map/gram/pallas_call | solution.py:335
  65.2 1.7 %collective-permute-start.15 = (f32[16,16]{1,0:T(8,128)S(1)}, f32[16,16]{1,0:T(8,128)S(1)}, u32[]{:S(2)}, u32[]{:S(2)}) collective-permute-start(f32[16,16]{1,0:T(8,128)S(1)} %gram.1), channel_id=1, source_target_pairs={{0,1},{1,0},{2,3},{3,2},{4,5},{5,4},{6,7},{7,6},{8,9},{9,8},{10,11... | collective-permute-start | bytes 3080 | tf_op jit(solution)/shard_map/ppermute | solution.py:256
  67.0 1.9 %collective-permute-done.15 = f32[16,16]{1,0:T(8,128)S(1)} collective-permute-done((f32[16,16]{1,0:T(8,128)S(1)}, f32[16,16]{1,0:T(8,128)S(1)}, u32[]{:S(2)}, u32[]{:S(2)}) %collective-permute-start.15) | collective-permute-done | bytes 1056 | tf_op jit(solution)/shard_map/ppermute | solution.py:256
  68.9 3.6 %collective-permute-done.16 = f32[16,16]{1,0:T(8,128)S(1)} collective-permute-done((f32[16,16]{1,0:T(8,128)S(1)}, f32[16,16]{1,0:T(8,128)S(1)}, u32[]{:S(2)}, u32[]{:S(2)}) %collective-permute-start.16) | collective-permute-done | bytes 1056 | tf_op jit(solution)/shard_map/ppermute | solution.py:256
  72.6 0.6 collective-permute-done.17.l2
  73.1 1.2 %collective-permute-start.18 = (f32[16,16]{1,0:T(8,128)S(1)}, f32[16,16]{1,0:T(8,128)S(1)}, u32[]{:S(2)}, u32[]{:S(2)}) collective-permute-start(f32[16,16]{1,0:T(8,128)S(1)} %add.10), channel_id=1, source_target_pairs={{0,4},{1,5},{2,6},{3,7},{4,0},{5,1},{6,2},{7,3},{8,12},{9,13},{10,... | collective-permute-start | bytes 3080 | tf_op jit(solution)/shard_map/ppermute | solution.py:256
  74.4 3.3 %collective-permute-done.18 = f32[16,16]{1,0:T(8,128)S(1)} collective-permute-done((f32[16,16]{1,0:T(8,128)S(1)}, f32[16,16]{1,0:T(8,128)S(1)}, u32[]{:S(2)}, u32[]{:S(2)}) %collective-permute-start.18) | collective-permute-done | bytes 1056 | tf_op jit(solution)/shard_map/ppermute | solution.py:256
  77.7 4.9 %final.1 = (f32[4,2,2,128,128]{4,3,2,1,0:T(8,128)}, f32[1,16]{1,0:T(1,128)}) custom-call(s32[1]{0:T(128)} %bitcast.me, f32[16,16]{1,0:T(8,128)S(1)} %add.11.gram, f32[4,2,2,128,128]{4,3,2,1,0:T(8,128)S(1)} %get-tuple-element.46.own, bf16[2,2,2,128,128]{4,3,2,1,0:T(8,128)(2,1)S(1)} %collective-permute-done.9.h1a, ...), custom_call_target="tpu_custom_call" | custom-call | tf_op jit(solution)/shard_map/final/pallas_call | solution.py:352
  (32 shorter events, 1.1 us)
Async XLA Ops:
  0.6 0.9 %copy-start.2 = (bf16[3,4,2,32,128]{4,3,2,1,0:T(8,128)(2,1)S(1)}, bf16[3,4,2,32,128]{4,3,2,1,0:T(8,128)(2,1)}, u32[]{:S(2)}) copy-start(bf16[3,4,2,32,128]{4,3,2,1,0:T(8,128)(2,1)} %background.3) | copy-start | bytes 589828
  1.6 9.7 %copy-start.3 = (bf16[3,4,2,32,128]{4,3,2,1,0:T(8,128)(2,1)S(1)}, bf16[3,4,2,32,128]{4,3,2,1,0:T(8,128)(2,1)}, u32[]{:S(2)}) copy-start(bf16[3,4,2,32,128]{4,3,2,1,0:T(8,128)(2,1)} %background.3) | copy-start | bytes 589828
  1.6 8.9 %collective-permute-start = (bf16[3,4,32,128]{3,2,1,0:T(8,128)(2,1)S(1)}, bf16[3,4,32,128]{3,2,1,0:T(8,128)(2,1)S(1)}, u32[]{:S(2)}, u32[]{:S(2)}) collective-permute-start(bf16[3,4,32,128]{3,2,1,0:T(8,128)(2,1)S(1)} %get-tuple-element.29), channel_id=1, source_target_pairs={{0,1},{1,2},{2,3},{3,4},{4,5},{5,6},{6,7},{7,0},{8,9},{9,10},{10,1... | collective-permute-start | bytes 294920 | tf_op jit(solution)/shard_map/ppermute | solution.py:252
  4.6 6.7 %collective-permute-start.1 = (bf16[3,4,32,128]{3,2,1,0:T(8,128)(2,1)S(1)}, bf16[3,4,32,128]{3,2,1,0:T(8,128)(2,1)S(1)}, u32[]{:S(2)}, u32[]{:S(2)}) collective-permute-start(bf16[3,4,32,128]{3,2,1,0:T(8,128)(2,1)S(1)} %get-tuple-element.30), channel_id=1, source_target_pairs={{0,7},{1,0},{2,1},{3,2},{4,3},{5,4},{6,5},{7,6},{8,15},{9,8},{10,9... | collective-permute-start | bytes 294920 | tf_op jit(solution)/shard_map/ppermute | solution.py:252
  7.7 1.2 %copy-start = (f32[4,2,2,128,128]{4,3,2,1,0:T(8,128)S(1)}, f32[4,2,2,128,128]{4,3,2,1,0:T(8,128)}, u32[]{:S(2)}) copy-start(f32[4,2,2,128,128]{4,3,2,1,0:T(8,128)} %own.3) | copy-start | bytes 3145732
  8.9 31.7 %copy-start.1 = (f32[4,2,2,128,128]{4,3,2,1,0:T(8,128)S(1)}, f32[4,2,2,128,128]{4,3,2,1,0:T(8,128)}, u32[]{:S(2)}) copy-start(f32[4,2,2,128,128]{4,3,2,1,0:T(8,128)} %own.3) | copy-start | bytes 3145732
  11.3 17.2 %collective-permute-start.4 = (bf16[12,4,32,128]{3,2,1,0:T(8,128)(2,1)S(1)}, bf16[12,4,32,128]{3,2,1,0:T(8,128)(2,1)S(1)}, u32[]{:S(2)}, u32[]{:S(2)}) collective-permute-start(bf16[12,4,32,128]{3,2,1,0:T(8,128)(2,1)S(1)} %pack.1.bg0), channel_id=1, source_target_pairs={{0,16},{8,24},{16,0},{24,8},{1,17},{9,25},{17,1},{25,9},{2,18},{10... | collective-permute-start | bytes 1179656 | tf_op jit(solution)/shard_map/ppermute | solution.py:256
  12.9 11.1 %collective-permute-start.5 = (bf16[4,2,128,128]{3,2,1,0:T(8,128)(2,1)S(1)}, bf16[4,2,128,128]{3,2,1,0:T(8,128)(2,1)S(1)}, u32[]{:S(2)}, u32[]{:S(2)}) collective-permute-start(bf16[4,2,128,128]{3,2,1,0:T(8,128)(2,1)S(1)} %get-tuple-element.34), channel_id=1, source_target_pairs={{0,2},{1,3},{2,4},{3,5},{4,6},{5,7},{6,0},{7,1},{8,10},{9,11},{10,... | collective-permute-start | bytes 786440 | tf_op jit(solution)/shard_map/ppermute | solution.py:252
  13.8 14.0 %collective-permute-start.6 = (bf16[4,2,128,128]{3,2,1,0:T(8,128)(2,1)S(1)}, bf16[4,2,128,128]{3,2,1,0:T(8,128)(2,1)S(1)}, u32[]{:S(2)}, u32[]{:S(2)}) collective-permute-start(bf16[4,2,128,128]{3,2,1,0:T(8,128)(2,1)S(1)} %get-tuple-element.35), channel_id=1, source_target_pairs={{0,6},{1,7},{2,0},{3,1},{4,2},{5,3},{6,4},{7,5},{8,14},{9,15},{10,... | collective-permute-start | bytes 786440 | tf_op jit(solution)/shard_map/ppermute | solution.py:252
  16.7 23.8 %collective-permute-start.3 = (bf16[2,4,2,128,128]{4,3,2,1,0:T(8,128)(2,1)}, bf16[2,4,2,128,128]{4,3,2,1,0:T(8,128)(2,1)S(1)}, u32[]{:S(2)}, u32[]{:S(2)}) collective-permute-start(bf16[2,4,2,128,128]{4,3,2,1,0:T(8,128)(2,1)} %get-tuple-element.31), channel_id=1, source_target_pairs={{0,7},{1,0},{2,1},{3,2},{4,3},{5,4},{6,5},{7,6},{8,15},{9,8},{10,9... | collective-permute-start | bytes 1572872 | tf_op jit(solution)/shard_map/ppermute | solution.py:252
  18.8 21.8 %collective-permute-start.2 = (bf16[2,4,2,128,128]{4,3,2,1,0:T(8,128)(2,1)}, bf16[2,4,2,128,128]{4,3,2,1,0:T(8,128)(2,1)S(1)}, u32[]{:S(2)}, u32[]{:S(2)}) collective-permute-start(bf16[2,4,2,128,128]{4,3,2,1,0:T(8,128)(2,1)} %get-tuple-element.31), channel_id=1, source_target_pairs={{0,1},{1,2},{2,3},{3,4},{4,5},{5,6},{6,7},{7,0},{8,9},{9,10},{10,1... | collective-permute-start | bytes 1572872 | tf_op jit(solution)/shard_map/ppermute | solution.py:252
  27.8 0.7 copy-start.4
  28.5 12.1 %collective-permute-start.7 = (bf16[12,4,32,128]{3,2,1,0:T(8,128)(2,1)S(1)}, bf16[12,4,32,128]{3,2,1,0:T(8,128)(2,1)S(1)}, u32[]{:S(2)}, u32[]{:S(2)}) collective-permute-start(bf16[12,4,32,128]{3,2,1,0:T(8,128)(2,1)S(1)} %pack.1.bg0), channel_id=1, source_target_pairs={{0,8},{8,0},{16,24},{24,16},{1,9},{9,1},{17,25},{25,17},{2,10},{10... | collective-permute-start | bytes 1179656 | tf_op jit(solution)/shard_map/ppermute | solution.py:256
  28.5 12.1 %collective-permute-start.8 = (bf16[12,4,32,128]{3,2,1,0:T(8,128)(2,1)S(1)}, bf16[12,4,32,128]{3,2,1,0:T(8,128)(2,1)}, u32[]{:S(2)}, u32[]{:S(2)}) collective-permute-start(bf16[12,4,32,128]{3,2,1,0:T(8,128)(2,1)S(1)} %collective-permute-done.4.bg2), channel_id=1, source_target_pairs={{0,8},{8,0},{16,24},{24,16},{1,9},{9,1},{17,25},{25,17},{2,10},{10... | collective-permute-start | bytes 1179656 | tf_op jit(solution)/shard_map/ppermute | solution.py:256
  40.6 1.0 %copy-start.5 = (bf16[4,2,128,128]{3,2,1,0:T(8,128)(2,1)S(1)}, bf16[4,2,128,128]{3,2,1,0:T(8,128)(2,1)}, u32[]{:S(2)}) copy-start(bf16[4,2,128,128]{3,2,1,0:T(8,128)(2,1)} %copy-done.4) | copy-start | bytes 786436
  47.4 2.6 %collective-permute-start.9 = (bf16[2,2,2,128,128]{4,3,2,1,0:T(8,128)(2,1)S(1)}, bf16[2,2,2,128,128]{4,3,2,1,0:T(8,128)(2,1)S(1)}, u32[]{:S(2)}, u32[]{:S(2)}) collective-permute-start(bf16[2,2,2,128,128]{4,3,2,1,0:T(8,128)(2,1)S(1)} %get-tuple-element.41.h0a), channel_id=1, source_target_pairs={{0,8},{8,0},{16,24},{24,16},{1,9},{9,1},{17,25},{25,17},{2,10},{10... | collective-permute-start | bytes 786440 | tf_op jit(solution)/shard_map/ppermute | solution.py:256
  47.5 2.5 %collective-permute-start.10 = (bf16[2,2,2,128,128]{4,3,2,1,0:T(8,128)(2,1)S(1)}, bf16[2,2,2,128,128]{4,3,2,1,0:T(8,128)(2,1)S(1)}, u32[]{:S(2)}, u32[]{:S(2)}) collective-permute-start(bf16[2,2,2,128,128]{4,3,2,1,0:T(8,128)(2,1)S(1)} %get-tuple-element.42.h0b), channel_id=1, source_target_pairs={{0,8},{8,0},{16,24},{24,16},{1,9},{9,1},{17,25},{25,17},{2,10},{10... | collective-permute-start | bytes 786440 | tf_op jit(solution)/shard_map/ppermute | solution.py:256
  48.0 9.2 %collective-permute-start.11 = (bf16[2,2,2,128,128]{4,3,2,1,0:T(8,128)(2,1)S(1)}, bf16[2,2,2,128,128]{4,3,2,1,0:T(8,128)(2,1)S(1)}, u32[]{:S(2)}, u32[]{:S(2)}) collective-permute-start(bf16[2,2,2,128,128]{4,3,2,1,0:T(8,128)(2,1)S(1)} %get-tuple-element.41.h0a), channel_id=1, source_target_pairs={{0,16},{8,24},{16,0},{24,8},{1,17},{9,25},{17,1},{25,9},{2,18},{10... | collective-permute-start | bytes 786440 | tf_op jit(solution)/shard_map/ppermute | solution.py:256
  48.5 14.3 %collective-permute-start.12 = (bf16[2,2,2,128,128]{4,3,2,1,0:T(8,128)(2,1)S(1)}, bf16[2,2,2,128,128]{4,3,2,1,0:T(8,128)(2,1)S(1)}, u32[]{:S(2)}, u32[]{:S(2)}) collective-permute-start(bf16[2,2,2,128,128]{4,3,2,1,0:T(8,128)(2,1)S(1)} %get-tuple-element.42.h0b), channel_id=1, source_target_pairs={{0,16},{8,24},{16,0},{24,8},{1,17},{9,25},{17,1},{25,9},{2,18},{10... | collective-permute-start | bytes 786440 | tf_op jit(solution)/shard_map/ppermute | solution.py:256
  50.5 22.6 %collective-permute-start.17 = (bf16[4,2,2,128,128]{4,3,2,1,0:T(8,128)(2,1)S(1)}, bf16[4,2,2,128,128]{4,3,2,1,0:T(8,128)(2,1)S(1)}, u32[]{:S(2)}, u32[]{:S(2)}) collective-permute-start(bf16[4,2,2,128,128]{4,3,2,1,0:T(8,128)(2,1)S(1)} %get-tuple-element.44), channel_id=1, source_target_pairs={{0,16},{8,24},{16,0},{24,8},{1,17},{9,25},{17,1},{25,9},{2,18},{10... | collective-permute-start | bytes 1572872 | tf_op jit(solution)/shard_map/ppermute | solution.py:256
  57.1 5.6 %collective-permute-start.13 = (bf16[2,2,2,128,128]{4,3,2,1,0:T(8,128)(2,1)S(1)}, bf16[2,2,2,128,128]{4,3,2,1,0:T(8,128)(2,1)S(1)}, u32[]{:S(2)}, u32[]{:S(2)}) collective-permute-start(bf16[2,2,2,128,128]{4,3,2,1,0:T(8,128)(2,1)S(1)} %collective-permute-done.11.h2a), channel_id=1, source_target_pairs={{0,8},{8,0},{16,24},{24,16},{1,9},{9,1},{17,25},{25,17},{2,10},{10... | collective-permute-start | bytes 786440 | tf_op jit(solution)/shard_map/ppermute | solution.py:256
  62.8 1.5 %collective-permute-start.14 = (bf16[2,2,2,128,128]{4,3,2,1,0:T(8,128)(2,1)S(1)}, bf16[2,2,2,128,128]{4,3,2,1,0:T(8,128)(2,1)S(1)}, u32[]{:S(2)}, u32[]{:S(2)}) collective-permute-start(bf16[2,2,2,128,128]{4,3,2,1,0:T(8,128)(2,1)S(1)} %collective-permute-done.12.h2b), channel_id=1, source_target_pairs={{0,8},{8,0},{16,24},{24,16},{1,9},{9,1},{17,25},{25,17},{2,10},{10... | collective-permute-start | bytes 786440 | tf_op jit(solution)/shard_map/ppermute | solution.py:256
  65.2 3.7 %collective-permute-start.15 = (f32[16,16]{1,0:T(8,128)S(1)}, f32[16,16]{1,0:T(8,128)S(1)}, u32[]{:S(2)}, u32[]{:S(2)}) collective-permute-start(f32[16,16]{1,0:T(8,128)S(1)} %gram.1), channel_id=1, source_target_pairs={{0,1},{1,0},{2,3},{3,2},{4,5},{5,4},{6,7},{7,6},{8,9},{9,8},{10,11... | collective-permute-start | bytes 3080 | tf_op jit(solution)/shard_map/ppermute | solution.py:256
  68.9 3.7 %collective-permute-start.16 = (f32[16,16]{1,0:T(8,128)S(1)}, f32[16,16]{1,0:T(8,128)S(1)}, u32[]{:S(2)}, u32[]{:S(2)}) collective-permute-start(f32[16,16]{1,0:T(8,128)S(1)} %add.9), channel_id=1, source_target_pairs={{0,2},{1,3},{2,0},{3,1},{4,6},{5,7},{6,4},{7,5},{8,10},{9,11},{10,... | collective-permute-start | bytes 3080 | tf_op jit(solution)/shard_map/ppermute | solution.py:256
  68.9 8.8 %collective-permute-start.19 = (bf16[4,2,2,128,128]{4,3,2,1,0:T(8,128)(2,1)S(1)}, bf16[4,2,2,128,128]{4,3,2,1,0:T(8,128)(2,1)S(1)}, u32[]{:S(2)}, u32[]{:S(2)}) collective-permute-start(bf16[4,2,2,128,128]{4,3,2,1,0:T(8,128)(2,1)S(1)} %get-tuple-element.44), channel_id=1, source_target_pairs={{0,8},{8,0},{16,24},{24,16},{1,9},{9,1},{17,25},{25,17},{2,10},{10... | collective-permute-start | bytes 1572872 | tf_op jit(solution)/shard_map/ppermute | solution.py:256
  73.1 4.6 %collective-permute-start.20 = (bf16[4,2,2,128,128]{4,3,2,1,0:T(8,128)(2,1)S(1)}, bf16[4,2,2,128,128]{4,3,2,1,0:T(8,128)(2,1)S(1)}, u32[]{:S(2)}, u32[]{:S(2)}) collective-permute-start(bf16[4,2,2,128,128]{4,3,2,1,0:T(8,128)(2,1)S(1)} %collective-permute-done.17.l2), channel_id=1, source_target_pairs={{0,8},{8,0},{16,24},{24,16},{1,9},{9,1},{17,25},{25,17},{2,10},{10... | collective-permute-start | bytes 1572872 | tf_op jit(solution)/shard_map/ppermute | solution.py:256
  73.1 4.6 %collective-permute-start.18 = (f32[16,16]{1,0:T(8,128)S(1)}, f32[16,16]{1,0:T(8,128)S(1)}, u32[]{:S(2)}, u32[]{:S(2)}) collective-permute-start(f32[16,16]{1,0:T(8,128)S(1)} %add.10), channel_id=1, source_target_pairs={{0,4},{1,5},{2,6},{3,7},{4,0},{5,1},{6,2},{7,3},{8,12},{9,13},{10,... | collective-permute-start | bytes 3080 | tf_op jit(solution)/shard_map/ppermute | solution.py:256

commit v6 on v5

--- a/solution.py
+++ b/solution.py
@@ -197,31 +197,32 @@
     vectors = own.shape[0]
     count = gram.shape[0]
     position = me[0]
-    row = lax.broadcasted_iota(jnp.int32, (count, 2 * count), 0)
-    lane = lax.broadcasted_iota(jnp.int32, (count, 2 * count), 1)
-    unit = lane - count
+    levels = own.shape[4]
+    scaled = gram[...] * scale
+    left = [jnp.broadcast_to(scaled[:, i : i + 1], (count, levels)) for i in range(count)]
+    unit = lax.broadcasted_iota(jnp.int32, (count, levels), 0)
     column = ((unit // vectors) ^ position) * vectors + unit % vectors
-    eye = jnp.where((lane >= count) & (row == column), 1.0, 0.0)
-    table = jnp.concatenate([gram[...] * scale, jnp.zeros((count, count), jnp.float32)], 1) + eye
-    pivots = jnp.zeros((1, count), jnp.float32)
-    wide = lax.broadcasted_iota(jnp.int32, (1, count), 1)
+    right = [jnp.where(column == i, 1.0, 0.0) for i in range(count)]
+    wide = lax.broadcasted_iota(jnp.int32, (1, levels), 1)
+    pivots = jnp.ones((1, levels), jnp.float32)
     for k in range(count):
-        pivot = table[k : k + 1, k : k + 1]
+        pivot = left[k][k : k + 1, :]
         pivots = jnp.where(wide == k, pivot, pivots)
-        root = lax.rsqrt(pivot)
-        root = root * (1.5 - 0.5 * pivot * root * root)
-        scaled = table[k : k + 1, :] * root
-        below = jnp.where(row[:, :1] > k, table[:, k : k + 1] * root, 0.0)
-        table = jnp.where(row == k, scaled, table - below * scaled)
-    growth[...] = 0.5 * jnp.log(pivots)
-    inv[...] = table
+        turn = 1.0 / pivot
+        line, unit_line = left[k] * turn, right[k] * turn
+        for i in range(k + 1, count):
+            factor = left[i][k : k + 1, :]
+            left[i] = left[i] - factor * line
+            right[i] = right[i] - factor * unit_line
+        inv[k] = right[k] / jnp.sqrt(pivot)
+    growth[...] = (0.5 * jnp.log(pivots))[:, :count]
     for first in range(0, vectors, 2):
         weights = []
         for i in range(first, first + 2):
-            line = inv[pl.ds(position * vectors + i, 1), :]
+            line = inv[position * vectors + i]
             weights.append(
                 [
-                    jnp.broadcast_to(line[:, count + j : count + j + 1], (CHUNK, own.shape[4]))
+                    jnp.broadcast_to(line[j : j + 1, :], (CHUNK, levels))
                     for j in range(count)
                 ]
             )
@@ -357,7 +358,7 @@
         ],
         in_specs=[SM] + [VM] * 11,
         out_specs=[VM, VM],
-        scratch_shapes=[pltpu.VMEM((count, 2 * count), jnp.float32)],
+        scratch_shapes=[pltpu.VMEM((count, count, levels), jnp.float32)],
         compiler_params=SMALL,
         name="final",
     )(me, gram, adv, *high[2:], l1, l2, l3)

time: 82.8 us -> 81.5 us (0.984)
  Pallas kernels: 13 us -> 11.7 us
    pallas_call x1, Pallas kernels: 4.86 us -> 3.56 us  [on_device(): pl.pallas_call(functools.partial(final_kernel, 1.0 / cells), out_shape=[j...]
where the time goes in v6:
time: 81.5 us; the launch traced here: 81.3 us
  waiting for transfers between devices  44.8 us (55%)
  starting transfers between devices  20.2 us (25%)
  Pallas kernels  11.7 us (14%)
  local copies, waits for them, and re-layouts  3.79 us (5%)
    ppermute x15, waiting for transfers between devices, swap(): lax.ppermute(value, axis, [(i, i ^ mask) for i in range(lax.axis_size(axi...  22.7 us
    ppermute x6, waiting for transfers between devices, shift(): lax.ppermute(value, axis, [(i, (i + step) % count) for i in range(count)])  22.1 us
    ppermute x6, starting transfers between devices, shift(): lax.ppermute(value, axis, [(i, (i + step) % count) for i in range(count)])  11.9 us
    ppermute x15, starting transfers between devices, swap(): lax.ppermute(value, axis, [(i, i ^ mask) for i in range(lax.axis_size(axi...  8.23 us
    pallas_call x1, Pallas kernels, on_device(): pl.pallas_call(advance_kernel, out_shape=[jax.ShapeDtypeStruct(tangents.s...  5.87 us
    unnamed x12, local copies, waits for them, and re-layouts  3.79 us
    pallas_call x1, Pallas kernels, on_device(): pl.pallas_call(functools.partial(final_kernel, 1.0 / cells), out_shape=[j...  3.56 us
  transfers between devices with their start and end apart: 21, of which 12 were waited for; matrix products, arithmetic and copies ran while one was open for 0% of the time, Pallas kernels for 3%

profile of v6, /device:TPU:0, one launch (start us, length us, event | category | flops | bytes accessed | tf_op | source)
XLA Modules:
  0.0 81.3 jit_solution(11669828637645112250)
XLA Ops:
  0.6 0.9 %copy-done.2 = bf16[3,4,2,32,128]{4,3,2,1,0:T(8,128)(2,1)S(1)} copy-done((bf16[3,4,2,32,128]{4,3,2,1,0:T(8,128)(2,1)S(1)}, bf16[3,4,2,32,128]{4,3,2,1,0:T(8,128)(2,1)}, u32[]{:S(2)}) %copy-start.2) | copy-done | bytes 196632
  1.6 3.0 %collective-permute-start = (bf16[3,4,32,128]{3,2,1,0:T(8,128)(2,1)S(1)}, bf16[3,4,32,128]{3,2,1,0:T(8,128)(2,1)S(1)}, u32[]{:S(2)}, u32[]{:S(2)}) collective-permute-start(bf16[3,4,32,128]{3,2,1,0:T(8,128)(2,1)S(1)} %get-tuple-element.29), channel_id=1, source_target_pairs={{0,1},{1,2},{2,3},{3,4},{4,5},{5,6},{6,7},{7,0},{8,9},{9,10},{10,1... | collective-permute-start | bytes 294920 | tf_op jit(solution)/shard_map/ppermute | solution.py:253
  4.6 3.1 %collective-permute-start.1 = (bf16[3,4,32,128]{3,2,1,0:T(8,128)(2,1)S(1)}, bf16[3,4,32,128]{3,2,1,0:T(8,128)(2,1)S(1)}, u32[]{:S(2)}, u32[]{:S(2)}) collective-permute-start(bf16[3,4,32,128]{3,2,1,0:T(8,128)(2,1)S(1)} %get-tuple-element.30), channel_id=1, source_target_pairs={{0,7},{1,0},{2,1},{3,2},{4,3},{5,4},{6,5},{7,6},{8,15},{9,8},{10,9... | collective-permute-start | bytes 294920 | tf_op jit(solution)/shard_map/ppermute | solution.py:253
  7.7 1.2 %copy-done = f32[4,2,2,128,128]{4,3,2,1,0:T(8,128)S(1)} copy-done((f32[4,2,2,128,128]{4,3,2,1,0:T(8,128)S(1)}, f32[4,2,2,128,128]{4,3,2,1,0:T(8,128)}, u32[]{:S(2)}) %copy-start) | copy-done | bytes 1048600
  8.9 0.9 %prep.1 = (bf16[2,4,2,128,128]{4,3,2,1,0:T(8,128)(2,1)}, bf16[4,2,128,128]{3,2,1,0:T(8,128)(2,1)S(1)}, bf16[4,2,128,128]{3,2,1,0:T(8,128)(2,1)S(1)}) custom-call(f32[4,2,2,128,128]{4,3,2,1,0:T(8,128)S(1)} %copy-done), custom_call_target="tpu_custom_call" | custom-call | tf_op jit(solution)/shard_map/prep/pallas_call | solution.py:267
  9.8 0.7 collective-permute-done.up
  10.5 0.8 collective-permute-done.1.dn
  11.3 1.6 %collective-permute-start.4 = (bf16[12,4,32,128]{3,2,1,0:T(8,128)(2,1)S(1)}, bf16[12,4,32,128]{3,2,1,0:T(8,128)(2,1)S(1)}, u32[]{:S(2)}, u32[]{:S(2)}) collective-permute-start(bf16[12,4,32,128]{3,2,1,0:T(8,128)(2,1)S(1)} %pack.1.bg0), channel_id=1, source_target_pairs={{0,16},{8,24},{16,0},{24,8},{1,17},{9,25},{17,1},{25,9},{2,18},{10... | collective-permute-start | bytes 1179656 | tf_op jit(solution)/shard_map/ppermute | solution.py:257
  12.9 0.9 %collective-permute-start.5 = (bf16[4,2,128,128]{3,2,1,0:T(8,128)(2,1)S(1)}, bf16[4,2,128,128]{3,2,1,0:T(8,128)(2,1)S(1)}, u32[]{:S(2)}, u32[]{:S(2)}) collective-permute-start(bf16[4,2,128,128]{3,2,1,0:T(8,128)(2,1)S(1)} %get-tuple-element.34), channel_id=1, source_target_pairs={{0,2},{1,3},{2,4},{3,5},{4,6},{5,7},{6,0},{7,1},{8,10},{9,11},{10,... | collective-permute-start | bytes 786440 | tf_op jit(solution)/shard_map/ppermute | solution.py:253
  13.8 2.9 %collective-permute-start.6 = (bf16[4,2,128,128]{3,2,1,0:T(8,128)(2,1)S(1)}, bf16[4,2,128,128]{3,2,1,0:T(8,128)(2,1)S(1)}, u32[]{:S(2)}, u32[]{:S(2)}) collective-permute-start(bf16[4,2,128,128]{3,2,1,0:T(8,128)(2,1)S(1)} %get-tuple-element.35), channel_id=1, source_target_pairs={{0,6},{1,7},{2,0},{3,1},{4,2},{5,3},{6,4},{7,5},{8,14},{9,15},{10,... | collective-permute-start | bytes 786440 | tf_op jit(solution)/shard_map/ppermute | solution.py:253
  16.7 2.0 %collective-permute-start.3 = (bf16[2,4,2,128,128]{4,3,2,1,0:T(8,128)(2,1)}, bf16[2,4,2,128,128]{4,3,2,1,0:T(8,128)(2,1)S(1)}, u32[]{:S(2)}, u32[]{:S(2)}) collective-permute-start(bf16[2,4,2,128,128]{4,3,2,1,0:T(8,128)(2,1)} %get-tuple-element.31), channel_id=1, source_target_pairs={{0,7},{1,0},{2,1},{3,2},{4,3},{5,4},{6,5},{7,6},{8,15},{9,8},{10,9... | collective-permute-start | bytes 1572872 | tf_op jit(solution)/shard_map/ppermute | solution.py:253
  18.8 5.2 %collective-permute-done.5.up2 = bf16[4,2,128,128]{3,2,1,0:T(8,128)(2,1)S(1)} collective-permute-done((bf16[4,2,128,128]{3,2,1,0:T(8,128)(2,1)S(1)}, bf16[4,2,128,128]{3,2,1,0:T(8,128)(2,1)S(1)}, u32[]{:S(2)}, u32[]{:S(2)}) %collective-permute-start.5) | collective-permute-done | bytes 262176 | tf_op jit(solution)/shard_map/ppermute | solution.py:253
  24.0 3.8 %collective-permute-done.6.dn2 = bf16[4,2,128,128]{3,2,1,0:T(8,128)(2,1)S(1)} collective-permute-done((bf16[4,2,128,128]{3,2,1,0:T(8,128)(2,1)S(1)}, bf16[4,2,128,128]{3,2,1,0:T(8,128)(2,1)S(1)}, u32[]{:S(2)}, u32[]{:S(2)}) %collective-permute-start.6) | collective-permute-done | bytes 262176 | tf_op jit(solution)/shard_map/ppermute | solution.py:253
  27.8 0.7 copy-done.4
  28.5 0.5 collective-permute-start.8
  29.0 11.5 %collective-permute-done.3.dn1 = bf16[2,4,2,128,128]{4,3,2,1,0:T(8,128)(2,1)S(1)} collective-permute-done((bf16[2,4,2,128,128]{4,3,2,1,0:T(8,128)(2,1)}, bf16[2,4,2,128,128]{4,3,2,1,0:T(8,128)(2,1)S(1)}, u32[]{:S(2)}, u32[]{:S(2)}) %collective-permute-start.3) | collective-permute-done | bytes 524320 | tf_op jit(solution)/shard_map/ppermute | solution.py:253
  40.6 0.9 %copy-done.5 = bf16[4,2,128,128]{3,2,1,0:T(8,128)(2,1)S(1)} copy-done((bf16[4,2,128,128]{3,2,1,0:T(8,128)(2,1)S(1)}, bf16[4,2,128,128]{3,2,1,0:T(8,128)(2,1)}, u32[]{:S(2)}) %copy-start.5) | copy-done | bytes 262168
  41.5 5.9 %advance.1 = (f32[4,2,2,128,128]{4,3,2,1,0:T(8,128)S(1)}, bf16[2,2,2,128,128]{4,3,2,1,0:T(8,128)(2,1)S(1)}, bf16[2,2,2,128,128]{4,3,2,1,0:T(8,128)(2,1)S(1)}, bf16[4,2,2,128,128]{4,3,2,1,0:T(8,128)(2,1)S(1)}) custom-call(s32[1]{0:T(128)} %bitcast.me, f32[4,2,2,128,128]{4,3,2,1,0:T(8,128)S(1)} %copy-done.1, ...), custom_call_target="tpu_custom_call" | custom-call | tf_op jit(solution)/shard_map/advance/pallas_call | solution.py:306
  48.0 0.5 collective-permute-start.11
  48.5 1.5 %collective-permute-start.12 = (bf16[2,2,2,128,128]{4,3,2,1,0:T(8,128)(2,1)S(1)}, bf16[2,2,2,128,128]{4,3,2,1,0:T(8,128)(2,1)S(1)}, u32[]{:S(2)}, u32[]{:S(2)}) collective-permute-start(bf16[2,2,2,128,128]{4,3,2,1,0:T(8,128)(2,1)S(1)} %get-tuple-element.42.h0b), channel_id=1, source_target_pairs={{0,16},{8,24},{16,0},{24,8},{1,17},{9,25},{17,1},{25,9},{2,18},{10... | collective-permute-start | bytes 786440 | tf_op jit(solution)/shard_map/ppermute | solution.py:257
  50.5 0.6 collective-permute-start.17
  51.0 6.1 %collective-permute-done.11.h2a = bf16[2,2,2,128,128]{4,3,2,1,0:T(8,128)(2,1)S(1)} collective-permute-done((bf16[2,2,2,128,128]{4,3,2,1,0:T(8,128)(2,1)S(1)}, bf16[2,2,2,128,128]{4,3,2,1,0:T(8,128)(2,1)S(1)}, u32[]{:S(2)}, u32[]{:S(2)}) %collective-permute-start.11) | collective-permute-done | bytes 262176 | tf_op jit(solution)/shard_map/ppermute | solution.py:257
  57.1 5.6 %collective-permute-done.12.h2b = bf16[2,2,2,128,128]{4,3,2,1,0:T(8,128)(2,1)S(1)} collective-permute-done((bf16[2,2,2,128,128]{4,3,2,1,0:T(8,128)(2,1)S(1)}, bf16[2,2,2,128,128]{4,3,2,1,0:T(8,128)(2,1)S(1)}, u32[]{:S(2)}, u32[]{:S(2)}) %collective-permute-start.12) | collective-permute-done | bytes 262176 | tf_op jit(solution)/shard_map/ppermute | solution.py:257
  62.8 1.5 %collective-permute-done.14.h3b = bf16[2,2,2,128,128]{4,3,2,1,0:T(8,128)(2,1)S(1)} collective-permute-done((bf16[2,2,2,128,128]{4,3,2,1,0:T(8,128)(2,1)S(1)}, bf16[2,2,2,128,128]{4,3,2,1,0:T(8,128)(2,1)S(1)}, u32[]{:S(2)}, u32[]{:S(2)}) %collective-permute-start.14) | collective-permute-done | bytes 262176 | tf_op jit(solution)/shard_map/ppermute | solution.py:257
  64.3 0.9 %gram.1 = f32[16,16]{1,0:T(8,128)S(1)} custom-call(s32[1]{0:T(128)} %bitcast.me, f32[8,128]{1,0:T(8,128)S(1)} %gram_own.1.near, bf16[2,2,2,128,128]{4,3,2,1,0:T(8,128)(2,1)S(1)} %get-tuple-element.41.h0a, bf16[2,2,2,128,128]{4,3,2,1,0:T(8,128)(2,1)S(1)} %get-tuple-element.42.h0b, bf16[2,2,2,128,128]{4,3,2,1,0:T(8,128)(2,1)S(1)} %collective-permute-done.9.h1a, ...), custom_call_target="tpu_custom_call" | custom-call | tf_op jit(solution)/shard_map/gram/pallas_call | solution.py:336
  65.2 1.7 %collective-permute-start.15 = (f32[16,16]{1,0:T(8,128)S(1)}, f32[16,16]{1,0:T(8,128)S(1)}, u32[]{:S(2)}, u32[]{:S(2)}) collective-permute-start(f32[16,16]{1,0:T(8,128)S(1)} %gram.1), channel_id=1, source_target_pairs={{0,1},{1,0},{2,3},{3,2},{4,5},{5,4},{6,7},{7,6},{8,9},{9,8},{10,11... | collective-permute-start | bytes 3080 | tf_op jit(solution)/shard_map/ppermute | solution.py:257
  67.0 1.9 %collective-permute-done.15 = f32[16,16]{1,0:T(8,128)S(1)} collective-permute-done((f32[16,16]{1,0:T(8,128)S(1)}, f32[16,16]{1,0:T(8,128)S(1)}, u32[]{:S(2)}, u32[]{:S(2)}) %collective-permute-start.15) | collective-permute-done | bytes 1056 | tf_op jit(solution)/shard_map/ppermute | solution.py:257
  68.9 3.6 %collective-permute-done.16 = f32[16,16]{1,0:T(8,128)S(1)} collective-permute-done((f32[16,16]{1,0:T(8,128)S(1)}, f32[16,16]{1,0:T(8,128)S(1)}, u32[]{:S(2)}, u32[]{:S(2)}) %collective-permute-start.16) | collective-permute-done | bytes 1056 | tf_op jit(solution)/shard_map/ppermute | solution.py:257
  72.6 0.6 collective-permute-done.17.l2
  73.1 1.2 %collective-permute-start.18 = (f32[16,16]{1,0:T(8,128)S(1)}, f32[16,16]{1,0:T(8,128)S(1)}, u32[]{:S(2)}, u32[]{:S(2)}) collective-permute-start(f32[16,16]{1,0:T(8,128)S(1)} %add.10), channel_id=1, source_target_pairs={{0,4},{1,5},{2,6},{3,7},{4,0},{5,1},{6,2},{7,3},{8,12},{9,13},{10,... | collective-permute-start | bytes 3080 | tf_op jit(solution)/shard_map/ppermute | solution.py:257
  74.4 3.3 %collective-permute-done.18 = f32[16,16]{1,0:T(8,128)S(1)} collective-permute-done((f32[16,16]{1,0:T(8,128)S(1)}, f32[16,16]{1,0:T(8,128)S(1)}, u32[]{:S(2)}, u32[]{:S(2)}) %collective-permute-start.18) | collective-permute-done | bytes 1056 | tf_op jit(solution)/shard_map/ppermute | solution.py:257
  77.7 3.6 %final.1 = (f32[4,2,2,128,128]{4,3,2,1,0:T(8,128)}, f32[1,16]{1,0:T(1,128)}) custom-call(s32[1]{0:T(128)} %bitcast.me, f32[16,16]{1,0:T(8,128)S(1)} %add.11.gram, f32[4,2,2,128,128]{4,3,2,1,0:T(8,128)S(1)} %get-tuple-element.46.own, bf16[2,2,2,128,128]{4,3,2,1,0:T(8,128)(2,1)S(1)} %collective-permute-done.9.h1a, ...), custom_call_target="tpu_custom_call" | custom-call | tf_op jit(solution)/shard_map/final/pallas_call | solution.py:353
  (32 shorter events, 1.1 us)
Async XLA Ops:
  0.6 0.9 %copy-start.2 = (bf16[3,4,2,32,128]{4,3,2,1,0:T(8,128)(2,1)S(1)}, bf16[3,4,2,32,128]{4,3,2,1,0:T(8,128)(2,1)}, u32[]{:S(2)}) copy-start(bf16[3,4,2,32,128]{4,3,2,1,0:T(8,128)(2,1)} %background.3) | copy-start | bytes 589828
  1.6 9.7 %copy-start.3 = (bf16[3,4,2,32,128]{4,3,2,1,0:T(8,128)(2,1)S(1)}, bf16[3,4,2,32,128]{4,3,2,1,0:T(8,128)(2,1)}, u32[]{:S(2)}) copy-start(bf16[3,4,2,32,128]{4,3,2,1,0:T(8,128)(2,1)} %background.3) | copy-start | bytes 589828
  1.6 8.9 %collective-permute-start = (bf16[3,4,32,128]{3,2,1,0:T(8,128)(2,1)S(1)}, bf16[3,4,32,128]{3,2,1,0:T(8,128)(2,1)S(1)}, u32[]{:S(2)}, u32[]{:S(2)}) collective-permute-start(bf16[3,4,32,128]{3,2,1,0:T(8,128)(2,1)S(1)} %get-tuple-element.29), channel_id=1, source_target_pairs={{0,1},{1,2},{2,3},{3,4},{4,5},{5,6},{6,7},{7,0},{8,9},{9,10},{10,1... | collective-permute-start | bytes 294920 | tf_op jit(solution)/shard_map/ppermute | solution.py:253
  4.6 6.7 %collective-permute-start.1 = (bf16[3,4,32,128]{3,2,1,0:T(8,128)(2,1)S(1)}, bf16[3,4,32,128]{3,2,1,0:T(8,128)(2,1)S(1)}, u32[]{:S(2)}, u32[]{:S(2)}) collective-permute-start(bf16[3,4,32,128]{3,2,1,0:T(8,128)(2,1)S(1)} %get-tuple-element.30), channel_id=1, source_target_pairs={{0,7},{1,0},{2,1},{3,2},{4,3},{5,4},{6,5},{7,6},{8,15},{9,8},{10,9... | collective-permute-start | bytes 294920 | tf_op jit(solution)/shard_map/ppermute | solution.py:253
  7.7 1.2 %copy-start = (f32[4,2,2,128,128]{4,3,2,1,0:T(8,128)S(1)}, f32[4,2,2,128,128]{4,3,2,1,0:T(8,128)}, u32[]{:S(2)}) copy-start(f32[4,2,2,128,128]{4,3,2,1,0:T(8,128)} %own.3) | copy-start | bytes 3145732
  8.9 31.7 %copy-start.1 = (f32[4,2,2,128,128]{4,3,2,1,0:T(8,128)S(1)}, f32[4,2,2,128,128]{4,3,2,1,0:T(8,128)}, u32[]{:S(2)}) copy-start(f32[4,2,2,128,128]{4,3,2,1,0:T(8,128)} %own.3) | copy-start | bytes 3145732
  11.3 17.2 %collective-permute-start.4 = (bf16[12,4,32,128]{3,2,1,0:T(8,128)(2,1)S(1)}, bf16[12,4,32,128]{3,2,1,0:T(8,128)(2,1)S(1)}, u32[]{:S(2)}, u32[]{:S(2)}) collective-permute-start(bf16[12,4,32,128]{3,2,1,0:T(8,128)(2,1)S(1)} %pack.1.bg0), channel_id=1, source_target_pairs={{0,16},{8,24},{16,0},{24,8},{1,17},{9,25},{17,1},{25,9},{2,18},{10... | collective-permute-start | bytes 1179656 | tf_op jit(solution)/shard_map/ppermute | solution.py:257
  12.9 11.1 %collective-permute-start.5 = (bf16[4,2,128,128]{3,2,1,0:T(8,128)(2,1)S(1)}, bf16[4,2,128,128]{3,2,1,0:T(8,128)(2,1)S(1)}, u32[]{:S(2)}, u32[]{:S(2)}) collective-permute-start(bf16[4,2,128,128]{3,2,1,0:T(8,128)(2,1)S(1)} %get-tuple-element.34), channel_id=1, source_target_pairs={{0,2},{1,3},{2,4},{3,5},{4,6},{5,7},{6,0},{7,1},{8,10},{9,11},{10,... | collective-permute-start | bytes 786440 | tf_op jit(solution)/shard_map/ppermute | solution.py:253
  13.8 14.0 %collective-permute-start.6 = (bf16[4,2,128,128]{3,2,1,0:T(8,128)(2,1)S(1)}, bf16[4,2,128,128]{3,2,1,0:T(8,128)(2,1)S(1)}, u32[]{:S(2)}, u32[]{:S(2)}) collective-permute-start(bf16[4,2,128,128]{3,2,1,0:T(8,128)(2,1)S(1)} %get-tuple-element.35), channel_id=1, source_target_pairs={{0,6},{1,7},{2,0},{3,1},{4,2},{5,3},{6,4},{7,5},{8,14},{9,15},{10,... | collective-permute-start | bytes 786440 | tf_op jit(solution)/shard_map/ppermute | solution.py:253
  16.7 23.8 %collective-permute-start.3 = (bf16[2,4,2,128,128]{4,3,2,1,0:T(8,128)(2,1)}, bf16[2,4,2,128,128]{4,3,2,1,0:T(8,128)(2,1)S(1)}, u32[]{:S(2)}, u32[]{:S(2)}) collective-permute-start(bf16[2,4,2,128,128]{4,3,2,1,0:T(8,128)(2,1)} %get-tuple-element.31), channel_id=1, source_target_pairs={{0,7},{1,0},{2,1},{3,2},{4,3},{5,4},{6,5},{7,6},{8,15},{9,8},{10,9... | collective-permute-start | bytes 1572872 | tf_op jit(solution)/shard_map/ppermute | solution.py:253
  18.8 21.8 %collective-permute-start.2 = (bf16[2,4,2,128,128]{4,3,2,1,0:T(8,128)(2,1)}, bf16[2,4,2,128,128]{4,3,2,1,0:T(8,128)(2,1)S(1)}, u32[]{:S(2)}, u32[]{:S(2)}) collective-permute-start(bf16[2,4,2,128,128]{4,3,2,1,0:T(8,128)(2,1)} %get-tuple-element.31), channel_id=1, source_target_pairs={{0,1},{1,2},{2,3},{3,4},{4,5},{5,6},{6,7},{7,0},{8,9},{9,10},{10,1... | collective-permute-start | bytes 1572872 | tf_op jit(solution)/shard_map/ppermute | solution.py:253
  27.8 0.7 copy-start.4
  28.5 12.1 %collective-permute-start.7 = (bf16[12,4,32,128]{3,2,1,0:T(8,128)(2,1)S(1)}, bf16[12,4,32,128]{3,2,1,0:T(8,128)(2,1)S(1)}, u32[]{:S(2)}, u32[]{:S(2)}) collective-permute-start(bf16[12,4,32,128]{3,2,1,0:T(8,128)(2,1)S(1)} %pack.1.bg0), channel_id=1, source_target_pairs={{0,8},{8,0},{16,24},{24,16},{1,9},{9,1},{17,25},{25,17},{2,10},{10... | collective-permute-start | bytes 1179656 | tf_op jit(solution)/shard_map/ppermute | solution.py:257
  28.5 12.1 %collective-permute-start.8 = (bf16[12,4,32,128]{3,2,1,0:T(8,128)(2,1)S(1)}, bf16[12,4,32,128]{3,2,1,0:T(8,128)(2,1)}, u32[]{:S(2)}, u32[]{:S(2)}) collective-permute-start(bf16[12,4,32,128]{3,2,1,0:T(8,128)(2,1)S(1)} %collective-permute-done.4.bg2), channel_id=1, source_target_pairs={{0,8},{8,0},{16,24},{24,16},{1,9},{9,1},{17,25},{25,17},{2,10},{10... | collective-permute-start | bytes 1179656 | tf_op jit(solution)/shard_map/ppermute | solution.py:257
  40.6 1.0 %copy-start.5 = (bf16[4,2,128,128]{3,2,1,0:T(8,128)(2,1)S(1)}, bf16[4,2,128,128]{3,2,1,0:T(8,128)(2,1)}, u32[]{:S(2)}) copy-start(bf16[4,2,128,128]{3,2,1,0:T(8,128)(2,1)} %copy-done.4) | copy-start | bytes 786436
  47.4 2.6 %collective-permute-start.9 = (bf16[2,2,2,128,128]{4,3,2,1,0:T(8,128)(2,1)S(1)}, bf16[2,2,2,128,128]{4,3,2,1,0:T(8,128)(2,1)S(1)}, u32[]{:S(2)}, u32[]{:S(2)}) collective-permute-start(bf16[2,2,2,128,128]{4,3,2,1,0:T(8,128)(2,1)S(1)} %get-tuple-element.41.h0a), channel_id=1, source_target_pairs={{0,8},{8,0},{16,24},{24,16},{1,9},{9,1},{17,25},{25,17},{2,10},{10... | collective-permute-start | bytes 786440 | tf_op jit(solution)/shard_map/ppermute | solution.py:257
  47.5 2.5 %collective-permute-start.10 = (bf16[2,2,2,128,128]{4,3,2,1,0:T(8,128)(2,1)S(1)}, bf16[2,2,2,128,128]{4,3,2,1,0:T(8,128)(2,1)S(1)}, u32[]{:S(2)}, u32[]{:S(2)}) collective-permute-start(bf16[2,2,2,128,128]{4,3,2,1,0:T(8,128)(2,1)S(1)} %get-tuple-element.42.h0b), channel_id=1, source_target_pairs={{0,8},{8,0},{16,24},{24,16},{1,9},{9,1},{17,25},{25,17},{2,10},{10... | collective-permute-start | bytes 786440 | tf_op jit(solution)/shard_map/ppermute | solution.py:257
  48.0 9.2 %collective-permute-start.11 = (bf16[2,2,2,128,128]{4,3,2,1,0:T(8,128)(2,1)S(1)}, bf16[2,2,2,128,128]{4,3,2,1,0:T(8,128)(2,1)S(1)}, u32[]{:S(2)}, u32[]{:S(2)}) collective-permute-start(bf16[2,2,2,128,128]{4,3,2,1,0:T(8,128)(2,1)S(1)} %get-tuple-element.41.h0a), channel_id=1, source_target_pairs={{0,16},{8,24},{16,0},{24,8},{1,17},{9,25},{17,1},{25,9},{2,18},{10... | collective-permute-start | bytes 786440 | tf_op jit(solution)/shard_map/ppermute | solution.py:257
  48.5 14.3 %collective-permute-start.12 = (bf16[2,2,2,128,128]{4,3,2,1,0:T(8,128)(2,1)S(1)}, bf16[2,2,2,128,128]{4,3,2,1,0:T(8,128)(2,1)S(1)}, u32[]{:S(2)}, u32[]{:S(2)}) collective-permute-start(bf16[2,2,2,128,128]{4,3,2,1,0:T(8,128)(2,1)S(1)} %get-tuple-element.42.h0b), channel_id=1, source_target_pairs={{0,16},{8,24},{16,0},{24,8},{1,17},{9,25},{17,1},{25,9},{2,18},{10... | collective-permute-start | bytes 786440 | tf_op jit(solution)/shard_map/ppermute | solution.py:257
  50.5 22.6 %collective-permute-start.17 = (bf16[4,2,2,128,128]{4,3,2,1,0:T(8,128)(2,1)S(1)}, bf16[4,2,2,128,128]{4,3,2,1,0:T(8,128)(2,1)S(1)}, u32[]{:S(2)}, u32[]{:S(2)}) collective-permute-start(bf16[4,2,2,128,128]{4,3,2,1,0:T(8,128)(2,1)S(1)} %get-tuple-element.44), channel_id=1, source_target_pairs={{0,16},{8,24},{16,0},{24,8},{1,17},{9,25},{17,1},{25,9},{2,18},{10... | collective-permute-start | bytes 1572872 | tf_op jit(solution)/shard_map/ppermute | solution.py:257
  57.1 5.6 %collective-permute-start.13 = (bf16[2,2,2,128,128]{4,3,2,1,0:T(8,128)(2,1)S(1)}, bf16[2,2,2,128,128]{4,3,2,1,0:T(8,128)(2,1)S(1)}, u32[]{:S(2)}, u32[]{:S(2)}) collective-permute-start(bf16[2,2,2,128,128]{4,3,2,1,0:T(8,128)(2,1)S(1)} %collective-permute-done.11.h2a), channel_id=1, source_target_pairs={{0,8},{8,0},{16,24},{24,16},{1,9},{9,1},{17,25},{25,17},{2,10},{10... | collective-permute-start | bytes 786440 | tf_op jit(solution)/shard_map/ppermute | solution.py:257
  62.8 1.5 %collective-permute-start.14 = (bf16[2,2,2,128,128]{4,3,2,1,0:T(8,128)(2,1)S(1)}, bf16[2,2,2,128,128]{4,3,2,1,0:T(8,128)(2,1)S(1)}, u32[]{:S(2)}, u32[]{:S(2)}) collective-permute-start(bf16[2,2,2,128,128]{4,3,2,1,0:T(8,128)(2,1)S(1)} %collective-permute-done.12.h2b), channel_id=1, source_target_pairs={{0,8},{8,0},{16,24},{24,16},{1,9},{9,1},{17,25},{25,17},{2,10},{10... | collective-permute-start | bytes 786440 | tf_op jit(solution)/shard_map/ppermute | solution.py:257
  65.2 3.7 %collective-permute-start.15 = (f32[16,16]{1,0:T(8,128)S(1)}, f32[16,16]{1,0:T(8,128)S(1)}, u32[]{:S(2)}, u32[]{:S(2)}) collective-permute-start(f32[16,16]{1,0:T(8,128)S(1)} %gram.1), channel_id=1, source_target_pairs={{0,1},{1,0},{2,3},{3,2},{4,5},{5,4},{6,7},{7,6},{8,9},{9,8},{10,11... | collective-permute-start | bytes 3080 | tf_op jit(solution)/shard_map/ppermute | solution.py:257
  68.9 3.7 %collective-permute-start.16 = (f32[16,16]{1,0:T(8,128)S(1)}, f32[16,16]{1,0:T(8,128)S(1)}, u32[]{:S(2)}, u32[]{:S(2)}) collective-permute-start(f32[16,16]{1,0:T(8,128)S(1)} %add.9), channel_id=1, source_target_pairs={{0,2},{1,3},{2,0},{3,1},{4,6},{5,7},{6,4},{7,5},{8,10},{9,11},{10,... | collective-permute-start | bytes 3080 | tf_op jit(solution)/shard_map/ppermute | solution.py:257
  68.9 8.8 %collective-permute-start.19 = (bf16[4,2,2,128,128]{4,3,2,1,0:T(8,128)(2,1)S(1)}, bf16[4,2,2,128,128]{4,3,2,1,0:T(8,128)(2,1)S(1)}, u32[]{:S(2)}, u32[]{:S(2)}) collective-permute-start(bf16[4,2,2,128,128]{4,3,2,1,0:T(8,128)(2,1)S(1)} %get-tuple-element.44), channel_id=1, source_target_pairs={{0,8},{8,0},{16,24},{24,16},{1,9},{9,1},{17,25},{25,17},{2,10},{10... | collective-permute-start | bytes 1572872 | tf_op jit(solution)/shard_map/ppermute | solution.py:257
  73.1 4.6 %collective-permute-start.20 = (bf16[4,2,2,128,128]{4,3,2,1,0:T(8,128)(2,1)S(1)}, bf16[4,2,2,128,128]{4,3,2,1,0:T(8,128)(2,1)S(1)}, u32[]{:S(2)}, u32[]{:S(2)}) collective-permute-start(bf16[4,2,2,128,128]{4,3,2,1,0:T(8,128)(2,1)S(1)} %collective-permute-done.17.l2), channel_id=1, source_target_pairs={{0,8},{8,0},{16,24},{24,16},{1,9},{9,1},{17,25},{25,17},{2,10},{10... | collective-permute-start | bytes 1572872 | tf_op jit(solution)/shard_map/ppermute | solution.py:257
  73.1 4.6 %collective-permute-start.18 = (f32[16,16]{1,0:T(8,128)S(1)}, f32[16,16]{1,0:T(8,128)S(1)}, u32[]{:S(2)}, u32[]{:S(2)}) collective-permute-start(f32[16,16]{1,0:T(8,128)S(1)} %add.10), channel_id=1, source_target_pairs={{0,4},{1,5},{2,6},{3,7},{4,0},{5,1},{6,2},{7,3},{8,12},{9,13},{10,... | collective-permute-start | bytes 3080 | tf_op jit(solution)/shard_map/ppermute | solution.py:257

commit v7 on v6

--- a/solution.py
+++ b/solution.py
@@ -60,7 +60,7 @@
                     store(row, vector, f, x, total)
         return carry
 
-    lax.fori_loop(0, rows, one_row, 0)
+    lax.fori_loop(0, rows, one_row, 0, unroll=2)
 
 
 def wrap(ref, columns):
@@ -329,7 +329,8 @@
         name="gram_own",
     )(hia, hib, h1a, h1b)
     lo, near = lax.optimization_barrier((lo, near))
-    l2, l1 = swap(lo, "vec", 2), swap(lo, "vec", 1)
+    l2 = lax.ppermute(lo, "vec", [(0, 2), (1, 3)])
+    l1 = lax.ppermute(lo, "vec", [(0, 1), (2, 3)])
     h3a, h3b = swap(h2a, "vec", 1), swap(h2b, "vec", 1)
     high = (hia, hib, h1a, h1b, h2a, h2b, h3a, h3b)
 
@@ -344,11 +345,15 @@
     )(me, near, *high)
     mask, size = 1, lax.axis_size("space")
     while mask < size:
-        if 2 * mask >= size:
+        if 4 * mask >= size:
             gram, l2 = lax.optimization_barrier((gram, l2))
-            l3 = swap(l2, "vec", 1)
-        gram = gram + swap(gram, "space", mask)
-        mask *= 2
+            l3 = lax.ppermute(l2, "vec", [(2, 3), (3, 2)])
+        if 2 * mask < size:
+            one, two, three = (swap(gram, "space", k) for k in (mask, 2 * mask, 3 * mask))
+            gram = (gram + one) + (two + three)
+        else:
+            gram = gram + swap(gram, "space", mask)
+        mask *= 4
 
     basis, growth = pl.pallas_call(
         functools.partial(final_kernel, 1.0 / cells),

time: 81.5 us -> 81 us (level); the launches traced: 81.3 us -> 79.8 us
  waiting for transfers between devices: 44.8 us -> 38.5 us
  starting transfers between devices: 20.2 us -> 25.4 us
    ppermute x15 -> x13, waiting for transfers between devices: 22.7 us -> 16.4 us  [swap(): lax.ppermute(value, axis, [(i, i ^ mask) for i in range(lax.axis_size(axi...]
    ppermute x0 -> x3, starting transfers between devices: none -> 4.44 us  [the longest x1 2.43 us: on_device(): l2 = lax.ppermute(lo, 'vec', [(0, 2), (1, 3)])]
    ppermute x15 -> x13, starting transfers between devices: 8.23 us -> 8.99 us  [swap(): lax.ppermute(value, axis, [(i, i ^ mask) for i in range(lax.axis_size(axi...]
  transfers between devices with their start and end apart: 21 -> 22, of which waited for: 12 -> 11; matrix products, arithmetic and copies ran while one was open for 0% -> 0% of each run, Pallas kernels for 3% -> 3%
where the time goes in v7:
time: 81 us; the launch traced here: 79.8 us
  waiting for transfers between devices  38.5 us (48%)
  starting transfers between devices  25.4 us (31%)
  Pallas kernels  11.4 us (14%)
  local copies, waits for them, and re-layouts  3.79 us (5%)
    ppermute x6, waiting for transfers between devices, shift(): lax.ppermute(value, axis, [(i, (i + step) % count) for i in range(count)])  22.1 us
    ppermute x13, waiting for transfers between devices, swap(): lax.ppermute(value, axis, [(i, i ^ mask) for i in range(lax.axis_size(axi...  16.4 us
    ppermute x6, starting transfers between devices, shift(): lax.ppermute(value, axis, [(i, (i + step) % count) for i in range(count)])  11.9 us
    ppermute x13, starting transfers between devices, swap(): lax.ppermute(value, axis, [(i, i ^ mask) for i in range(lax.axis_size(axi...  8.99 us
    pallas_call x1, Pallas kernels, on_device(): pl.pallas_call(advance_kernel, out_shape=[jax.ShapeDtypeStruct(tangents.s...  5.57 us
    unnamed x12, local copies, waits for them, and re-layouts  3.79 us
    pallas_call x1, Pallas kernels, on_device(): pl.pallas_call(functools.partial(final_kernel, 1.0 / cells), out_shape=[j...  3.56 us
    ppermute x1, starting transfers between devices, on_device(): l2 = lax.ppermute(lo, 'vec', [(0, 2), (1, 3)])  2.43 us
  transfers between devices with their start and end apart: 22, of which 11 were waited for; matrix products, arithmetic and copies ran while one was open for 0% of the time, Pallas kernels for 3%

profile of v7, /device:TPU:0, one launch (start us, length us, event | category | flops | bytes accessed | tf_op | source)
XLA Modules:
  0.0 79.8 jit_solution(11380382005019837088)
XLA Ops:
  0.6 0.9 %copy-done.2 = bf16[3,4,2,32,128]{4,3,2,1,0:T(8,128)(2,1)S(1)} copy-done((bf16[3,4,2,32,128]{4,3,2,1,0:T(8,128)(2,1)S(1)}, bf16[3,4,2,32,128]{4,3,2,1,0:T(8,128)(2,1)}, u32[]{:S(2)}) %copy-start.2) | copy-done | bytes 196632
  1.6 3.0 %collective-permute-start = (bf16[3,4,32,128]{3,2,1,0:T(8,128)(2,1)S(1)}, bf16[3,4,32,128]{3,2,1,0:T(8,128)(2,1)S(1)}, u32[]{:S(2)}, u32[]{:S(2)}) collective-permute-start(bf16[3,4,32,128]{3,2,1,0:T(8,128)(2,1)S(1)} %get-tuple-element.29), channel_id=1, source_target_pairs={{0,1},{1,2},{2,3},{3,4},{4,5},{5,6},{6,7},{7,0},{8,9},{9,10},{10,1... | collective-permute-start | bytes 294920 | tf_op jit(solution)/shard_map/ppermute | solution.py:253
  4.6 3.1 %collective-permute-start.1 = (bf16[3,4,32,128]{3,2,1,0:T(8,128)(2,1)S(1)}, bf16[3,4,32,128]{3,2,1,0:T(8,128)(2,1)S(1)}, u32[]{:S(2)}, u32[]{:S(2)}) collective-permute-start(bf16[3,4,32,128]{3,2,1,0:T(8,128)(2,1)S(1)} %get-tuple-element.30), channel_id=1, source_target_pairs={{0,7},{1,0},{2,1},{3,2},{4,3},{5,4},{6,5},{7,6},{8,15},{9,8},{10,9... | collective-permute-start | bytes 294920 | tf_op jit(solution)/shard_map/ppermute | solution.py:253
  7.7 1.2 %copy-done = f32[4,2,2,128,128]{4,3,2,1,0:T(8,128)S(1)} copy-done((f32[4,2,2,128,128]{4,3,2,1,0:T(8,128)S(1)}, f32[4,2,2,128,128]{4,3,2,1,0:T(8,128)}, u32[]{:S(2)}) %copy-start) | copy-done | bytes 1048600
  8.9 0.9 %prep.1 = (bf16[2,4,2,128,128]{4,3,2,1,0:T(8,128)(2,1)}, bf16[4,2,128,128]{3,2,1,0:T(8,128)(2,1)S(1)}, bf16[4,2,128,128]{3,2,1,0:T(8,128)(2,1)S(1)}) custom-call(f32[4,2,2,128,128]{4,3,2,1,0:T(8,128)S(1)} %copy-done), custom_call_target="tpu_custom_call" | custom-call | tf_op jit(solution)/shard_map/prep/pallas_call | solution.py:267
  9.8 0.7 collective-permute-done.up
  10.5 0.8 collective-permute-done.1.dn
  11.3 1.6 %collective-permute-start.4 = (bf16[12,4,32,128]{3,2,1,0:T(8,128)(2,1)S(1)}, bf16[12,4,32,128]{3,2,1,0:T(8,128)(2,1)S(1)}, u32[]{:S(2)}, u32[]{:S(2)}) collective-permute-start(bf16[12,4,32,128]{3,2,1,0:T(8,128)(2,1)S(1)} %pack.1.bg0), channel_id=1, source_target_pairs={{0,16},{8,24},{16,0},{24,8},{1,17},{9,25},{17,1},{25,9},{2,18},{10... | collective-permute-start | bytes 1179656 | tf_op jit(solution)/shard_map/ppermute | solution.py:257
  12.9 0.9 %collective-permute-start.5 = (bf16[4,2,128,128]{3,2,1,0:T(8,128)(2,1)S(1)}, bf16[4,2,128,128]{3,2,1,0:T(8,128)(2,1)S(1)}, u32[]{:S(2)}, u32[]{:S(2)}) collective-permute-start(bf16[4,2,128,128]{3,2,1,0:T(8,128)(2,1)S(1)} %get-tuple-element.34), channel_id=1, source_target_pairs={{0,2},{1,3},{2,4},{3,5},{4,6},{5,7},{6,0},{7,1},{8,10},{9,11},{10,... | collective-permute-start | bytes 786440 | tf_op jit(solution)/shard_map/ppermute | solution.py:253
  13.8 2.9 %collective-permute-start.6 = (bf16[4,2,128,128]{3,2,1,0:T(8,128)(2,1)S(1)}, bf16[4,2,128,128]{3,2,1,0:T(8,128)(2,1)S(1)}, u32[]{:S(2)}, u32[]{:S(2)}) collective-permute-start(bf16[4,2,128,128]{3,2,1,0:T(8,128)(2,1)S(1)} %get-tuple-element.35), channel_id=1, source_target_pairs={{0,6},{1,7},{2,0},{3,1},{4,2},{5,3},{6,4},{7,5},{8,14},{9,15},{10,... | collective-permute-start | bytes 786440 | tf_op jit(solution)/shard_map/ppermute | solution.py:253
  16.7 2.0 %collective-permute-start.3 = (bf16[2,4,2,128,128]{4,3,2,1,0:T(8,128)(2,1)}, bf16[2,4,2,128,128]{4,3,2,1,0:T(8,128)(2,1)S(1)}, u32[]{:S(2)}, u32[]{:S(2)}) collective-permute-start(bf16[2,4,2,128,128]{4,3,2,1,0:T(8,128)(2,1)} %get-tuple-element.31), channel_id=1, source_target_pairs={{0,7},{1,0},{2,1},{3,2},{4,3},{5,4},{6,5},{7,6},{8,15},{9,8},{10,9... | collective-permute-start | bytes 1572872 | tf_op jit(solution)/shard_map/ppermute | solution.py:253
  18.8 5.2 %collective-permute-done.5.up2 = bf16[4,2,128,128]{3,2,1,0:T(8,128)(2,1)S(1)} collective-permute-done((bf16[4,2,128,128]{3,2,1,0:T(8,128)(2,1)S(1)}, bf16[4,2,128,128]{3,2,1,0:T(8,128)(2,1)S(1)}, u32[]{:S(2)}, u32[]{:S(2)}) %collective-permute-start.5) | collective-permute-done | bytes 262176 | tf_op jit(solution)/shard_map/ppermute | solution.py:253
  24.0 3.8 %collective-permute-done.6.dn2 = bf16[4,2,128,128]{3,2,1,0:T(8,128)(2,1)S(1)} collective-permute-done((bf16[4,2,128,128]{3,2,1,0:T(8,128)(2,1)S(1)}, bf16[4,2,128,128]{3,2,1,0:T(8,128)(2,1)S(1)}, u32[]{:S(2)}, u32[]{:S(2)}) %collective-permute-start.6) | collective-permute-done | bytes 262176 | tf_op jit(solution)/shard_map/ppermute | solution.py:253
  27.8 0.7 copy-done.4
  28.5 0.5 collective-permute-start.8
  29.0 11.5 %collective-permute-done.3.dn1 = bf16[2,4,2,128,128]{4,3,2,1,0:T(8,128)(2,1)S(1)} collective-permute-done((bf16[2,4,2,128,128]{4,3,2,1,0:T(8,128)(2,1)}, bf16[2,4,2,128,128]{4,3,2,1,0:T(8,128)(2,1)S(1)}, u32[]{:S(2)}, u32[]{:S(2)}) %collective-permute-start.3) | collective-permute-done | bytes 524320 | tf_op jit(solution)/shard_map/ppermute | solution.py:253
  40.6 0.9 %copy-done.5 = bf16[4,2,128,128]{3,2,1,0:T(8,128)(2,1)S(1)} copy-done((bf16[4,2,128,128]{3,2,1,0:T(8,128)(2,1)S(1)}, bf16[4,2,128,128]{3,2,1,0:T(8,128)(2,1)}, u32[]{:S(2)}) %copy-start.5) | copy-done | bytes 262168
  41.5 5.6 %advance.1 = (f32[4,2,2,128,128]{4,3,2,1,0:T(8,128)S(1)}, bf16[2,2,2,128,128]{4,3,2,1,0:T(8,128)(2,1)S(1)}, bf16[2,2,2,128,128]{4,3,2,1,0:T(8,128)(2,1)S(1)}, bf16[4,2,2,128,128]{4,3,2,1,0:T(8,128)(2,1)S(1)}) custom-call(s32[1]{0:T(128)} %bitcast.me, f32[4,2,2,128,128]{4,3,2,1,0:T(8,128)S(1)} %copy-done.1, ...), custom_call_target="tpu_custom_call" | custom-call | tf_op jit(solution)/shard_map/advance/pallas_call | solution.py:306
  48.2 1.5 %collective-permute-start.12 = (bf16[2,2,2,128,128]{4,3,2,1,0:T(8,128)(2,1)S(1)}, bf16[2,2,2,128,128]{4,3,2,1,0:T(8,128)(2,1)S(1)}, u32[]{:S(2)}, u32[]{:S(2)}) collective-permute-start(bf16[2,2,2,128,128]{4,3,2,1,0:T(8,128)(2,1)S(1)} %get-tuple-element.42.h0b), channel_id=1, source_target_pairs={{0,16},{8,24},{16,0},{24,8},{1,17},{9,25},{17,1},{25,9},{2,18},{10... | collective-permute-start | bytes 786440 | tf_op jit(solution)/shard_map/ppermute | solution.py:257
  50.2 2.4 %collective-permute-start.18 = (bf16[4,2,2,128,128]{4,3,2,1,0:T(8,128)(2,1)S(1)}, bf16[4,2,2,128,128]{4,3,2,1,0:T(8,128)(2,1)S(1)}, u32[]{:S(2)}, u32[]{:S(2)}) collective-permute-start(bf16[4,2,2,128,128]{4,3,2,1,0:T(8,128)(2,1)S(1)} %get-tuple-element.44), channel_id=1, source_target_pairs={{0,16},{8,24},{1,17},{9,25},{2,18},{10,26},{3,19},{11,27},{4,20},{... | collective-permute-start | bytes 1572872 | tf_op jit(solution)/shard_map/ppermute | solution.py:332
  52.6 4.2 %collective-permute-done.11.h2a = bf16[2,2,2,128,128]{4,3,2,1,0:T(8,128)(2,1)S(1)} collective-permute-done((bf16[2,2,2,128,128]{4,3,2,1,0:T(8,128)(2,1)S(1)}, bf16[2,2,2,128,128]{4,3,2,1,0:T(8,128)(2,1)S(1)}, u32[]{:S(2)}, u32[]{:S(2)}) %collective-permute-start.11) | collective-permute-done | bytes 262176 | tf_op jit(solution)/shard_map/ppermute | solution.py:257
  56.8 4.7 %collective-permute-done.12.h2b = bf16[2,2,2,128,128]{4,3,2,1,0:T(8,128)(2,1)S(1)} collective-permute-done((bf16[2,2,2,128,128]{4,3,2,1,0:T(8,128)(2,1)S(1)}, bf16[2,2,2,128,128]{4,3,2,1,0:T(8,128)(2,1)S(1)}, u32[]{:S(2)}, u32[]{:S(2)}) %collective-permute-start.12) | collective-permute-done | bytes 262176 | tf_op jit(solution)/shard_map/ppermute | solution.py:257
  61.6 1.5 %collective-permute-done.14.h3b = bf16[2,2,2,128,128]{4,3,2,1,0:T(8,128)(2,1)S(1)} collective-permute-done((bf16[2,2,2,128,128]{4,3,2,1,0:T(8,128)(2,1)S(1)}, bf16[2,2,2,128,128]{4,3,2,1,0:T(8,128)(2,1)S(1)}, u32[]{:S(2)}, u32[]{:S(2)}) %collective-permute-start.14) | collective-permute-done | bytes 262176 | tf_op jit(solution)/shard_map/ppermute | solution.py:257
  63.1 0.9 %gram.1 = f32[16,16]{1,0:T(8,128)S(1)} custom-call(s32[1]{0:T(128)} %bitcast.me, f32[8,128]{1,0:T(8,128)S(1)} %gram_own.1.near, bf16[2,2,2,128,128]{4,3,2,1,0:T(8,128)(2,1)S(1)} %get-tuple-element.41.h0a, bf16[2,2,2,128,128]{4,3,2,1,0:T(8,128)(2,1)S(1)} %get-tuple-element.42.h0b, bf16[2,2,2,128,128]{4,3,2,1,0:T(8,128)(2,1)S(1)} %collective-permute-done.9.h1a, ...), custom_call_target="tpu_custom_call" | custom-call | tf_op jit(solution)/shard_map/gram/pallas_call | solution.py:337
  64.1 1.0 %collective-permute-start.17 = (f32[16,16]{1,0:T(8,128)S(1)}, f32[16,16]{1,0:T(8,128)S(1)}, u32[]{:S(2)}, u32[]{:S(2)}) collective-permute-start(f32[16,16]{1,0:T(8,128)S(1)} %gram.1), channel_id=1, source_target_pairs={{0,3},{1,2},{2,1},{3,0},{4,7},{5,6},{6,5},{7,4},{8,11},{9,10},{10,... | collective-permute-start | bytes 3080 | tf_op jit(solution)/shard_map/ppermute | solution.py:257
  65.0 2.2 %collective-permute-start.16 = (f32[16,16]{1,0:T(8,128)S(1)}, f32[16,16]{1,0:T(8,128)S(1)}, u32[]{:S(2)}, u32[]{:S(2)}) collective-permute-start(f32[16,16]{1,0:T(8,128)S(1)} %gram.1), channel_id=1, source_target_pairs={{0,2},{1,3},{2,0},{3,1},{4,6},{5,7},{6,4},{7,5},{8,10},{9,11},{10,... | collective-permute-start | bytes 3080 | tf_op jit(solution)/shard_map/ppermute | solution.py:257
  67.6 1.3 %collective-permute-start.20 = (bf16[4,2,2,128,128]{4,3,2,1,0:T(8,128)(2,1)S(1)}, bf16[4,2,2,128,128]{4,3,2,1,0:T(8,128)(2,1)S(1)}, u32[]{:S(2)}, u32[]{:S(2)}) collective-permute-start(bf16[4,2,2,128,128]{4,3,2,1,0:T(8,128)(2,1)S(1)} %get-tuple-element.44), channel_id=1, source_target_pairs={{0,8},{16,24},{1,9},{17,25},{2,10},{18,26},{3,11},{19,27},{4,12},{... | collective-permute-start | bytes 1572872 | tf_op jit(solution)/shard_map/ppermute | solution.py:333
  69.0 1.9 %collective-permute-done.15 = f32[16,16]{1,0:T(8,128)S(1)} collective-permute-done((f32[16,16]{1,0:T(8,128)S(1)}, f32[16,16]{1,0:T(8,128)S(1)}, u32[]{:S(2)}, u32[]{:S(2)}) %collective-permute-start.15) | collective-permute-done | bytes 1056 | tf_op jit(solution)/shard_map/ppermute | solution.py:257
  70.9 0.7 collective-permute-start.21
  71.6 0.8 collective-permute-start.19
  72.4 3.8 %collective-permute-done.19 = f32[16,16]{1,0:T(8,128)S(1)} collective-permute-done((f32[16,16]{1,0:T(8,128)S(1)}, f32[16,16]{1,0:T(8,128)S(1)}, u32[]{:S(2)}, u32[]{:S(2)}) %collective-permute-start.19) | collective-permute-done | bytes 1056 | tf_op jit(solution)/shard_map/ppermute | solution.py:257
  76.3 3.6 %final.1 = (f32[4,2,2,128,128]{4,3,2,1,0:T(8,128)}, f32[1,16]{1,0:T(1,128)}) custom-call(s32[1]{0:T(128)} %bitcast.me, f32[16,16]{1,0:T(8,128)S(1)} %add.15.gram, f32[4,2,2,128,128]{4,3,2,1,0:T(8,128)S(1)} %get-tuple-element.46.own, bf16[2,2,2,128,128]{4,3,2,1,0:T(8,128)(2,1)S(1)} %collective-permute-done.9.h1a, ...), custom_call_target="tpu_custom_call" | custom-call | tf_op jit(solution)/shard_map/final/pallas_call | solution.py:358
  (33 shorter events, 2.0 us)
Async XLA Ops:
  0.6 0.9 %copy-start.2 = (bf16[3,4,2,32,128]{4,3,2,1,0:T(8,128)(2,1)S(1)}, bf16[3,4,2,32,128]{4,3,2,1,0:T(8,128)(2,1)}, u32[]{:S(2)}) copy-start(bf16[3,4,2,32,128]{4,3,2,1,0:T(8,128)(2,1)} %background.3) | copy-start | bytes 589828
  1.6 9.7 %copy-start.3 = (bf16[3,4,2,32,128]{4,3,2,1,0:T(8,128)(2,1)S(1)}, bf16[3,4,2,32,128]{4,3,2,1,0:T(8,128)(2,1)}, u32[]{:S(2)}) copy-start(bf16[3,4,2,32,128]{4,3,2,1,0:T(8,128)(2,1)} %background.3) | copy-start | bytes 589828
  1.6 8.9 %collective-permute-start = (bf16[3,4,32,128]{3,2,1,0:T(8,128)(2,1)S(1)}, bf16[3,4,32,128]{3,2,1,0:T(8,128)(2,1)S(1)}, u32[]{:S(2)}, u32[]{:S(2)}) collective-permute-start(bf16[3,4,32,128]{3,2,1,0:T(8,128)(2,1)S(1)} %get-tuple-element.29), channel_id=1, source_target_pairs={{0,1},{1,2},{2,3},{3,4},{4,5},{5,6},{6,7},{7,0},{8,9},{9,10},{10,1... | collective-permute-start | bytes 294920 | tf_op jit(solution)/shard_map/ppermute | solution.py:253
  4.6 6.7 %collective-permute-start.1 = (bf16[3,4,32,128]{3,2,1,0:T(8,128)(2,1)S(1)}, bf16[3,4,32,128]{3,2,1,0:T(8,128)(2,1)S(1)}, u32[]{:S(2)}, u32[]{:S(2)}) collective-permute-start(bf16[3,4,32,128]{3,2,1,0:T(8,128)(2,1)S(1)} %get-tuple-element.30), channel_id=1, source_target_pairs={{0,7},{1,0},{2,1},{3,2},{4,3},{5,4},{6,5},{7,6},{8,15},{9,8},{10,9... | collective-permute-start | bytes 294920 | tf_op jit(solution)/shard_map/ppermute | solution.py:253
  7.7 1.2 %copy-start = (f32[4,2,2,128,128]{4,3,2,1,0:T(8,128)S(1)}, f32[4,2,2,128,128]{4,3,2,1,0:T(8,128)}, u32[]{:S(2)}) copy-start(f32[4,2,2,128,128]{4,3,2,1,0:T(8,128)} %own.3) | copy-start | bytes 3145732
  8.9 31.7 %copy-start.1 = (f32[4,2,2,128,128]{4,3,2,1,0:T(8,128)S(1)}, f32[4,2,2,128,128]{4,3,2,1,0:T(8,128)}, u32[]{:S(2)}) copy-start(f32[4,2,2,128,128]{4,3,2,1,0:T(8,128)} %own.3) | copy-start | bytes 3145732
  11.3 17.2 %collective-permute-start.4 = (bf16[12,4,32,128]{3,2,1,0:T(8,128)(2,1)S(1)}, bf16[12,4,32,128]{3,2,1,0:T(8,128)(2,1)S(1)}, u32[]{:S(2)}, u32[]{:S(2)}) collective-permute-start(bf16[12,4,32,128]{3,2,1,0:T(8,128)(2,1)S(1)} %pack.1.bg0), channel_id=1, source_target_pairs={{0,16},{8,24},{16,0},{24,8},{1,17},{9,25},{17,1},{25,9},{2,18},{10... | collective-permute-start | bytes 1179656 | tf_op jit(solution)/shard_map/ppermute | solution.py:257
  12.9 11.1 %collective-permute-start.5 = (bf16[4,2,128,128]{3,2,1,0:T(8,128)(2,1)S(1)}, bf16[4,2,128,128]{3,2,1,0:T(8,128)(2,1)S(1)}, u32[]{:S(2)}, u32[]{:S(2)}) collective-permute-start(bf16[4,2,128,128]{3,2,1,0:T(8,128)(2,1)S(1)} %get-tuple-element.34), channel_id=1, source_target_pairs={{0,2},{1,3},{2,4},{3,5},{4,6},{5,7},{6,0},{7,1},{8,10},{9,11},{10,... | collective-permute-start | bytes 786440 | tf_op jit(solution)/shard_map/ppermute | solution.py:253
  13.8 14.0 %collective-permute-start.6 = (bf16[4,2,128,128]{3,2,1,0:T(8,128)(2,1)S(1)}, bf16[4,2,128,128]{3,2,1,0:T(8,128)(2,1)S(1)}, u32[]{:S(2)}, u32[]{:S(2)}) collective-permute-start(bf16[4,2,128,128]{3,2,1,0:T(8,128)(2,1)S(1)} %get-tuple-element.35), channel_id=1, source_target_pairs={{0,6},{1,7},{2,0},{3,1},{4,2},{5,3},{6,4},{7,5},{8,14},{9,15},{10,... | collective-permute-start | bytes 786440 | tf_op jit(solution)/shard_map/ppermute | solution.py:253
  16.7 23.8 %collective-permute-start.3 = (bf16[2,4,2,128,128]{4,3,2,1,0:T(8,128)(2,1)}, bf16[2,4,2,128,128]{4,3,2,1,0:T(8,128)(2,1)S(1)}, u32[]{:S(2)}, u32[]{:S(2)}) collective-permute-start(bf16[2,4,2,128,128]{4,3,2,1,0:T(8,128)(2,1)} %get-tuple-element.31), channel_id=1, source_target_pairs={{0,7},{1,0},{2,1},{3,2},{4,3},{5,4},{6,5},{7,6},{8,15},{9,8},{10,9... | collective-permute-start | bytes 1572872 | tf_op jit(solution)/shard_map/ppermute | solution.py:253
  18.8 21.8 %collective-permute-start.2 = (bf16[2,4,2,128,128]{4,3,2,1,0:T(8,128)(2,1)}, bf16[2,4,2,128,128]{4,3,2,1,0:T(8,128)(2,1)S(1)}, u32[]{:S(2)}, u32[]{:S(2)}) collective-permute-start(bf16[2,4,2,128,128]{4,3,2,1,0:T(8,128)(2,1)} %get-tuple-element.31), channel_id=1, source_target_pairs={{0,1},{1,2},{2,3},{3,4},{4,5},{5,6},{6,7},{7,0},{8,9},{9,10},{10,1... | collective-permute-start | bytes 1572872 | tf_op jit(solution)/shard_map/ppermute | solution.py:253
  27.8 0.7 copy-start.4
  28.5 12.1 %collective-permute-start.7 = (bf16[12,4,32,128]{3,2,1,0:T(8,128)(2,1)S(1)}, bf16[12,4,32,128]{3,2,1,0:T(8,128)(2,1)S(1)}, u32[]{:S(2)}, u32[]{:S(2)}) collective-permute-start(bf16[12,4,32,128]{3,2,1,0:T(8,128)(2,1)S(1)} %pack.1.bg0), channel_id=1, source_target_pairs={{0,8},{8,0},{16,24},{24,16},{1,9},{9,1},{17,25},{25,17},{2,10},{10... | collective-permute-start | bytes 1179656 | tf_op jit(solution)/shard_map/ppermute | solution.py:257
  28.5 12.1 %collective-permute-start.8 = (bf16[12,4,32,128]{3,2,1,0:T(8,128)(2,1)S(1)}, bf16[12,4,32,128]{3,2,1,0:T(8,128)(2,1)}, u32[]{:S(2)}, u32[]{:S(2)}) collective-permute-start(bf16[12,4,32,128]{3,2,1,0:T(8,128)(2,1)S(1)} %collective-permute-done.4.bg2), channel_id=1, source_target_pairs={{0,8},{8,0},{16,24},{24,16},{1,9},{9,1},{17,25},{25,17},{2,10},{10... | collective-permute-start | bytes 1179656 | tf_op jit(solution)/shard_map/ppermute | solution.py:257
  40.6 1.0 %copy-start.5 = (bf16[4,2,128,128]{3,2,1,0:T(8,128)(2,1)S(1)}, bf16[4,2,128,128]{3,2,1,0:T(8,128)(2,1)}, u32[]{:S(2)}) copy-start(bf16[4,2,128,128]{3,2,1,0:T(8,128)(2,1)} %copy-done.4) | copy-start | bytes 786436
  47.1 2.6 %collective-permute-start.9 = (bf16[2,2,2,128,128]{4,3,2,1,0:T(8,128)(2,1)S(1)}, bf16[2,2,2,128,128]{4,3,2,1,0:T(8,128)(2,1)S(1)}, u32[]{:S(2)}, u32[]{:S(2)}) collective-permute-start(bf16[2,2,2,128,128]{4,3,2,1,0:T(8,128)(2,1)S(1)} %get-tuple-element.41.h0a), channel_id=1, source_target_pairs={{0,8},{8,0},{16,24},{24,16},{1,9},{9,1},{17,25},{25,17},{2,10},{10... | collective-permute-start | bytes 786440 | tf_op jit(solution)/shard_map/ppermute | solution.py:257
  47.2 2.5 %collective-permute-start.10 = (bf16[2,2,2,128,128]{4,3,2,1,0:T(8,128)(2,1)S(1)}, bf16[2,2,2,128,128]{4,3,2,1,0:T(8,128)(2,1)S(1)}, u32[]{:S(2)}, u32[]{:S(2)}) collective-permute-start(bf16[2,2,2,128,128]{4,3,2,1,0:T(8,128)(2,1)S(1)} %get-tuple-element.42.h0b), channel_id=1, source_target_pairs={{0,8},{8,0},{16,24},{24,16},{1,9},{9,1},{17,25},{25,17},{2,10},{10... | collective-permute-start | bytes 786440 | tf_op jit(solution)/shard_map/ppermute | solution.py:257
  47.7 9.2 %collective-permute-start.11 = (bf16[2,2,2,128,128]{4,3,2,1,0:T(8,128)(2,1)S(1)}, bf16[2,2,2,128,128]{4,3,2,1,0:T(8,128)(2,1)S(1)}, u32[]{:S(2)}, u32[]{:S(2)}) collective-permute-start(bf16[2,2,2,128,128]{4,3,2,1,0:T(8,128)(2,1)S(1)} %get-tuple-element.41.h0a), channel_id=1, source_target_pairs={{0,16},{8,24},{16,0},{24,8},{1,17},{9,25},{17,1},{25,9},{2,18},{10... | collective-permute-start | bytes 786440 | tf_op jit(solution)/shard_map/ppermute | solution.py:257
  48.2 13.4 %collective-permute-start.12 = (bf16[2,2,2,128,128]{4,3,2,1,0:T(8,128)(2,1)S(1)}, bf16[2,2,2,128,128]{4,3,2,1,0:T(8,128)(2,1)S(1)}, u32[]{:S(2)}, u32[]{:S(2)}) collective-permute-start(bf16[2,2,2,128,128]{4,3,2,1,0:T(8,128)(2,1)S(1)} %get-tuple-element.42.h0b), channel_id=1, source_target_pairs={{0,16},{8,24},{16,0},{24,8},{1,17},{9,25},{17,1},{25,9},{2,18},{10... | collective-permute-start | bytes 786440 | tf_op jit(solution)/shard_map/ppermute | solution.py:257
  50.2 20.8 %collective-permute-start.18 = (bf16[4,2,2,128,128]{4,3,2,1,0:T(8,128)(2,1)S(1)}, bf16[4,2,2,128,128]{4,3,2,1,0:T(8,128)(2,1)S(1)}, u32[]{:S(2)}, u32[]{:S(2)}) collective-permute-start(bf16[4,2,2,128,128]{4,3,2,1,0:T(8,128)(2,1)S(1)} %get-tuple-element.44), channel_id=1, source_target_pairs={{0,16},{8,24},{1,17},{9,25},{2,18},{10,26},{3,19},{11,27},{4,20},{... | collective-permute-start | bytes 1572872 | tf_op jit(solution)/shard_map/ppermute | solution.py:332
  56.8 4.8 %collective-permute-start.13 = (bf16[2,2,2,128,128]{4,3,2,1,0:T(8,128)(2,1)S(1)}, bf16[2,2,2,128,128]{4,3,2,1,0:T(8,128)(2,1)S(1)}, u32[]{:S(2)}, u32[]{:S(2)}) collective-permute-start(bf16[2,2,2,128,128]{4,3,2,1,0:T(8,128)(2,1)S(1)} %collective-permute-done.11.h2a), channel_id=1, source_target_pairs={{0,8},{8,0},{16,24},{24,16},{1,9},{9,1},{17,25},{25,17},{2,10},{10... | collective-permute-start | bytes 786440 | tf_op jit(solution)/shard_map/ppermute | solution.py:257
  61.6 1.5 %collective-permute-start.14 = (bf16[2,2,2,128,128]{4,3,2,1,0:T(8,128)(2,1)S(1)}, bf16[2,2,2,128,128]{4,3,2,1,0:T(8,128)(2,1)S(1)}, u32[]{:S(2)}, u32[]{:S(2)}) collective-permute-start(bf16[2,2,2,128,128]{4,3,2,1,0:T(8,128)(2,1)S(1)} %collective-permute-done.12.h2b), channel_id=1, source_target_pairs={{0,8},{8,0},{16,24},{24,16},{1,9},{9,1},{17,25},{25,17},{2,10},{10... | collective-permute-start | bytes 786440 | tf_op jit(solution)/shard_map/ppermute | solution.py:257
  64.1 4.8 %collective-permute-start.17 = (f32[16,16]{1,0:T(8,128)S(1)}, f32[16,16]{1,0:T(8,128)S(1)}, u32[]{:S(2)}, u32[]{:S(2)}) collective-permute-start(f32[16,16]{1,0:T(8,128)S(1)} %gram.1), channel_id=1, source_target_pairs={{0,3},{1,2},{2,1},{3,0},{4,7},{5,6},{6,5},{7,4},{8,11},{9,10},{10,... | collective-permute-start | bytes 3080 | tf_op jit(solution)/shard_map/ppermute | solution.py:257
  65.0 4.0 %collective-permute-start.16 = (f32[16,16]{1,0:T(8,128)S(1)}, f32[16,16]{1,0:T(8,128)S(1)}, u32[]{:S(2)}, u32[]{:S(2)}) collective-permute-start(f32[16,16]{1,0:T(8,128)S(1)} %gram.1), channel_id=1, source_target_pairs={{0,2},{1,3},{2,0},{3,1},{4,6},{5,7},{6,4},{7,5},{8,10},{9,11},{10,... | collective-permute-start | bytes 3080 | tf_op jit(solution)/shard_map/ppermute | solution.py:257
  67.3 3.7 %collective-permute-start.15 = (f32[16,16]{1,0:T(8,128)S(1)}, f32[16,16]{1,0:T(8,128)S(1)}, u32[]{:S(2)}, u32[]{:S(2)}) collective-permute-start(f32[16,16]{1,0:T(8,128)S(1)} %gram.1), channel_id=1, source_target_pairs={{0,1},{1,0},{2,3},{3,2},{4,5},{5,4},{6,7},{7,6},{8,9},{9,8},{10,11... | collective-permute-start | bytes 3080 | tf_op jit(solution)/shard_map/ppermute | solution.py:257
  67.6 8.7 %collective-permute-start.20 = (bf16[4,2,2,128,128]{4,3,2,1,0:T(8,128)(2,1)S(1)}, bf16[4,2,2,128,128]{4,3,2,1,0:T(8,128)(2,1)S(1)}, u32[]{:S(2)}, u32[]{:S(2)}) collective-permute-start(bf16[4,2,2,128,128]{4,3,2,1,0:T(8,128)(2,1)S(1)} %get-tuple-element.44), channel_id=1, source_target_pairs={{0,8},{16,24},{1,9},{17,25},{2,10},{18,26},{3,11},{19,27},{4,12},{... | collective-permute-start | bytes 1572872 | tf_op jit(solution)/shard_map/ppermute | solution.py:333
  70.9 5.3 %collective-permute-start.21 = (bf16[4,2,2,128,128]{4,3,2,1,0:T(8,128)(2,1)S(1)}, bf16[4,2,2,128,128]{4,3,2,1,0:T(8,128)(2,1)S(1)}, u32[]{:S(2)}, u32[]{:S(2)}) collective-permute-start(bf16[4,2,2,128,128]{4,3,2,1,0:T(8,128)(2,1)S(1)} %collective-permute-done.18.l2), channel_id=1, source_target_pairs={{16,24},{24,16},{17,25},{25,17},{18,26},{26,18},{19,27},{27,19},{2... | collective-permute-start | bytes 1572872 | tf_op jit(solution)/shard_map/ppermute | solution.py:350
  71.6 4.6 %collective-permute-start.19 = (f32[16,16]{1,0:T(8,128)S(1)}, f32[16,16]{1,0:T(8,128)S(1)}, u32[]{:S(2)}, u32[]{:S(2)}) collective-permute-start(f32[16,16]{1,0:T(8,128)S(1)} %add_add_fusion), channel_id=1, source_target_pairs={{0,4},{1,5},{2,6},{3,7},{4,0},{5,1},{6,2},{7,3},{8,12},{9,13},{10,... | collective-permute-start | bytes 3080 | tf_op jit(solution)/shard_map/ppermute | solution.py:257

commit v8 on v7

--- a/solution.py
+++ b/solution.py
@@ -297,7 +297,7 @@
         name="pack",
     )(background, bg_up, bg_dn)
     bg2 = swap(packed, "vec", 2)
-    near_bg, far_bg, up2, dn2 = lax.optimization_barrier((packed, bg2, up2, dn2))
+    near_bg, far_bg, _ = lax.optimization_barrier((packed, bg2, dn2))
     bgs = [packed, swap(near_bg, "vec", 1), bg2, swap(far_bg, "vec", 1)]
 
     low = jax.ShapeDtypeStruct(tangents.shape, jnp.bfloat16)

time: 81 us -> 79.8 us (0.985)
  local copies, waits for them, and re-layouts: 3.79 us -> 2.15 us
    unnamed x12 -> x8, local copies, waits for them, and re-layouts: 3.79 us -> 2.15 us
where the time goes in v8:
time: 79.8 us; the launch traced here: 78.9 us
  waiting for transfers between devices  38.8 us (49%)
  starting transfers between devices  25.6 us (32%)
  Pallas kernels  11.6 us (15%)
  local copies, waits for them, and re-layouts  2.15 us (3%)
    ppermute x6, waiting for transfers between devices, shift(): lax.ppermute(value, axis, [(i, (i + step) % count) for i in range(count)])  22.9 us
    ppermute x13, waiting for transfers between devices, swap(): lax.ppermute(value, axis, [(i, i ^ mask) for i in range(lax.axis_size(axi...  15.7 us
    ppermute x6, starting transfers between devices, shift(): lax.ppermute(value, axis, [(i, (i + step) % count) for i in range(count)])  11.8 us
    ppermute x13, starting transfers between devices, swap(): lax.ppermute(value, axis, [(i, i ^ mask) for i in range(lax.axis_size(axi...  9.34 us
    pallas_call x1, Pallas kernels, on_device(): pl.pallas_call(advance_kernel, out_shape=[jax.ShapeDtypeStruct(tangents.s...  5.66 us
    pallas_call x1, Pallas kernels, on_device(): pl.pallas_call(functools.partial(final_kernel, 1.0 / cells), out_shape=[j...  3.56 us
    ppermute x1, starting transfers between devices, on_device(): l2 = lax.ppermute(lo, 'vec', [(0, 2), (1, 3)])  2.44 us
    unnamed x8, local copies, waits for them, and re-layouts  2.15 us
  transfers between devices with their start and end apart: 22, of which 11 were waited for; matrix products, arithmetic and copies ran while one was open for 0% of the time, Pallas kernels for 3%

profile of v8, /device:TPU:0, one launch (start us, length us, event | category | flops | bytes accessed | tf_op | source)
XLA Modules:
  0.0 78.9 jit_solution(7773730092553647148)
XLA Ops:
  0.6 0.9 %copy-done.2 = bf16[3,4,2,32,128]{4,3,2,1,0:T(8,128)(2,1)S(1)} copy-done((bf16[3,4,2,32,128]{4,3,2,1,0:T(8,128)(2,1)S(1)}, bf16[3,4,2,32,128]{4,3,2,1,0:T(8,128)(2,1)}, u32[]{:S(2)}) %copy-start.2) | copy-done | bytes 196632
  1.6 3.0 %collective-permute-start = (bf16[3,4,32,128]{3,2,1,0:T(8,128)(2,1)S(1)}, bf16[3,4,32,128]{3,2,1,0:T(8,128)(2,1)S(1)}, u32[]{:S(2)}, u32[]{:S(2)}) collective-permute-start(bf16[3,4,32,128]{3,2,1,0:T(8,128)(2,1)S(1)} %get-tuple-element.27), channel_id=1, source_target_pairs={{0,1},{1,2},{2,3},{3,4},{4,5},{5,6},{6,7},{7,0},{8,9},{9,10},{10,1... | collective-permute-start | bytes 294920 | tf_op jit(solution)/shard_map/ppermute | solution.py:253
  4.6 3.1 %collective-permute-start.1 = (bf16[3,4,32,128]{3,2,1,0:T(8,128)(2,1)S(1)}, bf16[3,4,32,128]{3,2,1,0:T(8,128)(2,1)S(1)}, u32[]{:S(2)}, u32[]{:S(2)}) collective-permute-start(bf16[3,4,32,128]{3,2,1,0:T(8,128)(2,1)S(1)} %get-tuple-element.28), channel_id=1, source_target_pairs={{0,7},{1,0},{2,1},{3,2},{4,3},{5,4},{6,5},{7,6},{8,15},{9,8},{10,9... | collective-permute-start | bytes 294920 | tf_op jit(solution)/shard_map/ppermute | solution.py:253
  7.7 1.2 %copy-done = f32[4,2,2,128,128]{4,3,2,1,0:T(8,128)S(1)} copy-done((f32[4,2,2,128,128]{4,3,2,1,0:T(8,128)S(1)}, f32[4,2,2,128,128]{4,3,2,1,0:T(8,128)}, u32[]{:S(2)}) %copy-start) | copy-done | bytes 1048600
  8.9 0.9 %prep.1 = (bf16[2,4,2,128,128]{4,3,2,1,0:T(8,128)(2,1)}, bf16[4,2,128,128]{3,2,1,0:T(8,128)(2,1)}, bf16[4,2,128,128]{3,2,1,0:T(8,128)(2,1)S(1)}) custom-call(f32[4,2,2,128,128]{4,3,2,1,0:T(8,128)S(1)} %copy-done), custom_call_target="tpu_custom_call" | custom-call | tf_op jit(solution)/shard_map/prep/pallas_call | solution.py:267
  9.9 0.7 collective-permute-done.up
  10.5 0.8 collective-permute-done.1.dn
  11.3 1.6 %collective-permute-start.6 = (bf16[12,4,32,128]{3,2,1,0:T(8,128)(2,1)S(1)}, bf16[12,4,32,128]{3,2,1,0:T(8,128)(2,1)S(1)}, u32[]{:S(2)}, u32[]{:S(2)}) collective-permute-start(bf16[12,4,32,128]{3,2,1,0:T(8,128)(2,1)S(1)} %pack.1.bg0), channel_id=1, source_target_pairs={{0,16},{8,24},{16,0},{24,8},{1,17},{9,25},{17,1},{25,9},{2,18},{10... | collective-permute-start | bytes 1179656 | tf_op jit(solution)/shard_map/ppermute | solution.py:257
  12.9 2.9 %collective-permute-start.5 = (bf16[4,2,128,128]{3,2,1,0:T(8,128)(2,1)S(1)}, bf16[4,2,128,128]{3,2,1,0:T(8,128)(2,1)S(1)}, u32[]{:S(2)}, u32[]{:S(2)}) collective-permute-start(bf16[4,2,128,128]{3,2,1,0:T(8,128)(2,1)S(1)} %get-tuple-element.31), channel_id=1, source_target_pairs={{0,6},{1,7},{2,0},{3,1},{4,2},{5,3},{6,4},{7,5},{8,14},{9,15},{10,... | collective-permute-start | bytes 786440 | tf_op jit(solution)/shard_map/ppermute | solution.py:253
  15.8 0.9 %collective-permute-start.3 = (bf16[2,4,2,128,128]{4,3,2,1,0:T(8,128)(2,1)}, bf16[2,4,2,128,128]{4,3,2,1,0:T(8,128)(2,1)S(1)}, u32[]{:S(2)}, u32[]{:S(2)}) collective-permute-start(bf16[2,4,2,128,128]{4,3,2,1,0:T(8,128)(2,1)} %get-tuple-element.29), channel_id=1, source_target_pairs={{0,7},{1,0},{2,1},{3,2},{4,3},{5,4},{6,5},{7,6},{8,15},{9,8},{10,9... | collective-permute-start | bytes 1572872 | tf_op jit(solution)/shard_map/ppermute | solution.py:253
  16.7 1.1 %collective-permute-start.2 = (bf16[2,4,2,128,128]{4,3,2,1,0:T(8,128)(2,1)}, bf16[2,4,2,128,128]{4,3,2,1,0:T(8,128)(2,1)S(1)}, u32[]{:S(2)}, u32[]{:S(2)}) collective-permute-start(bf16[2,4,2,128,128]{4,3,2,1,0:T(8,128)(2,1)} %get-tuple-element.29), channel_id=1, source_target_pairs={{0,1},{1,2},{2,3},{3,4},{4,5},{5,6},{6,7},{7,0},{8,9},{9,10},{10,1... | collective-permute-start | bytes 1572872 | tf_op jit(solution)/shard_map/ppermute | solution.py:253
  17.9 4.7 %collective-permute-done.5.dn2 = bf16[4,2,128,128]{3,2,1,0:T(8,128)(2,1)S(1)} collective-permute-done((bf16[4,2,128,128]{3,2,1,0:T(8,128)(2,1)S(1)}, bf16[4,2,128,128]{3,2,1,0:T(8,128)(2,1)S(1)}, u32[]{:S(2)}, u32[]{:S(2)}) %collective-permute-start.5) | collective-permute-done | bytes 262176 | tf_op jit(solution)/shard_map/ppermute | solution.py:253
  22.6 0.5 collective-permute-start.8
  23.1 0.7 collective-permute-start.4
  23.8 15.4 %collective-permute-done.4.up2 = bf16[4,2,128,128]{3,2,1,0:T(8,128)(2,1)} collective-permute-done((bf16[4,2,128,128]{3,2,1,0:T(8,128)(2,1)}, bf16[4,2,128,128]{3,2,1,0:T(8,128)(2,1)}, u32[]{:S(2)}, u32[]{:S(2)}) %collective-permute-start.4) | collective-permute-done | bytes 262176 | tf_op jit(solution)/shard_map/ppermute | solution.py:253
  39.2 1.4 %collective-permute-done.3.dn1 = bf16[2,4,2,128,128]{4,3,2,1,0:T(8,128)(2,1)S(1)} collective-permute-done((bf16[2,4,2,128,128]{4,3,2,1,0:T(8,128)(2,1)}, bf16[2,4,2,128,128]{4,3,2,1,0:T(8,128)(2,1)S(1)}, u32[]{:S(2)}, u32[]{:S(2)}) %collective-permute-start.3) | collective-permute-done | bytes 524320 | tf_op jit(solution)/shard_map/ppermute | solution.py:253
  40.6 5.7 %advance.1 = (f32[4,2,2,128,128]{4,3,2,1,0:T(8,128)S(1)}, bf16[2,2,2,128,128]{4,3,2,1,0:T(8,128)(2,1)S(1)}, bf16[2,2,2,128,128]{4,3,2,1,0:T(8,128)(2,1)S(1)}, bf16[4,2,2,128,128]{4,3,2,1,0:T(8,128)(2,1)S(1)}) custom-call(s32[1]{0:T(128)} %bitcast.me, f32[4,2,2,128,128]{4,3,2,1,0:T(8,128)S(1)} %copy-done.1, ...), custom_call_target="tpu_custom_call" | custom-call | tf_op jit(solution)/shard_map/advance/pallas_call | solution.py:306
  47.3 1.5 %collective-permute-start.12 = (bf16[2,2,2,128,128]{4,3,2,1,0:T(8,128)(2,1)S(1)}, bf16[2,2,2,128,128]{4,3,2,1,0:T(8,128)(2,1)S(1)}, u32[]{:S(2)}, u32[]{:S(2)}) collective-permute-start(bf16[2,2,2,128,128]{4,3,2,1,0:T(8,128)(2,1)S(1)} %get-tuple-element.38.h0b), channel_id=1, source_target_pairs={{0,16},{8,24},{16,0},{24,8},{1,17},{9,25},{17,1},{25,9},{2,18},{10... | collective-permute-start | bytes 786440 | tf_op jit(solution)/shard_map/ppermute | solution.py:257
  49.3 2.4 %collective-permute-start.18 = (bf16[4,2,2,128,128]{4,3,2,1,0:T(8,128)(2,1)S(1)}, bf16[4,2,2,128,128]{4,3,2,1,0:T(8,128)(2,1)S(1)}, u32[]{:S(2)}, u32[]{:S(2)}) collective-permute-start(bf16[4,2,2,128,128]{4,3,2,1,0:T(8,128)(2,1)S(1)} %get-tuple-element.40), channel_id=1, source_target_pairs={{0,16},{8,24},{1,17},{9,25},{2,18},{10,26},{3,19},{11,27},{4,20},{... | collective-permute-start | bytes 1572872 | tf_op jit(solution)/shard_map/ppermute | solution.py:332
  51.7 4.2 %collective-permute-done.11.h2a = bf16[2,2,2,128,128]{4,3,2,1,0:T(8,128)(2,1)S(1)} collective-permute-done((bf16[2,2,2,128,128]{4,3,2,1,0:T(8,128)(2,1)S(1)}, bf16[2,2,2,128,128]{4,3,2,1,0:T(8,128)(2,1)S(1)}, u32[]{:S(2)}, u32[]{:S(2)}) %collective-permute-start.11) | collective-permute-done | bytes 262176 | tf_op jit(solution)/shard_map/ppermute | solution.py:257
  56.0 4.7 %collective-permute-done.12.h2b = bf16[2,2,2,128,128]{4,3,2,1,0:T(8,128)(2,1)S(1)} collective-permute-done((bf16[2,2,2,128,128]{4,3,2,1,0:T(8,128)(2,1)S(1)}, bf16[2,2,2,128,128]{4,3,2,1,0:T(8,128)(2,1)S(1)}, u32[]{:S(2)}, u32[]{:S(2)}) %collective-permute-start.12) | collective-permute-done | bytes 262176 | tf_op jit(solution)/shard_map/ppermute | solution.py:257
  60.7 1.5 %collective-permute-done.14.h3b = bf16[2,2,2,128,128]{4,3,2,1,0:T(8,128)(2,1)S(1)} collective-permute-done((bf16[2,2,2,128,128]{4,3,2,1,0:T(8,128)(2,1)S(1)}, bf16[2,2,2,128,128]{4,3,2,1,0:T(8,128)(2,1)S(1)}, u32[]{:S(2)}, u32[]{:S(2)}) %collective-permute-start.14) | collective-permute-done | bytes 262176 | tf_op jit(solution)/shard_map/ppermute | solution.py:257
  62.3 0.9 %gram.1 = f32[16,16]{1,0:T(8,128)S(1)} custom-call(s32[1]{0:T(128)} %bitcast.me, f32[8,128]{1,0:T(8,128)S(1)} %gram_own.1.near, bf16[2,2,2,128,128]{4,3,2,1,0:T(8,128)(2,1)S(1)} %get-tuple-element.37.h0a, bf16[2,2,2,128,128]{4,3,2,1,0:T(8,128)(2,1)S(1)} %get-tuple-element.38.h0b, bf16[2,2,2,128,128]{4,3,2,1,0:T(8,128)(2,1)S(1)} %collective-permute-done.9.h1a, ...), custom_call_target="tpu_custom_call" | custom-call | tf_op jit(solution)/shard_map/gram/pallas_call | solution.py:337
  63.2 1.0 %collective-permute-start.17 = (f32[16,16]{1,0:T(8,128)S(1)}, f32[16,16]{1,0:T(8,128)S(1)}, u32[]{:S(2)}, u32[]{:S(2)}) collective-permute-start(f32[16,16]{1,0:T(8,128)S(1)} %gram.1), channel_id=1, source_target_pairs={{0,3},{1,2},{2,1},{3,0},{4,7},{5,6},{6,5},{7,4},{8,11},{9,10},{10,... | collective-permute-start | bytes 3080 | tf_op jit(solution)/shard_map/ppermute | solution.py:257
  64.2 2.0 %collective-permute-start.16 = (f32[16,16]{1,0:T(8,128)S(1)}, f32[16,16]{1,0:T(8,128)S(1)}, u32[]{:S(2)}, u32[]{:S(2)}) collective-permute-start(f32[16,16]{1,0:T(8,128)S(1)} %gram.1), channel_id=1, source_target_pairs={{0,2},{1,3},{2,0},{3,1},{4,6},{5,7},{6,4},{7,5},{8,10},{9,11},{10,... | collective-permute-start | bytes 3080 | tf_op jit(solution)/shard_map/ppermute | solution.py:257
  66.1 0.6 collective-permute-start.15
  66.7 1.3 %collective-permute-start.20 = (bf16[4,2,2,128,128]{4,3,2,1,0:T(8,128)(2,1)S(1)}, bf16[4,2,2,128,128]{4,3,2,1,0:T(8,128)(2,1)S(1)}, u32[]{:S(2)}, u32[]{:S(2)}) collective-permute-start(bf16[4,2,2,128,128]{4,3,2,1,0:T(8,128)(2,1)S(1)} %get-tuple-element.40), channel_id=1, source_target_pairs={{0,8},{16,24},{1,9},{17,25},{2,10},{18,26},{3,11},{19,27},{4,12},{... | collective-permute-start | bytes 1572872 | tf_op jit(solution)/shard_map/ppermute | solution.py:333
  68.0 1.8 %collective-permute-done.15 = f32[16,16]{1,0:T(8,128)S(1)} collective-permute-done((f32[16,16]{1,0:T(8,128)S(1)}, f32[16,16]{1,0:T(8,128)S(1)}, u32[]{:S(2)}, u32[]{:S(2)}) %collective-permute-start.15) | collective-permute-done | bytes 1056 | tf_op jit(solution)/shard_map/ppermute | solution.py:257
  70.0 0.7 collective-permute-start.21
  70.7 1.1 %collective-permute-start.19 = (f32[16,16]{1,0:T(8,128)S(1)}, f32[16,16]{1,0:T(8,128)S(1)}, u32[]{:S(2)}, u32[]{:S(2)}) collective-permute-start(f32[16,16]{1,0:T(8,128)S(1)} %add_add_fusion), channel_id=1, source_target_pairs={{0,4},{1,5},{2,6},{3,7},{4,0},{5,1},{6,2},{7,3},{8,12},{9,13},{10,... | collective-permute-start | bytes 3080 | tf_op jit(solution)/shard_map/ppermute | solution.py:257
  71.8 3.5 %collective-permute-done.19 = f32[16,16]{1,0:T(8,128)S(1)} collective-permute-done((f32[16,16]{1,0:T(8,128)S(1)}, f32[16,16]{1,0:T(8,128)S(1)}, u32[]{:S(2)}, u32[]{:S(2)}) %collective-permute-start.19) | collective-permute-done | bytes 1056 | tf_op jit(solution)/shard_map/ppermute | solution.py:257
  75.3 3.6 %final.1 = (f32[4,2,2,128,128]{4,3,2,1,0:T(8,128)}, f32[1,16]{1,0:T(1,128)}) custom-call(s32[1]{0:T(128)} %bitcast.me, f32[16,16]{1,0:T(8,128)S(1)} %add.15.gram, f32[4,2,2,128,128]{4,3,2,1,0:T(8,128)S(1)} %get-tuple-element.42.own, bf16[2,2,2,128,128]{4,3,2,1,0:T(8,128)(2,1)S(1)} %collective-permute-done.9.h1a, ...), custom_call_target="tpu_custom_call" | custom-call | tf_op jit(solution)/shard_map/final/pallas_call | solution.py:358
  (29 shorter events, 1.8 us)
Async XLA Ops:
  0.6 0.9 %copy-start.2 = (bf16[3,4,2,32,128]{4,3,2,1,0:T(8,128)(2,1)S(1)}, bf16[3,4,2,32,128]{4,3,2,1,0:T(8,128)(2,1)}, u32[]{:S(2)}) copy-start(bf16[3,4,2,32,128]{4,3,2,1,0:T(8,128)(2,1)} %background.3) | copy-start | bytes 589828
  1.6 9.7 %copy-start.3 = (bf16[3,4,2,32,128]{4,3,2,1,0:T(8,128)(2,1)S(1)}, bf16[3,4,2,32,128]{4,3,2,1,0:T(8,128)(2,1)}, u32[]{:S(2)}) copy-start(bf16[3,4,2,32,128]{4,3,2,1,0:T(8,128)(2,1)} %background.3) | copy-start | bytes 589828
  1.6 8.9 %collective-permute-start = (bf16[3,4,32,128]{3,2,1,0:T(8,128)(2,1)S(1)}, bf16[3,4,32,128]{3,2,1,0:T(8,128)(2,1)S(1)}, u32[]{:S(2)}, u32[]{:S(2)}) collective-permute-start(bf16[3,4,32,128]{3,2,1,0:T(8,128)(2,1)S(1)} %get-tuple-element.27), channel_id=1, source_target_pairs={{0,1},{1,2},{2,3},{3,4},{4,5},{5,6},{6,7},{7,0},{8,9},{9,10},{10,1... | collective-permute-start | bytes 294920 | tf_op jit(solution)/shard_map/ppermute | solution.py:253
  4.6 6.7 %collective-permute-start.1 = (bf16[3,4,32,128]{3,2,1,0:T(8,128)(2,1)S(1)}, bf16[3,4,32,128]{3,2,1,0:T(8,128)(2,1)S(1)}, u32[]{:S(2)}, u32[]{:S(2)}) collective-permute-start(bf16[3,4,32,128]{3,2,1,0:T(8,128)(2,1)S(1)} %get-tuple-element.28), channel_id=1, source_target_pairs={{0,7},{1,0},{2,1},{3,2},{4,3},{5,4},{6,5},{7,6},{8,15},{9,8},{10,9... | collective-permute-start | bytes 294920 | tf_op jit(solution)/shard_map/ppermute | solution.py:253
  7.7 1.2 %copy-start = (f32[4,2,2,128,128]{4,3,2,1,0:T(8,128)S(1)}, f32[4,2,2,128,128]{4,3,2,1,0:T(8,128)}, u32[]{:S(2)}) copy-start(f32[4,2,2,128,128]{4,3,2,1,0:T(8,128)} %own.3) | copy-start | bytes 3145732
  8.9 31.7 %copy-start.1 = (f32[4,2,2,128,128]{4,3,2,1,0:T(8,128)S(1)}, f32[4,2,2,128,128]{4,3,2,1,0:T(8,128)}, u32[]{:S(2)}) copy-start(f32[4,2,2,128,128]{4,3,2,1,0:T(8,128)} %own.3) | copy-start | bytes 3145732
  11.3 11.2 %collective-permute-start.6 = (bf16[12,4,32,128]{3,2,1,0:T(8,128)(2,1)S(1)}, bf16[12,4,32,128]{3,2,1,0:T(8,128)(2,1)S(1)}, u32[]{:S(2)}, u32[]{:S(2)}) collective-permute-start(bf16[12,4,32,128]{3,2,1,0:T(8,128)(2,1)S(1)} %pack.1.bg0), channel_id=1, source_target_pairs={{0,16},{8,24},{16,0},{24,8},{1,17},{9,25},{17,1},{25,9},{2,18},{10... | collective-permute-start | bytes 1179656 | tf_op jit(solution)/shard_map/ppermute | solution.py:257
  12.9 9.7 %collective-permute-start.5 = (bf16[4,2,128,128]{3,2,1,0:T(8,128)(2,1)S(1)}, bf16[4,2,128,128]{3,2,1,0:T(8,128)(2,1)S(1)}, u32[]{:S(2)}, u32[]{:S(2)}) collective-permute-start(bf16[4,2,128,128]{3,2,1,0:T(8,128)(2,1)S(1)} %get-tuple-element.31), channel_id=1, source_target_pairs={{0,6},{1,7},{2,0},{3,1},{4,2},{5,3},{6,4},{7,5},{8,14},{9,15},{10,... | collective-permute-start | bytes 786440 | tf_op jit(solution)/shard_map/ppermute | solution.py:253
  15.8 24.7 %collective-permute-start.3 = (bf16[2,4,2,128,128]{4,3,2,1,0:T(8,128)(2,1)}, bf16[2,4,2,128,128]{4,3,2,1,0:T(8,128)(2,1)S(1)}, u32[]{:S(2)}, u32[]{:S(2)}) collective-permute-start(bf16[2,4,2,128,128]{4,3,2,1,0:T(8,128)(2,1)} %get-tuple-element.29), channel_id=1, source_target_pairs={{0,7},{1,0},{2,1},{3,2},{4,3},{5,4},{6,5},{7,6},{8,15},{9,8},{10,9... | collective-permute-start | bytes 1572872 | tf_op jit(solution)/shard_map/ppermute | solution.py:253
  16.7 23.8 %collective-permute-start.2 = (bf16[2,4,2,128,128]{4,3,2,1,0:T(8,128)(2,1)}, bf16[2,4,2,128,128]{4,3,2,1,0:T(8,128)(2,1)S(1)}, u32[]{:S(2)}, u32[]{:S(2)}) collective-permute-start(bf16[2,4,2,128,128]{4,3,2,1,0:T(8,128)(2,1)} %get-tuple-element.29), channel_id=1, source_target_pairs={{0,1},{1,2},{2,3},{3,4},{4,5},{5,6},{6,7},{7,0},{8,9},{9,10},{10,1... | collective-permute-start | bytes 1572872 | tf_op jit(solution)/shard_map/ppermute | solution.py:253
  22.6 18.0 %collective-permute-start.7 = (bf16[12,4,32,128]{3,2,1,0:T(8,128)(2,1)S(1)}, bf16[12,4,32,128]{3,2,1,0:T(8,128)(2,1)S(1)}, u32[]{:S(2)}, u32[]{:S(2)}) collective-permute-start(bf16[12,4,32,128]{3,2,1,0:T(8,128)(2,1)S(1)} %pack.1.bg0), channel_id=1, source_target_pairs={{0,8},{8,0},{16,24},{24,16},{1,9},{9,1},{17,25},{25,17},{2,10},{10... | collective-permute-start | bytes 1179656 | tf_op jit(solution)/shard_map/ppermute | solution.py:257
  22.6 18.0 %collective-permute-start.8 = (bf16[12,4,32,128]{3,2,1,0:T(8,128)(2,1)S(1)}, bf16[12,4,32,128]{3,2,1,0:T(8,128)(2,1)}, u32[]{:S(2)}, u32[]{:S(2)}) collective-permute-start(bf16[12,4,32,128]{3,2,1,0:T(8,128)(2,1)S(1)} %collective-permute-done.6.bg2), channel_id=1, source_target_pairs={{0,8},{8,0},{16,24},{24,16},{1,9},{9,1},{17,25},{25,17},{2,10},{10... | collective-permute-start | bytes 1179656 | tf_op jit(solution)/shard_map/ppermute | solution.py:257
  23.1 16.1 %collective-permute-start.4 = (bf16[4,2,128,128]{3,2,1,0:T(8,128)(2,1)}, bf16[4,2,128,128]{3,2,1,0:T(8,128)(2,1)}, u32[]{:S(2)}, u32[]{:S(2)}) collective-permute-start(bf16[4,2,128,128]{3,2,1,0:T(8,128)(2,1)} %get-tuple-element.30), channel_id=1, source_target_pairs={{0,2},{1,3},{2,4},{3,5},{4,6},{5,7},{6,0},{7,1},{8,10},{9,11},{10,... | collective-permute-start | bytes 786440 | tf_op jit(solution)/shard_map/ppermute | solution.py:253
  46.2 2.6 %collective-permute-start.9 = (bf16[2,2,2,128,128]{4,3,2,1,0:T(8,128)(2,1)S(1)}, bf16[2,2,2,128,128]{4,3,2,1,0:T(8,128)(2,1)S(1)}, u32[]{:S(2)}, u32[]{:S(2)}) collective-permute-start(bf16[2,2,2,128,128]{4,3,2,1,0:T(8,128)(2,1)S(1)} %get-tuple-element.37.h0a), channel_id=1, source_target_pairs={{0,8},{8,0},{16,24},{24,16},{1,9},{9,1},{17,25},{25,17},{2,10},{10... | collective-permute-start | bytes 786440 | tf_op jit(solution)/shard_map/ppermute | solution.py:257
  46.3 2.5 %collective-permute-start.10 = (bf16[2,2,2,128,128]{4,3,2,1,0:T(8,128)(2,1)S(1)}, bf16[2,2,2,128,128]{4,3,2,1,0:T(8,128)(2,1)S(1)}, u32[]{:S(2)}, u32[]{:S(2)}) collective-permute-start(bf16[2,2,2,128,128]{4,3,2,1,0:T(8,128)(2,1)S(1)} %get-tuple-element.38.h0b), channel_id=1, source_target_pairs={{0,8},{8,0},{16,24},{24,16},{1,9},{9,1},{17,25},{25,17},{2,10},{10... | collective-permute-start | bytes 786440 | tf_op jit(solution)/shard_map/ppermute | solution.py:257
  46.8 9.2 %collective-permute-start.11 = (bf16[2,2,2,128,128]{4,3,2,1,0:T(8,128)(2,1)S(1)}, bf16[2,2,2,128,128]{4,3,2,1,0:T(8,128)(2,1)S(1)}, u32[]{:S(2)}, u32[]{:S(2)}) collective-permute-start(bf16[2,2,2,128,128]{4,3,2,1,0:T(8,128)(2,1)S(1)} %get-tuple-element.37.h0a), channel_id=1, source_target_pairs={{0,16},{8,24},{16,0},{24,8},{1,17},{9,25},{17,1},{25,9},{2,18},{10... | collective-permute-start | bytes 786440 | tf_op jit(solution)/shard_map/ppermute | solution.py:257
  47.3 13.4 %collective-permute-start.12 = (bf16[2,2,2,128,128]{4,3,2,1,0:T(8,128)(2,1)S(1)}, bf16[2,2,2,128,128]{4,3,2,1,0:T(8,128)(2,1)S(1)}, u32[]{:S(2)}, u32[]{:S(2)}) collective-permute-start(bf16[2,2,2,128,128]{4,3,2,1,0:T(8,128)(2,1)S(1)} %get-tuple-element.38.h0b), channel_id=1, source_target_pairs={{0,16},{8,24},{16,0},{24,8},{1,17},{9,25},{17,1},{25,9},{2,18},{10... | collective-permute-start | bytes 786440 | tf_op jit(solution)/shard_map/ppermute | solution.py:257
  49.3 20.7 %collective-permute-start.18 = (bf16[4,2,2,128,128]{4,3,2,1,0:T(8,128)(2,1)S(1)}, bf16[4,2,2,128,128]{4,3,2,1,0:T(8,128)(2,1)S(1)}, u32[]{:S(2)}, u32[]{:S(2)}) collective-permute-start(bf16[4,2,2,128,128]{4,3,2,1,0:T(8,128)(2,1)S(1)} %get-tuple-element.40), channel_id=1, source_target_pairs={{0,16},{8,24},{1,17},{9,25},{2,18},{10,26},{3,19},{11,27},{4,20},{... | collective-permute-start | bytes 1572872 | tf_op jit(solution)/shard_map/ppermute | solution.py:332
  56.0 4.8 %collective-permute-start.13 = (bf16[2,2,2,128,128]{4,3,2,1,0:T(8,128)(2,1)S(1)}, bf16[2,2,2,128,128]{4,3,2,1,0:T(8,128)(2,1)S(1)}, u32[]{:S(2)}, u32[]{:S(2)}) collective-permute-start(bf16[2,2,2,128,128]{4,3,2,1,0:T(8,128)(2,1)S(1)} %collective-permute-done.11.h2a), channel_id=1, source_target_pairs={{0,8},{8,0},{16,24},{24,16},{1,9},{9,1},{17,25},{25,17},{2,10},{10... | collective-permute-start | bytes 786440 | tf_op jit(solution)/shard_map/ppermute | solution.py:257
  60.7 1.5 %collective-permute-start.14 = (bf16[2,2,2,128,128]{4,3,2,1,0:T(8,128)(2,1)S(1)}, bf16[2,2,2,128,128]{4,3,2,1,0:T(8,128)(2,1)S(1)}, u32[]{:S(2)}, u32[]{:S(2)}) collective-permute-start(bf16[2,2,2,128,128]{4,3,2,1,0:T(8,128)(2,1)S(1)} %collective-permute-done.12.h2b), channel_id=1, source_target_pairs={{0,8},{8,0},{16,24},{24,16},{1,9},{9,1},{17,25},{25,17},{2,10},{10... | collective-permute-start | bytes 786440 | tf_op jit(solution)/shard_map/ppermute | solution.py:257
  63.2 4.8 %collective-permute-start.17 = (f32[16,16]{1,0:T(8,128)S(1)}, f32[16,16]{1,0:T(8,128)S(1)}, u32[]{:S(2)}, u32[]{:S(2)}) collective-permute-start(f32[16,16]{1,0:T(8,128)S(1)} %gram.1), channel_id=1, source_target_pairs={{0,3},{1,2},{2,1},{3,0},{4,7},{5,6},{6,5},{7,4},{8,11},{9,10},{10,... | collective-permute-start | bytes 3080 | tf_op jit(solution)/shard_map/ppermute | solution.py:257
  64.2 3.9 %collective-permute-start.16 = (f32[16,16]{1,0:T(8,128)S(1)}, f32[16,16]{1,0:T(8,128)S(1)}, u32[]{:S(2)}, u32[]{:S(2)}) collective-permute-start(f32[16,16]{1,0:T(8,128)S(1)} %gram.1), channel_id=1, source_target_pairs={{0,2},{1,3},{2,0},{3,1},{4,6},{5,7},{6,4},{7,5},{8,10},{9,11},{10,... | collective-permute-start | bytes 3080 | tf_op jit(solution)/shard_map/ppermute | solution.py:257
  66.1 3.7 %collective-permute-start.15 = (f32[16,16]{1,0:T(8,128)S(1)}, f32[16,16]{1,0:T(8,128)S(1)}, u32[]{:S(2)}, u32[]{:S(2)}) collective-permute-start(f32[16,16]{1,0:T(8,128)S(1)} %gram.1), channel_id=1, source_target_pairs={{0,1},{1,0},{2,3},{3,2},{4,5},{5,4},{6,7},{7,6},{8,9},{9,8},{10,11... | collective-permute-start | bytes 3080 | tf_op jit(solution)/shard_map/ppermute | solution.py:257
  66.7 8.6 %collective-permute-start.20 = (bf16[4,2,2,128,128]{4,3,2,1,0:T(8,128)(2,1)S(1)}, bf16[4,2,2,128,128]{4,3,2,1,0:T(8,128)(2,1)S(1)}, u32[]{:S(2)}, u32[]{:S(2)}) collective-permute-start(bf16[4,2,2,128,128]{4,3,2,1,0:T(8,128)(2,1)S(1)} %get-tuple-element.40), channel_id=1, source_target_pairs={{0,8},{16,24},{1,9},{17,25},{2,10},{18,26},{3,11},{19,27},{4,12},{... | collective-permute-start | bytes 1572872 | tf_op jit(solution)/shard_map/ppermute | solution.py:333
  70.0 5.3 %collective-permute-start.21 = (bf16[4,2,2,128,128]{4,3,2,1,0:T(8,128)(2,1)S(1)}, bf16[4,2,2,128,128]{4,3,2,1,0:T(8,128)(2,1)S(1)}, u32[]{:S(2)}, u32[]{:S(2)}) collective-permute-start(bf16[4,2,2,128,128]{4,3,2,1,0:T(8,128)(2,1)S(1)} %collective-permute-done.18.l2), channel_id=1, source_target_pairs={{16,24},{24,16},{17,25},{25,17},{18,26},{26,18},{19,27},{27,19},{2... | collective-permute-start | bytes 1572872 | tf_op jit(solution)/shard_map/ppermute | solution.py:350
  70.7 4.6 %collective-permute-start.19 = (f32[16,16]{1,0:T(8,128)S(1)}, f32[16,16]{1,0:T(8,128)S(1)}, u32[]{:S(2)}, u32[]{:S(2)}) collective-permute-start(f32[16,16]{1,0:T(8,128)S(1)} %add_add_fusion), channel_id=1, source_target_pairs={{0,4},{1,5},{2,6},{3,7},{4,0},{5,1},{6,2},{7,3},{8,12},{9,13},{10,... | collective-permute-start | bytes 3080 | tf_op jit(solution)/shard_map/ppermute | solution.py:257

commit v9 on v8

--- a/solution.py
+++ b/solution.py
@@ -297,8 +297,8 @@
         name="pack",
     )(background, bg_up, bg_dn)
     bg2 = swap(packed, "vec", 2)
-    near_bg, far_bg, _ = lax.optimization_barrier((packed, bg2, dn2))
-    bgs = [packed, swap(near_bg, "vec", 1), bg2, swap(far_bg, "vec", 1)]
+    far_bg, _ = lax.optimization_barrier((bg2, dn2))
+    bgs = [packed, swap(packed, "vec", 1), bg2, swap(far_bg, "vec", 1)]
 
     low = jax.ShapeDtypeStruct(tangents.shape, jnp.bfloat16)
     pair = jax.ShapeDtypeStruct((vectors // 2,) + tangents.shape[1:], jnp.bfloat16)

time: 79.8 us -> 79.8 us (level)
  no operation moved by 1% of the time
where the time goes in v9:
time: 79.8 us; the launch traced here: 78.8 us
  waiting for transfers between devices  39.3 us (49%)
  starting transfers between devices  25.1 us (31%)
  Pallas kernels  11.6 us (15%)
  local copies, waits for them, and re-layouts  2.15 us (3%)
    ppermute x6, waiting for transfers between devices, shift(): lax.ppermute(value, axis, [(i, (i + step) % count) for i in range(count)])  23.4 us
    ppermute x13, waiting for transfers between devices, swap(): lax.ppermute(value, axis, [(i, i ^ mask) for i in range(lax.axis_size(axi...  15.7 us
    ppermute x6, starting transfers between devices, shift(): lax.ppermute(value, axis, [(i, (i + step) % count) for i in range(count)])  11.8 us
    ppermute x13, starting transfers between devices, swap(): lax.ppermute(value, axis, [(i, i ^ mask) for i in range(lax.axis_size(axi...  8.85 us
    pallas_call x1, Pallas kernels, on_device(): pl.pallas_call(advance_kernel, out_shape=[jax.ShapeDtypeStruct(tangents.s...  5.66 us
    pallas_call x1, Pallas kernels, on_device(): pl.pallas_call(functools.partial(final_kernel, 1.0 / cells), out_shape=[j...  3.56 us
    ppermute x1, starting transfers between devices, on_device(): l2 = lax.ppermute(lo, 'vec', [(0, 2), (1, 3)])  2.45 us
    unnamed x8, local copies, waits for them, and re-layouts  2.15 us
  transfers between devices with their start and end apart: 22, of which 11 were waited for; matrix products, arithmetic and copies ran while one was open for 0% of the time, Pallas kernels for 3%

profile of v9, /device:TPU:0, one launch (start us, length us, event | category | flops | bytes accessed | tf_op | source)
XLA Modules:
  0.0 78.8 jit_solution(9722227386481575374)
XLA Ops:
  0.6 0.9 %copy-done.2 = bf16[3,4,2,32,128]{4,3,2,1,0:T(8,128)(2,1)S(1)} copy-done((bf16[3,4,2,32,128]{4,3,2,1,0:T(8,128)(2,1)S(1)}, bf16[3,4,2,32,128]{4,3,2,1,0:T(8,128)(2,1)}, u32[]{:S(2)}) %copy-start.2) | copy-done | bytes 196632
  1.6 3.0 %collective-permute-start = (bf16[3,4,32,128]{3,2,1,0:T(8,128)(2,1)S(1)}, bf16[3,4,32,128]{3,2,1,0:T(8,128)(2,1)S(1)}, u32[]{:S(2)}, u32[]{:S(2)}) collective-permute-start(bf16[3,4,32,128]{3,2,1,0:T(8,128)(2,1)S(1)} %get-tuple-element.26), channel_id=1, source_target_pairs={{0,1},{1,2},{2,3},{3,4},{4,5},{5,6},{6,7},{7,0},{8,9},{9,10},{10,1... | collective-permute-start | bytes 294920 | tf_op jit(solution)/shard_map/ppermute | solution.py:253
  4.6 3.1 %collective-permute-start.1 = (bf16[3,4,32,128]{3,2,1,0:T(8,128)(2,1)S(1)}, bf16[3,4,32,128]{3,2,1,0:T(8,128)(2,1)S(1)}, u32[]{:S(2)}, u32[]{:S(2)}) collective-permute-start(bf16[3,4,32,128]{3,2,1,0:T(8,128)(2,1)S(1)} %get-tuple-element.27), channel_id=1, source_target_pairs={{0,7},{1,0},{2,1},{3,2},{4,3},{5,4},{6,5},{7,6},{8,15},{9,8},{10,9... | collective-permute-start | bytes 294920 | tf_op jit(solution)/shard_map/ppermute | solution.py:253
  7.7 1.2 %copy-done = f32[4,2,2,128,128]{4,3,2,1,0:T(8,128)S(1)} copy-done((f32[4,2,2,128,128]{4,3,2,1,0:T(8,128)S(1)}, f32[4,2,2,128,128]{4,3,2,1,0:T(8,128)}, u32[]{:S(2)}) %copy-start) | copy-done | bytes 1048600
  8.9 0.9 %prep.1 = (bf16[2,4,2,128,128]{4,3,2,1,0:T(8,128)(2,1)}, bf16[4,2,128,128]{3,2,1,0:T(8,128)(2,1)}, bf16[4,2,128,128]{3,2,1,0:T(8,128)(2,1)S(1)}) custom-call(f32[4,2,2,128,128]{4,3,2,1,0:T(8,128)S(1)} %copy-done), custom_call_target="tpu_custom_call" | custom-call | tf_op jit(solution)/shard_map/prep/pallas_call | solution.py:267
  9.9 0.7 collective-permute-done.up
  10.5 0.8 collective-permute-done.1.dn
  11.3 1.6 %collective-permute-start.7 = (bf16[12,4,32,128]{3,2,1,0:T(8,128)(2,1)S(1)}, bf16[12,4,32,128]{3,2,1,0:T(8,128)(2,1)S(1)}, u32[]{:S(2)}, u32[]{:S(2)}) collective-permute-start(bf16[12,4,32,128]{3,2,1,0:T(8,128)(2,1)S(1)} %pack.1.bg0), channel_id=1, source_target_pairs={{0,16},{8,24},{16,0},{24,8},{1,17},{9,25},{17,1},{25,9},{2,18},{10... | collective-permute-start | bytes 1179656 | tf_op jit(solution)/shard_map/ppermute | solution.py:257
  12.9 2.9 %collective-permute-start.5 = (bf16[4,2,128,128]{3,2,1,0:T(8,128)(2,1)S(1)}, bf16[4,2,128,128]{3,2,1,0:T(8,128)(2,1)S(1)}, u32[]{:S(2)}, u32[]{:S(2)}) collective-permute-start(bf16[4,2,128,128]{3,2,1,0:T(8,128)(2,1)S(1)} %get-tuple-element.30), channel_id=1, source_target_pairs={{0,6},{1,7},{2,0},{3,1},{4,2},{5,3},{6,4},{7,5},{8,14},{9,15},{10,... | collective-permute-start | bytes 786440 | tf_op jit(solution)/shard_map/ppermute | solution.py:253
  15.8 0.9 %collective-permute-start.3 = (bf16[2,4,2,128,128]{4,3,2,1,0:T(8,128)(2,1)}, bf16[2,4,2,128,128]{4,3,2,1,0:T(8,128)(2,1)S(1)}, u32[]{:S(2)}, u32[]{:S(2)}) collective-permute-start(bf16[2,4,2,128,128]{4,3,2,1,0:T(8,128)(2,1)} %get-tuple-element.28), channel_id=1, source_target_pairs={{0,7},{1,0},{2,1},{3,2},{4,3},{5,4},{6,5},{7,6},{8,15},{9,8},{10,9... | collective-permute-start | bytes 1572872 | tf_op jit(solution)/shard_map/ppermute | solution.py:253
  16.7 1.1 %collective-permute-start.2 = (bf16[2,4,2,128,128]{4,3,2,1,0:T(8,128)(2,1)}, bf16[2,4,2,128,128]{4,3,2,1,0:T(8,128)(2,1)S(1)}, u32[]{:S(2)}, u32[]{:S(2)}) collective-permute-start(bf16[2,4,2,128,128]{4,3,2,1,0:T(8,128)(2,1)} %get-tuple-element.28), channel_id=1, source_target_pairs={{0,1},{1,2},{2,3},{3,4},{4,5},{5,6},{6,7},{7,0},{8,9},{9,10},{10,1... | collective-permute-start | bytes 1572872 | tf_op jit(solution)/shard_map/ppermute | solution.py:253
  17.9 4.7 %collective-permute-done.5.dn2 = bf16[4,2,128,128]{3,2,1,0:T(8,128)(2,1)S(1)} collective-permute-done((bf16[4,2,128,128]{3,2,1,0:T(8,128)(2,1)S(1)}, bf16[4,2,128,128]{3,2,1,0:T(8,128)(2,1)S(1)}, u32[]{:S(2)}, u32[]{:S(2)}) %collective-permute-start.5) | collective-permute-done | bytes 262176 | tf_op jit(solution)/shard_map/ppermute | solution.py:253
  22.6 0.7 collective-permute-start.4
  23.3 15.9 %collective-permute-done.4.up2 = bf16[4,2,128,128]{3,2,1,0:T(8,128)(2,1)} collective-permute-done((bf16[4,2,128,128]{3,2,1,0:T(8,128)(2,1)}, bf16[4,2,128,128]{3,2,1,0:T(8,128)(2,1)}, u32[]{:S(2)}, u32[]{:S(2)}) %collective-permute-start.4) | collective-permute-done | bytes 262176 | tf_op jit(solution)/shard_map/ppermute | solution.py:253
  39.2 1.4 %collective-permute-done.3.dn1 = bf16[2,4,2,128,128]{4,3,2,1,0:T(8,128)(2,1)S(1)} collective-permute-done((bf16[2,4,2,128,128]{4,3,2,1,0:T(8,128)(2,1)}, bf16[2,4,2,128,128]{4,3,2,1,0:T(8,128)(2,1)S(1)}, u32[]{:S(2)}, u32[]{:S(2)}) %collective-permute-start.3) | collective-permute-done | bytes 524320 | tf_op jit(solution)/shard_map/ppermute | solution.py:253
  40.6 5.7 %advance.1 = (f32[4,2,2,128,128]{4,3,2,1,0:T(8,128)S(1)}, bf16[2,2,2,128,128]{4,3,2,1,0:T(8,128)(2,1)S(1)}, bf16[2,2,2,128,128]{4,3,2,1,0:T(8,128)(2,1)S(1)}, bf16[4,2,2,128,128]{4,3,2,1,0:T(8,128)(2,1)S(1)}) custom-call(s32[1]{0:T(128)} %bitcast.me, f32[4,2,2,128,128]{4,3,2,1,0:T(8,128)S(1)} %copy-done.1, ...), custom_call_target="tpu_custom_call" | custom-call | tf_op jit(solution)/shard_map/advance/pallas_call | solution.py:306
  46.8 0.5 collective-permute-start.11
  47.3 1.5 %collective-permute-start.12 = (bf16[2,2,2,128,128]{4,3,2,1,0:T(8,128)(2,1)S(1)}, bf16[2,2,2,128,128]{4,3,2,1,0:T(8,128)(2,1)S(1)}, u32[]{:S(2)}, u32[]{:S(2)}) collective-permute-start(bf16[2,2,2,128,128]{4,3,2,1,0:T(8,128)(2,1)S(1)} %get-tuple-element.36.h0b), channel_id=1, source_target_pairs={{0,16},{8,24},{16,0},{24,8},{1,17},{9,25},{17,1},{25,9},{2,18},{10... | collective-permute-start | bytes 786440 | tf_op jit(solution)/shard_map/ppermute | solution.py:257
  49.3 2.4 %collective-permute-start.18 = (bf16[4,2,2,128,128]{4,3,2,1,0:T(8,128)(2,1)S(1)}, bf16[4,2,2,128,128]{4,3,2,1,0:T(8,128)(2,1)S(1)}, u32[]{:S(2)}, u32[]{:S(2)}) collective-permute-start(bf16[4,2,2,128,128]{4,3,2,1,0:T(8,128)(2,1)S(1)} %get-tuple-element.38), channel_id=1, source_target_pairs={{0,16},{8,24},{1,17},{9,25},{2,18},{10,26},{3,19},{11,27},{4,20},{... | collective-permute-start | bytes 1572872 | tf_op jit(solution)/shard_map/ppermute | solution.py:332
  51.7 4.2 %collective-permute-done.11.h2a = bf16[2,2,2,128,128]{4,3,2,1,0:T(8,128)(2,1)S(1)} collective-permute-done((bf16[2,2,2,128,128]{4,3,2,1,0:T(8,128)(2,1)S(1)}, bf16[2,2,2,128,128]{4,3,2,1,0:T(8,128)(2,1)S(1)}, u32[]{:S(2)}, u32[]{:S(2)}) %collective-permute-start.11) | collective-permute-done | bytes 262176 | tf_op jit(solution)/shard_map/ppermute | solution.py:257
  56.0 4.7 %collective-permute-done.12.h2b = bf16[2,2,2,128,128]{4,3,2,1,0:T(8,128)(2,1)S(1)} collective-permute-done((bf16[2,2,2,128,128]{4,3,2,1,0:T(8,128)(2,1)S(1)}, bf16[2,2,2,128,128]{4,3,2,1,0:T(8,128)(2,1)S(1)}, u32[]{:S(2)}, u32[]{:S(2)}) %collective-permute-start.12) | collective-permute-done | bytes 262176 | tf_op jit(solution)/shard_map/ppermute | solution.py:257
  60.7 1.5 %collective-permute-done.14.h3b = bf16[2,2,2,128,128]{4,3,2,1,0:T(8,128)(2,1)S(1)} collective-permute-done((bf16[2,2,2,128,128]{4,3,2,1,0:T(8,128)(2,1)S(1)}, bf16[2,2,2,128,128]{4,3,2,1,0:T(8,128)(2,1)S(1)}, u32[]{:S(2)}, u32[]{:S(2)}) %collective-permute-start.14) | collective-permute-done | bytes 262176 | tf_op jit(solution)/shard_map/ppermute | solution.py:257
  62.2 0.9 %gram.1 = f32[16,16]{1,0:T(8,128)S(1)} custom-call(s32[1]{0:T(128)} %bitcast.me, f32[8,128]{1,0:T(8,128)S(1)} %gram_own.1.near, bf16[2,2,2,128,128]{4,3,2,1,0:T(8,128)(2,1)S(1)} %get-tuple-element.35.h0a, bf16[2,2,2,128,128]{4,3,2,1,0:T(8,128)(2,1)S(1)} %get-tuple-element.36.h0b, bf16[2,2,2,128,128]{4,3,2,1,0:T(8,128)(2,1)S(1)} %collective-permute-done.9.h1a, ...), custom_call_target="tpu_custom_call" | custom-call | tf_op jit(solution)/shard_map/gram/pallas_call | solution.py:337
  63.2 1.0 %collective-permute-start.17 = (f32[16,16]{1,0:T(8,128)S(1)}, f32[16,16]{1,0:T(8,128)S(1)}, u32[]{:S(2)}, u32[]{:S(2)}) collective-permute-start(f32[16,16]{1,0:T(8,128)S(1)} %gram.1), channel_id=1, source_target_pairs={{0,3},{1,2},{2,1},{3,0},{4,7},{5,6},{6,5},{7,4},{8,11},{9,10},{10,... | collective-permute-start | bytes 3080 | tf_op jit(solution)/shard_map/ppermute | solution.py:257
  64.2 2.0 %collective-permute-start.16 = (f32[16,16]{1,0:T(8,128)S(1)}, f32[16,16]{1,0:T(8,128)S(1)}, u32[]{:S(2)}, u32[]{:S(2)}) collective-permute-start(f32[16,16]{1,0:T(8,128)S(1)} %gram.1), channel_id=1, source_target_pairs={{0,2},{1,3},{2,0},{3,1},{4,6},{5,7},{6,4},{7,5},{8,10},{9,11},{10,... | collective-permute-start | bytes 3080 | tf_op jit(solution)/shard_map/ppermute | solution.py:257
  66.1 0.5 collective-permute-start.15
  66.7 1.3 %collective-permute-start.20 = (bf16[4,2,2,128,128]{4,3,2,1,0:T(8,128)(2,1)S(1)}, bf16[4,2,2,128,128]{4,3,2,1,0:T(8,128)(2,1)S(1)}, u32[]{:S(2)}, u32[]{:S(2)}) collective-permute-start(bf16[4,2,2,128,128]{4,3,2,1,0:T(8,128)(2,1)S(1)} %get-tuple-element.38), channel_id=1, source_target_pairs={{0,8},{16,24},{1,9},{17,25},{2,10},{18,26},{3,11},{19,27},{4,12},{... | collective-permute-start | bytes 1572872 | tf_op jit(solution)/shard_map/ppermute | solution.py:333
  68.0 1.8 %collective-permute-done.15 = f32[16,16]{1,0:T(8,128)S(1)} collective-permute-done((f32[16,16]{1,0:T(8,128)S(1)}, f32[16,16]{1,0:T(8,128)S(1)}, u32[]{:S(2)}, u32[]{:S(2)}) %collective-permute-start.15) | collective-permute-done | bytes 1056 | tf_op jit(solution)/shard_map/ppermute | solution.py:257
  70.0 0.7 collective-permute-start.21
  70.7 1.2 %collective-permute-start.19 = (f32[16,16]{1,0:T(8,128)S(1)}, f32[16,16]{1,0:T(8,128)S(1)}, u32[]{:S(2)}, u32[]{:S(2)}) collective-permute-start(f32[16,16]{1,0:T(8,128)S(1)} %add_add_fusion), channel_id=1, source_target_pairs={{0,4},{1,5},{2,6},{3,7},{4,0},{5,1},{6,2},{7,3},{8,12},{9,13},{10,... | collective-permute-start | bytes 3080 | tf_op jit(solution)/shard_map/ppermute | solution.py:257
  71.8 3.5 %collective-permute-done.19 = f32[16,16]{1,0:T(8,128)S(1)} collective-permute-done((f32[16,16]{1,0:T(8,128)S(1)}, f32[16,16]{1,0:T(8,128)S(1)}, u32[]{:S(2)}, u32[]{:S(2)}) %collective-permute-start.19) | collective-permute-done | bytes 1056 | tf_op jit(solution)/shard_map/ppermute | solution.py:257
  75.3 3.6 %final.1 = (f32[4,2,2,128,128]{4,3,2,1,0:T(8,128)}, f32[1,16]{1,0:T(1,128)}) custom-call(s32[1]{0:T(128)} %bitcast.me, f32[16,16]{1,0:T(8,128)S(1)} %add.15.gram, f32[4,2,2,128,128]{4,3,2,1,0:T(8,128)S(1)} %get-tuple-element.40.own, bf16[2,2,2,128,128]{4,3,2,1,0:T(8,128)(2,1)S(1)} %collective-permute-done.9.h1a, ...), custom_call_target="tpu_custom_call" | custom-call | tf_op jit(solution)/shard_map/final/pallas_call | solution.py:358
  (29 shorter events, 1.3 us)
Async XLA Ops:
  0.6 0.9 %copy-start.2 = (bf16[3,4,2,32,128]{4,3,2,1,0:T(8,128)(2,1)S(1)}, bf16[3,4,2,32,128]{4,3,2,1,0:T(8,128)(2,1)}, u32[]{:S(2)}) copy-start(bf16[3,4,2,32,128]{4,3,2,1,0:T(8,128)(2,1)} %background.3) | copy-start | bytes 589828
  1.6 9.7 %copy-start.3 = (bf16[3,4,2,32,128]{4,3,2,1,0:T(8,128)(2,1)S(1)}, bf16[3,4,2,32,128]{4,3,2,1,0:T(8,128)(2,1)}, u32[]{:S(2)}) copy-start(bf16[3,4,2,32,128]{4,3,2,1,0:T(8,128)(2,1)} %background.3) | copy-start | bytes 589828
  1.6 8.9 %collective-permute-start = (bf16[3,4,32,128]{3,2,1,0:T(8,128)(2,1)S(1)}, bf16[3,4,32,128]{3,2,1,0:T(8,128)(2,1)S(1)}, u32[]{:S(2)}, u32[]{:S(2)}) collective-permute-start(bf16[3,4,32,128]{3,2,1,0:T(8,128)(2,1)S(1)} %get-tuple-element.26), channel_id=1, source_target_pairs={{0,1},{1,2},{2,3},{3,4},{4,5},{5,6},{6,7},{7,0},{8,9},{9,10},{10,1... | collective-permute-start | bytes 294920 | tf_op jit(solution)/shard_map/ppermute | solution.py:253
  4.6 6.7 %collective-permute-start.1 = (bf16[3,4,32,128]{3,2,1,0:T(8,128)(2,1)S(1)}, bf16[3,4,32,128]{3,2,1,0:T(8,128)(2,1)S(1)}, u32[]{:S(2)}, u32[]{:S(2)}) collective-permute-start(bf16[3,4,32,128]{3,2,1,0:T(8,128)(2,1)S(1)} %get-tuple-element.27), channel_id=1, source_target_pairs={{0,7},{1,0},{2,1},{3,2},{4,3},{5,4},{6,5},{7,6},{8,15},{9,8},{10,9... | collective-permute-start | bytes 294920 | tf_op jit(solution)/shard_map/ppermute | solution.py:253
  7.7 1.2 %copy-start = (f32[4,2,2,128,128]{4,3,2,1,0:T(8,128)S(1)}, f32[4,2,2,128,128]{4,3,2,1,0:T(8,128)}, u32[]{:S(2)}) copy-start(f32[4,2,2,128,128]{4,3,2,1,0:T(8,128)} %own.3) | copy-start | bytes 3145732
  8.9 31.6 %copy-start.1 = (f32[4,2,2,128,128]{4,3,2,1,0:T(8,128)S(1)}, f32[4,2,2,128,128]{4,3,2,1,0:T(8,128)}, u32[]{:S(2)}) copy-start(f32[4,2,2,128,128]{4,3,2,1,0:T(8,128)} %own.3) | copy-start | bytes 3145732
  11.3 11.2 %collective-permute-start.7 = (bf16[12,4,32,128]{3,2,1,0:T(8,128)(2,1)S(1)}, bf16[12,4,32,128]{3,2,1,0:T(8,128)(2,1)S(1)}, u32[]{:S(2)}, u32[]{:S(2)}) collective-permute-start(bf16[12,4,32,128]{3,2,1,0:T(8,128)(2,1)S(1)} %pack.1.bg0), channel_id=1, source_target_pairs={{0,16},{8,24},{16,0},{24,8},{1,17},{9,25},{17,1},{25,9},{2,18},{10... | collective-permute-start | bytes 1179656 | tf_op jit(solution)/shard_map/ppermute | solution.py:257
  12.9 9.7 %collective-permute-start.5 = (bf16[4,2,128,128]{3,2,1,0:T(8,128)(2,1)S(1)}, bf16[4,2,128,128]{3,2,1,0:T(8,128)(2,1)S(1)}, u32[]{:S(2)}, u32[]{:S(2)}) collective-permute-start(bf16[4,2,128,128]{3,2,1,0:T(8,128)(2,1)S(1)} %get-tuple-element.30), channel_id=1, source_target_pairs={{0,6},{1,7},{2,0},{3,1},{4,2},{5,3},{6,4},{7,5},{8,14},{9,15},{10,... | collective-permute-start | bytes 786440 | tf_op jit(solution)/shard_map/ppermute | solution.py:253
  15.8 24.7 %collective-permute-start.3 = (bf16[2,4,2,128,128]{4,3,2,1,0:T(8,128)(2,1)}, bf16[2,4,2,128,128]{4,3,2,1,0:T(8,128)(2,1)S(1)}, u32[]{:S(2)}, u32[]{:S(2)}) collective-permute-start(bf16[2,4,2,128,128]{4,3,2,1,0:T(8,128)(2,1)} %get-tuple-element.28), channel_id=1, source_target_pairs={{0,7},{1,0},{2,1},{3,2},{4,3},{5,4},{6,5},{7,6},{8,15},{9,8},{10,9... | collective-permute-start | bytes 1572872 | tf_op jit(solution)/shard_map/ppermute | solution.py:253
  16.7 23.8 %collective-permute-start.2 = (bf16[2,4,2,128,128]{4,3,2,1,0:T(8,128)(2,1)}, bf16[2,4,2,128,128]{4,3,2,1,0:T(8,128)(2,1)S(1)}, u32[]{:S(2)}, u32[]{:S(2)}) collective-permute-start(bf16[2,4,2,128,128]{4,3,2,1,0:T(8,128)(2,1)} %get-tuple-element.28), channel_id=1, source_target_pairs={{0,1},{1,2},{2,3},{3,4},{4,5},{5,6},{6,7},{7,0},{8,9},{9,10},{10,1... | collective-permute-start | bytes 1572872 | tf_op jit(solution)/shard_map/ppermute | solution.py:253
  17.9 21.3 %collective-permute-start.6 = (bf16[12,4,32,128]{3,2,1,0:T(8,128)(2,1)S(1)}, bf16[12,4,32,128]{3,2,1,0:T(8,128)(2,1)S(1)}, u32[]{:S(2)}, u32[]{:S(2)}) collective-permute-start(bf16[12,4,32,128]{3,2,1,0:T(8,128)(2,1)S(1)} %pack.1.bg0), channel_id=1, source_target_pairs={{0,8},{8,0},{16,24},{24,16},{1,9},{9,1},{17,25},{25,17},{2,10},{10... | collective-permute-start | bytes 1179656 | tf_op jit(solution)/shard_map/ppermute | solution.py:257
  22.6 18.0 %collective-permute-start.8 = (bf16[12,4,32,128]{3,2,1,0:T(8,128)(2,1)S(1)}, bf16[12,4,32,128]{3,2,1,0:T(8,128)(2,1)}, u32[]{:S(2)}, u32[]{:S(2)}) collective-permute-start(bf16[12,4,32,128]{3,2,1,0:T(8,128)(2,1)S(1)} %collective-permute-done.7.bg2), channel_id=1, source_target_pairs={{0,8},{8,0},{16,24},{24,16},{1,9},{9,1},{17,25},{25,17},{2,10},{10... | collective-permute-start | bytes 1179656 | tf_op jit(solution)/shard_map/ppermute | solution.py:257
  22.6 16.6 %collective-permute-start.4 = (bf16[4,2,128,128]{3,2,1,0:T(8,128)(2,1)}, bf16[4,2,128,128]{3,2,1,0:T(8,128)(2,1)}, u32[]{:S(2)}, u32[]{:S(2)}) collective-permute-start(bf16[4,2,128,128]{3,2,1,0:T(8,128)(2,1)} %get-tuple-element.29), channel_id=1, source_target_pairs={{0,2},{1,3},{2,4},{3,5},{4,6},{5,7},{6,0},{7,1},{8,10},{9,11},{10,... | collective-permute-start | bytes 786440 | tf_op jit(solution)/shard_map/ppermute | solution.py:253
  46.2 2.6 %collective-permute-start.9 = (bf16[2,2,2,128,128]{4,3,2,1,0:T(8,128)(2,1)S(1)}, bf16[2,2,2,128,128]{4,3,2,1,0:T(8,128)(2,1)S(1)}, u32[]{:S(2)}, u32[]{:S(2)}) collective-permute-start(bf16[2,2,2,128,128]{4,3,2,1,0:T(8,128)(2,1)S(1)} %get-tuple-element.35.h0a), channel_id=1, source_target_pairs={{0,8},{8,0},{16,24},{24,16},{1,9},{9,1},{17,25},{25,17},{2,10},{10... | collective-permute-start | bytes 786440 | tf_op jit(solution)/shard_map/ppermute | solution.py:257
  46.3 2.5 %collective-permute-start.10 = (bf16[2,2,2,128,128]{4,3,2,1,0:T(8,128)(2,1)S(1)}, bf16[2,2,2,128,128]{4,3,2,1,0:T(8,128)(2,1)S(1)}, u32[]{:S(2)}, u32[]{:S(2)}) collective-permute-start(bf16[2,2,2,128,128]{4,3,2,1,0:T(8,128)(2,1)S(1)} %get-tuple-element.36.h0b), channel_id=1, source_target_pairs={{0,8},{8,0},{16,24},{24,16},{1,9},{9,1},{17,25},{25,17},{2,10},{10... | collective-permute-start | bytes 786440 | tf_op jit(solution)/shard_map/ppermute | solution.py:257
  46.8 9.2 %collective-permute-start.11 = (bf16[2,2,2,128,128]{4,3,2,1,0:T(8,128)(2,1)S(1)}, bf16[2,2,2,128,128]{4,3,2,1,0:T(8,128)(2,1)S(1)}, u32[]{:S(2)}, u32[]{:S(2)}) collective-permute-start(bf16[2,2,2,128,128]{4,3,2,1,0:T(8,128)(2,1)S(1)} %get-tuple-element.35.h0a), channel_id=1, source_target_pairs={{0,16},{8,24},{16,0},{24,8},{1,17},{9,25},{17,1},{25,9},{2,18},{10... | collective-permute-start | bytes 786440 | tf_op jit(solution)/shard_map/ppermute | solution.py:257
  47.3 13.4 %collective-permute-start.12 = (bf16[2,2,2,128,128]{4,3,2,1,0:T(8,128)(2,1)S(1)}, bf16[2,2,2,128,128]{4,3,2,1,0:T(8,128)(2,1)S(1)}, u32[]{:S(2)}, u32[]{:S(2)}) collective-permute-start(bf16[2,2,2,128,128]{4,3,2,1,0:T(8,128)(2,1)S(1)} %get-tuple-element.36.h0b), channel_id=1, source_target_pairs={{0,16},{8,24},{16,0},{24,8},{1,17},{9,25},{17,1},{25,9},{2,18},{10... | collective-permute-start | bytes 786440 | tf_op jit(solution)/shard_map/ppermute | solution.py:257
  49.3 20.7 %collective-permute-start.18 = (bf16[4,2,2,128,128]{4,3,2,1,0:T(8,128)(2,1)S(1)}, bf16[4,2,2,128,128]{4,3,2,1,0:T(8,128)(2,1)S(1)}, u32[]{:S(2)}, u32[]{:S(2)}) collective-permute-start(bf16[4,2,2,128,128]{4,3,2,1,0:T(8,128)(2,1)S(1)} %get-tuple-element.38), channel_id=1, source_target_pairs={{0,16},{8,24},{1,17},{9,25},{2,18},{10,26},{3,19},{11,27},{4,20},{... | collective-permute-start | bytes 1572872 | tf_op jit(solution)/shard_map/ppermute | solution.py:332
  56.0 4.8 %collective-permute-start.13 = (bf16[2,2,2,128,128]{4,3,2,1,0:T(8,128)(2,1)S(1)}, bf16[2,2,2,128,128]{4,3,2,1,0:T(8,128)(2,1)S(1)}, u32[]{:S(2)}, u32[]{:S(2)}) collective-permute-start(bf16[2,2,2,128,128]{4,3,2,1,0:T(8,128)(2,1)S(1)} %collective-permute-done.11.h2a), channel_id=1, source_target_pairs={{0,8},{8,0},{16,24},{24,16},{1,9},{9,1},{17,25},{25,17},{2,10},{10... | collective-permute-start | bytes 786440 | tf_op jit(solution)/shard_map/ppermute | solution.py:257
  60.7 1.5 %collective-permute-start.14 = (bf16[2,2,2,128,128]{4,3,2,1,0:T(8,128)(2,1)S(1)}, bf16[2,2,2,128,128]{4,3,2,1,0:T(8,128)(2,1)S(1)}, u32[]{:S(2)}, u32[]{:S(2)}) collective-permute-start(bf16[2,2,2,128,128]{4,3,2,1,0:T(8,128)(2,1)S(1)} %collective-permute-done.12.h2b), channel_id=1, source_target_pairs={{0,8},{8,0},{16,24},{24,16},{1,9},{9,1},{17,25},{25,17},{2,10},{10... | collective-permute-start | bytes 786440 | tf_op jit(solution)/shard_map/ppermute | solution.py:257
  63.2 4.8 %collective-permute-start.17 = (f32[16,16]{1,0:T(8,128)S(1)}, f32[16,16]{1,0:T(8,128)S(1)}, u32[]{:S(2)}, u32[]{:S(2)}) collective-permute-start(f32[16,16]{1,0:T(8,128)S(1)} %gram.1), channel_id=1, source_target_pairs={{0,3},{1,2},{2,1},{3,0},{4,7},{5,6},{6,5},{7,4},{8,11},{9,10},{10,... | collective-permute-start | bytes 3080 | tf_op jit(solution)/shard_map/ppermute | solution.py:257
  64.2 3.9 %collective-permute-start.16 = (f32[16,16]{1,0:T(8,128)S(1)}, f32[16,16]{1,0:T(8,128)S(1)}, u32[]{:S(2)}, u32[]{:S(2)}) collective-permute-start(f32[16,16]{1,0:T(8,128)S(1)} %gram.1), channel_id=1, source_target_pairs={{0,2},{1,3},{2,0},{3,1},{4,6},{5,7},{6,4},{7,5},{8,10},{9,11},{10,... | collective-permute-start | bytes 3080 | tf_op jit(solution)/shard_map/ppermute | solution.py:257
  66.1 3.7 %collective-permute-start.15 = (f32[16,16]{1,0:T(8,128)S(1)}, f32[16,16]{1,0:T(8,128)S(1)}, u32[]{:S(2)}, u32[]{:S(2)}) collective-permute-start(f32[16,16]{1,0:T(8,128)S(1)} %gram.1), channel_id=1, source_target_pairs={{0,1},{1,0},{2,3},{3,2},{4,5},{5,4},{6,7},{7,6},{8,9},{9,8},{10,11... | collective-permute-start | bytes 3080 | tf_op jit(solution)/shard_map/ppermute | solution.py:257
  66.7 8.6 %collective-permute-start.20 = (bf16[4,2,2,128,128]{4,3,2,1,0:T(8,128)(2,1)S(1)}, bf16[4,2,2,128,128]{4,3,2,1,0:T(8,128)(2,1)S(1)}, u32[]{:S(2)}, u32[]{:S(2)}) collective-permute-start(bf16[4,2,2,128,128]{4,3,2,1,0:T(8,128)(2,1)S(1)} %get-tuple-element.38), channel_id=1, source_target_pairs={{0,8},{16,24},{1,9},{17,25},{2,10},{18,26},{3,11},{19,27},{4,12},{... | collective-permute-start | bytes 1572872 | tf_op jit(solution)/shard_map/ppermute | solution.py:333
  70.0 5.3 %collective-permute-start.21 = (bf16[4,2,2,128,128]{4,3,2,1,0:T(8,128)(2,1)S(1)}, bf16[4,2,2,128,128]{4,3,2,1,0:T(8,128)(2,1)S(1)}, u32[]{:S(2)}, u32[]{:S(2)}) collective-permute-start(bf16[4,2,2,128,128]{4,3,2,1,0:T(8,128)(2,1)S(1)} %collective-permute-done.18.l2), channel_id=1, source_target_pairs={{16,24},{24,16},{17,25},{25,17},{18,26},{26,18},{19,27},{27,19},{2... | collective-permute-start | bytes 1572872 | tf_op jit(solution)/shard_map/ppermute | solution.py:350
  70.7 4.6 %collective-permute-start.19 = (f32[16,16]{1,0:T(8,128)S(1)}, f32[16,16]{1,0:T(8,128)S(1)}, u32[]{:S(2)}, u32[]{:S(2)}) collective-permute-start(f32[16,16]{1,0:T(8,128)S(1)} %add_add_fusion), channel_id=1, source_target_pairs={{0,4},{1,5},{2,6},{3,7},{4,0},{5,1},{6,2},{7,3},{8,12},{9,13},{10,... | collective-permute-start | bytes 3080 | tf_op jit(solution)/shard_map/ppermute | solution.py:257
